TPU v7x, 32 devices: a whole 2x2x4 slice. The times are simulated.
32 devices in a mesh: groups: 2 (over y), ctx: 4 (over z), exp: 2 (over x), tp: 2 (over core).
Axes of the slice: x: 2, y: 2, z: 4, core: 2. Of those that a mesh axis runs over, the one named last changes fastest.
Arguments:
- queries: bfloat16 [4, 512, 20, 128], P(('groups', 'exp'), 'ctx', 'tp'), parts along dimension 0, may hold values from -9 to 9
- key_states: bfloat16 [4, 512, 4, 128], P(('groups', 'exp'), 'ctx', 'tp'), parts along dimension 0, may hold values from -9 to 9
- values: bfloat16 [4, 512, 4, 128], P(('groups', 'exp'), 'ctx', 'tp'), parts along dimension 0, may hold values from -6 to 6
- doc_ids: int32 [4, 512], P(('groups', 'exp'), 'ctx'), parts along dimension 0, may hold values from 0 to 3, never falling along the last dimension, each value on 1 to 256 neighbouring positions
- residual: bfloat16 [4, 512, 5120], P(('groups', 'exp'), ('ctx', 'tp')), parts along dimension 0, may hold values from -6 to 6
- out_proj: bfloat16 [2560, 5120], P('tp', 'ctx'), may hold values from -0.125 to 0.125
- norm_gain: bfloat16 [5120], replicated, may hold values from 0.5 to 1.5
- router: bfloat16 [5120, 64], P(None, 'exp'), may hold values from -0.078125 to 0.078125
- expert_ids: int32 [4, 512, 1], P(('groups', 'exp'), ('ctx', 'tp')), parts along dimension 0, may hold values from 0 to 63; in each aligned block of 64 rows (0 to 63, 64 to 127, ..., all dimensions but the last counted through in order) at most 2 rows name the same one
- keep_counts: int32 [128], P('groups'), parts along dimension 0, may hold values from 1 to 2
Outputs:
- expert_inputs: bfloat16 [32, 64, 2, 5120], P(('groups', 'ctx', 'tp'), 'exp'), parts along dimension 0
There are 2 independent parts, one for each index of `groups`. A program takes and returns all parts, laid end to end along the dimension named above; an argument that names none is the same for every part. Nothing has to cross between parts.
Inputs may be any that keep to these rules, and one draw needn't show every extreme that they name: `doc_ids`: doc ids never fall along a request; a document holds at most 256 tokens, and some document holds exactly that many. `expert_ids`: in each aligned block of 64 tokens (the rows of one device) no expert is named more than 2 times, and in some blocks one expert is named exactly 2 times.
All inputs are finite; a program needn't handle non-finite values.
Results may differ from a plain program's by a relative error of at most 0.013.
Values may be sent and summed in bfloat16 or wider, within the bound.
No kernel may reach another device: no remote copies, remote signals or barrier semaphores. Data moves between devices by JAX's collectives and lax.ppermute only.
A program may use at most 64 MiB of HBM per device.

v0:
```python
import math

import jax
import jax.numpy as jnp
from jax import lax
from jax.sharding import PartitionSpec as P

CAP = 2


EPSILON = 1e-05


def on_device(
    queries,
    key_states,
    values,
    doc_ids,
    residual,
    out_proj,
    norm_gain,
    router,
    expert_ids,
    keep_counts,
):
    tokens_here = queries.shape[1]
    heads_here = queries.shape[2]
    head_size = queries.shape[3]
    groups_here = key_states.shape[2]
    mixing_ratio = heads_here // groups_here
    ctx_count = lax.axis_size("ctx")
    pair_count = lax.axis_size("tp")
    part_rows = tokens_here // pair_count
    first_token = lax.axis_index("ctx") * tokens_here
    scale = 1.0 / math.sqrt(head_size)
    query_rows = (
        queries[0].reshape(tokens_here, groups_here, mixing_ratio, head_size).transpose(1, 0, 2, 3)
    )
    query_rows = query_rows.reshape(groups_here, tokens_here * mixing_ratio, head_size)
    query_place = (
        first_token
        + lax.broadcasted_iota(jnp.int32, (tokens_here * mixing_ratio,), 0) // mixing_ratio
    )
    query_docs = jnp.repeat(doc_ids[0], mixing_ratio)

    def update(running, key_block, value_block, doc_block, key_first):
        highest, totals, accum = running
        scores = (
            jnp.einsum("gqd,kgd->gqk", query_rows, key_block, preferred_element_type=jnp.float32)
            * scale
        )
        key_place = key_first + lax.broadcasted_iota(jnp.int32, (key_block.shape[0],), 0)
        allowed = (key_place[None, :] <= query_place[:, None]) & (
            doc_block[None, :] == query_docs[:, None]
        )
        masked = jnp.where(allowed[None], scores, -1e30)
        new_highest = jnp.maximum(highest, jnp.max(masked, axis=2))
        weights = jnp.where(allowed[None], jnp.exp(scores - new_highest[..., None]), 0.0)
        factor = jnp.exp(highest - new_highest)
        totals = totals * factor + jnp.sum(weights, axis=2)
        accum = accum * factor[..., None] + jnp.einsum(
            "gqk,kgd->gqd",
            weights.astype(jnp.bfloat16),
            value_block,
            preferred_element_type=jnp.float32,
        )
        return (new_highest, totals, accum)

    start_state = (
        jnp.full((groups_here, tokens_here * mixing_ratio), -1e30, jnp.float32),
        jnp.zeros((groups_here, tokens_here * mixing_ratio), jnp.float32),
        jnp.zeros((groups_here, tokens_here * mixing_ratio, head_size), jnp.float32),
    )
    key_piece = lax.all_gather(key_states, "ctx", axis=1, tiled=True)
    value_piece = lax.all_gather(values, "ctx", axis=1, tiled=True)
    doc_piece = lax.all_gather(doc_ids, "ctx", axis=1, tiled=True)
    piece_rows = key_piece.shape[1]
    block_rows = math.gcd(piece_rows, 512)

    def step(block_number, inner):
        block_offset = block_number * block_rows
        key_block = lax.dynamic_slice_in_dim(key_piece[0], block_offset, block_rows, 0)
        value_block = lax.dynamic_slice_in_dim(value_piece[0], block_offset, block_rows, 0)
        doc_block = lax.dynamic_slice_in_dim(doc_piece[0], block_offset, block_rows, 0)
        return update(inner, key_block, value_block, doc_block, block_offset)

    highest, totals, accum = lax.fori_loop(0, piece_rows // block_rows, step, start_state)
    blended_output = (accum / totals[..., None]).astype(jnp.bfloat16)
    blended_output = blended_output.reshape(
        groups_here, tokens_here, mixing_ratio, head_size
    ).transpose(1, 0, 2, 3)
    attn_rows = blended_output.reshape(pair_count, part_rows, heads_here * head_size)
    columns = out_proj.shape[1]
    gathered = lax.all_gather(attn_rows, "ctx", axis=1, tiled=True)
    gathered = gathered.reshape(pair_count * ctx_count * part_rows, heads_here * head_size)
    own_columns = lax.psum_scatter(
        jnp.dot(gathered, out_proj, preferred_element_type=jnp.float32).astype(jnp.bfloat16),
        "tp",
        scatter_dimension=0,
        tiled=True,
    ).astype(jnp.float32)
    own_columns = own_columns.reshape(ctx_count, part_rows, columns)
    projected = (
        lax.all_to_all(
            own_columns.astype(jnp.bfloat16), "ctx", split_axis=0, concat_axis=2, tiled=True
        )
        .astype(own_columns.dtype)
        .reshape(part_rows, columns * ctx_count)
    )
    hidden = residual[0].astype(jnp.float32) + projected
    power = jnp.mean(hidden * hidden, axis=1, keepdims=True)
    normed = (hidden * lax.rsqrt(power + EPSILON) * norm_gain.astype(jnp.float32)).astype(
        jnp.bfloat16
    )
    expert_count = keep_counts.shape[0]
    chosen = expert_ids[0, :, 0]
    onehot = (
        chosen[:, None] == lax.broadcasted_iota(jnp.int32, (part_rows, expert_count), 1)
    ).astype(jnp.float32)
    lower = (
        lax.broadcasted_iota(jnp.int32, (part_rows, part_rows), 0)
        > lax.broadcasted_iota(jnp.int32, (part_rows, part_rows), 1)
    ).astype(jnp.float32)
    earlier = jnp.dot(lower, onehot, preferred_element_type=jnp.float32)
    ranking = jnp.sum(onehot * earlier, axis=1)
    limits = jnp.sum(onehot * keep_counts.astype(jnp.float32)[None, :], axis=1)
    kept = ranking < limits
    target = chosen.astype(jnp.float32) * CAP + ranking
    slot_iota = lax.broadcasted_iota(jnp.int32, (expert_count * CAP, part_rows), 0).astype(
        jnp.float32
    )
    table = (slot_iota == target[None, :]) & kept[None, :]
    outgoing = jnp.dot(
        table.astype(jnp.bfloat16), normed, preferred_element_type=jnp.float32
    ).astype(jnp.bfloat16)
    exp_count = lax.axis_size("exp")
    outgoing = outgoing.reshape(exp_count, expert_count // exp_count, CAP, normed.shape[1])
    arrived = lax.all_to_all(outgoing, "exp", split_axis=0, concat_axis=0, tiled=True)
    logits = jnp.einsum("secd,de->sec", arrived, router, preferred_element_type=jnp.float32)
    return (arrived.astype(jnp.float32) * jax.nn.sigmoid(logits)[..., None]).astype(jnp.bfloat16)


def solution(mesh):
    placed = (
        P(("groups", "exp"), "ctx", "tp", None),
        P(("groups", "exp"), "ctx", "tp", None),
        P(("groups", "exp"), "ctx", "tp", None),
        P(("groups", "exp"), "ctx"),
        P(("groups", "exp"), ("ctx", "tp"), None),
        P("tp", "ctx"),
        P(),
        P(None, "exp"),
        P(("groups", "exp"), ("ctx", "tp"), None),
        P("groups"),
    )
    return jax.shard_map(
        on_device,
        mesh=mesh,
        in_specs=placed,
        out_specs=P(("groups", "ctx", "tp"), "exp", None, None),
        check_vma=False,
    )
```

profile of v0, /device:TPU:0, one launch (start us, length us, event | category | flops | bytes accessed | tf_op | source)
XLA Modules:
  0.0 172.5 jit_solution(3476322581073212627)
XLA Ops:
  6.5 12.8 %all_gather.14 = s32[1,512]{1,0:T(1,128)S(1)} all-gather(s32[1,128]{1,0:T(1,128)} %param.13), channel_id=1, replica_groups=mesh['groups'=2,'ctx'=4,'exp'=2,'tp'=2] {'ctx'}, dimensions={1}, use_global_device_ids=true | all-gather | bytes 2560 | tf_op jit(solution)/shard_map/all_gather | solution.py:76
  19.4 0.7 broadcast_in_dim.55
  20.1 0.2 eq.47
  20.3 0.9 copy.17
  21.2 13.9 %all_gather.16 = bf16[1,512,2,128]{3,1,2,0:T(8,128)(2,1)S(1)} all-gather(bf16[1,128,2,128]{3,1,2,0:T(8,128)(2,1)S(1)} %copy.17), channel_id=1, replica_groups=mesh['groups'=2,'ctx'=4,'exp'=2,'tp'=2] {'ctx'}, dimensions={1}, use_global_device_ids=true | all-gather | bytes 327680 | tf_op jit(solution)/shard_map/all_gather | solution.py:74
  35.1 1.3 copy.16
  36.4 0.3 fusion.7
  36.7 0.7 select_reduce_fusion
  37.4 0.6 fusion
  38.1 0.2 copy-done.2
  38.3 14.2 %all_gather.17 = bf16[1,512,2,128]{3,1,2,0:T(8,128)(2,1)S(1)} all-gather(bf16[1,128,2,128]{3,1,2,0:T(8,128)(2,1)S(1)} %copy.19), channel_id=1, replica_groups=mesh['groups'=2,'ctx'=4,'exp'=2,'tp'=2] {'ctx'}, dimensions={1}, use_global_device_ids=true | all-gather | bytes 327680 | tf_op jit(solution)/shard_map/all_gather | solution.py:75
  52.4 1.2 fusion.18
  53.7 0.3 copy.21
  54.0 0.9 copy.22
  54.9 2.2 %reshape.135 = bf16[2,64,1280]{2,1,0:T(8,128)(2,1)} reshape(bf16[128,2,5,128]{3,2,1,0:T(8,128)(2,1)} %copy.22) | data formatting | bytes 655360 | tf_op jit(solution)/shard_map/reshape | solution.py:92
  57.1 31.1 %all-gather.2.cloned.1.call-done = bf16[2,256,1280]{2,1,0:T(8,128)(2,1)} async-done(((bf16[2,64,1280]{2,1,0:T(8,128)(2,1)}), bf16[2,256,1280]{2,1,0:T(8,128)(2,1)}) %all-gather.2.cloned.1.call-update) | async-done | bytes 1310736 | tf_op jit(solution)/shard_map/all_gather | solution.py:94
  88.2 4.2 %convolution_convert_fusion.1 = bf16[512,1280]{1,0:T(8,128)(2,1)} fusion(bf16[512,1280]{1,0:T(8,128)(2,1)} %bitcast.62, bf16[1280,1280]{1,0:T(8,128)(2,1)S(1)} %copy-done), kind=kOutput, calls=%fused_computation.1 | convolution fusion | flops 1678376960 | bytes 5898240 | tf_op jit(solution)/shard_map/dot_general | solution.py:97
  92.5 7.9 %reduce-scatter.2.cloned.1.call-done = bf16[256,1280]{1,0:T(8,128)(2,1)} async-done(((bf16[512,1280]{1,0:T(8,128)(2,1)}), bf16[256,1280]{1,0:T(8,128)(2,1)}) %reduce-scatter.2.cloned.1.call-update) | async-done | bytes 655376 | tf_op jit(solution)/shard_map/reduce_scatter | solution.py:96
  100.4 4.9 %all-to-all-start = ((bf16[4,64,1280]{2,1,0:T(8,128)(2,1)}), bf16[4,64,1280]{2,1,0:T(8,128)(2,1)}, u32[]{:S(2)}, u32[]{:S(2)}) async-start(bf16[4,64,1280]{2,1,0:T(8,128)(2,1)} %bitcast.55), calls=%async_computation.1 | async-start | bytes 1310720 | tf_op jit(solution)/shard_map/all_to_all | solution.py:104
  105.3 0.2 fusion.14
  105.5 0.1 select_reduce_fusion.1
  105.6 17.5 %all-to-all-done = bf16[4,64,1280]{2,1,0:T(8,128)(2,1)} async-done(((bf16[4,64,1280]{2,1,0:T(8,128)(2,1)}), bf16[4,64,1280]{2,1,0:T(8,128)(2,1)}, u32[]{:S(2)}, u32[]{:S(2)}) %all-to-all-start) | async-done | bytes 655392 | tf_op jit(solution)/shard_map/all_to_all | solution.py:104
  123.1 1.2 convert_bitcast_fusion
  124.3 0.8 copy.23
  125.2 0.2 copy.28
  125.4 0.8 copy-done.1
  126.3 0.3 multiply_reduce_fusion
  126.6 1.6 convolution_convert_fusion
  128.2 3.9 %reshape.137 = bf16[2,32,2,5120]{3,2,1,0:T(2,128)(2,1)} reshape(bf16[128,5120]{1,0:T(8,128)(2,1)} %convolution_convert_fusion) | data formatting | bytes 2621440 | tf_op jit(solution)/shard_map/reshape | solution.py:137
  132.1 19.7 %all_to_all.14 = bf16[2,32,2,5120]{3,2,1,0:T(2,128)(2,1)S(1)} all-to-all(bf16[2,32,2,5120]{3,2,1,0:T(2,128)(2,1)} %reshape.137), channel_id=1, replica_groups=mesh['groups'=2,'ctx'=4,'exp'=2,'tp'=2] {'exp'}, dimensions={0} | all-to-all | bytes 2621440 | tf_op jit(solution)/shard_map/all_to_all | solution.py:138
  151.8 11.5 %fusion.9 = f32[32,1,2,2]{3,1,2,0:T(1,128)S(1)} fusion(bf16[2,32,2,5120]{3,2,1,0:T(2,128)(2,1)S(1)} %all_to_all.14, bf16[5120,32,1,1]{0,1,2,3:T(8,128)(2,1)S(1)} %bitcast.63), kind=kOutput, calls=%fused_computation.18 | convolution fusion | flops 1310720 | bytes 1638912 | tf_op jit(solution)/shard_map/secd,de->sec/dot_general | solution.py:139
  163.4 2.2 %multiply_convert_fusion = bf16[2,32,2,5120]{3,2,1,0:T(2,128)(2,1)} fusion(bf16[2,32,2,5120]{3,2,1,0:T(2,128)(2,1)S(1)} %all_to_all.14, f32[2,32,2]{2,1,0:T(8,128)S(1)} %fusion.34), kind=kLoop, calls=%fused_computation.2 | loop fusion | flops 1966080 | bytes 2621952 | tf_op jit(solution)/shard_map/convert_element_type | solution.py:140
  (26 shorter events, 0.2 us)
Async XLA Ops:
  6.5 81.7 %copy-start = (bf16[1280,1280]{1,0:T(8,128)(2,1)S(1)}, bf16[1280,1280]{1,0:T(8,128)(2,1)}, u32[]{:S(2)}) copy-start(bf16[1280,1280]{1,0:T(8,128)(2,1)} %param.15) | copy-start | bytes 9830404
  6.5 81.7 %all-gather.2.cloned.1.call-start = ((), (), s32[]{:S(2)}) async-start(), calls=%async_computation.3 | async-start | bytes 1638400 | tf_op jit(solution)/shard_map/all_gather | solution.py:94
  37.4 0.8 copy-start.2
  57.1 43.3 %reduce-scatter.2.cloned.1.call-start = ((), (), s32[]{:S(2)}) async-start(), calls=%async_computation.4 | async-start | bytes 1966080 | tf_op jit(solution)/shard_map/reduce_scatter | solution.py:96
  92.5 12.8 %copy-start.6 = (s32[64]{0:T(128)S(1)}, s32[64]{0:T(128)}, u32[]{:S(2)}) copy-start(s32[64]{0:T(128)} %param.19) | copy-start | bytes 772
  92.5 12.8 %copy-start.3 = (bf16[5120]{0:T(1024)(128)(2,1)S(1)}, bf16[5120]{0:T(1024)(128)(2,1)}, u32[]{:S(2)}) copy-start(bf16[5120]{0:T(1024)(128)(2,1)} %param.16) | copy-start | bytes 30724
  92.5 12.9 %copy-start.4 = (s32[1,64,1]{1,2,0:T(1,128)S(1)}, s32[1,64,1]{1,2,0:T(1,128)}, u32[]{:S(2)}) copy-start(s32[1,64,1]{1,2,0:T(1,128)} %param.18) | copy-start | bytes 772
  100.4 22.7 %all-to-all-start = ((bf16[4,64,1280]{2,1,0:T(8,128)(2,1)}), bf16[4,64,1280]{2,1,0:T(8,128)(2,1)}, u32[]{:S(2)}, u32[]{:S(2)}) async-start(bf16[4,64,1280]{2,1,0:T(8,128)(2,1)} %bitcast.55), calls=%async_computation.1 | async-start | bytes 1310720 | tf_op jit(solution)/shard_map/all_to_all | solution.py:104
  125.2 1.1 copy-start.1
  132.1 19.8 %copy-start.5 = (bf16[5120,32]{0,1:T(8,128)(2,1)S(1)}, bf16[5120,32]{0,1:T(8,128)(2,1)}, u32[]{:S(2)}) copy-start(bf16[5120,32]{0,1:T(8,128)(2,1)} %param.17) | copy-start | bytes 983044
Sparse Core Ops, SparseCore 0:
  57.2 30.9 all-gather.1
  92.6 7.7 reduce-scatter.1
where the time goes:
time: 173 us; the launch traced here: 172 us
  blocking collectives  60.6 us (35%)
  waiting for transfers between devices  56.6 us (33%)
  matrix products  19.5 us (11%)
  between operations  13.6 us (8%)
  local copies, waits for them, and re-layouts  12.5 us (7%)
  starting transfers between devices  4.93 us (3%)
  other arithmetic  4.83 us (3%)
    all_gather x1, waiting for transfers between devices, on_device(): gathered = lax.all_gather(attn_rows, 'ctx', axis=1, tiled=True)  31.1 us
    all_to_all x1, blocking collectives, on_device(): lax.all_to_all(outgoing, 'exp', split_axis=0, concat_axis=0, tiled=True)  19.7 us
    all_to_all x1, waiting for transfers between devices, on_device(): lax.all_to_all(own_columns.astype(jnp.bfloat16), 'ctx', split_axis=0, con...  17.5 us
    all_gather x1, blocking collectives, on_device(): value_piece = lax.all_gather(values, 'ctx', axis=1, tiled=True)  14.2 us
    all_gather x1, blocking collectives, on_device(): key_piece = lax.all_gather(key_states, 'ctx', axis=1, tiled=True)  13.9 us
    all_gather x1, blocking collectives, on_device(): doc_piece = lax.all_gather(doc_ids, 'ctx', axis=1, tiled=True)  12.8 us
    dot_general x1, matrix products, on_device(): jnp.einsum('secd,de->sec', arrived, router, preferred_element_type=jnp.fl...  11.5 us
    reduce_scatter x1, waiting for transfers between devices, on_device(): lax.psum_scatter(jnp.dot(gathered, out_proj, preferred_element_type=jnp.f...  7.92 us
  transfers between devices with their start and end apart: 3, of which 3 were waited for; matrix products, arithmetic and copies ran while one was open for 0% of the time, Pallas kernels for 0%

commit v1 on v0

v1 whole, which is shorter than its diff:
```python
import functools
import math

import jax
import jax.numpy as jnp
from jax import lax
from jax.experimental import pallas as pl
from jax.experimental.pallas import tpu as pltpu
from jax.sharding import PartitionSpec as P

CAP = 2
EPSILON = 1e-05
DOC_ROWS = 16
VMEM_LIMIT = 40 * 1024 * 1024


def attention_kernel(ratio, pair, core_ref, query_ref, doc_ref, *refs):
    pack_refs, out_refs = refs[:-pair], refs[-pair:]
    heads, tokens, head_size = query_ref.shape
    groups = heads // ratio
    scale = 1.0 / math.sqrt(head_size)
    own_doc = doc_ref[...]
    rows = lax.broadcasted_iota(jnp.int32, (tokens, tokens), 0)
    columns = lax.broadcasted_iota(jnp.int32, (tokens, tokens), 1)
    allowed = []
    for place, ref in enumerate(pack_refs):
        docs = ref[2 * groups * tokens : 2 * groups * tokens + 1, :].astype(jnp.float32)
        same = own_doc == docs
        allowed.append(same & (columns <= rows) if place == 0 else same)
    allowed = jnp.concatenate(allowed, axis=1)
    core = core_ref[0]
    part_rows = tokens // pair
    for group in range(groups):
        first = group * tokens
        keys = jnp.concatenate([ref[first : first + tokens, :] for ref in pack_refs], axis=0)
        first = (groups + group) * tokens
        held = jnp.concatenate([ref[first : first + tokens, :] for ref in pack_refs], axis=0)
        for head in range(group * ratio, (group + 1) * ratio):
            scores = lax.dot_general(
                query_ref[head], keys, (((1,), (1,)), ((), ())), preferred_element_type=jnp.float32
            )
            scores = jnp.where(allowed, scores * scale, -1e30)
            weights = jnp.exp(scores - jnp.max(scores, axis=1, keepdims=True))
            totals = jnp.sum(weights, axis=1, keepdims=True)
            mixed = jnp.dot(
                weights.astype(jnp.bfloat16), held, preferred_element_type=jnp.float32
            )
            mixed = (mixed / totals).astype(jnp.bfloat16)
            parts = [mixed[i * part_rows : (i + 1) * part_rows] for i in range(pair)]
            for turn in range(pair):
                piece = parts[turn]
                for own in range(1, pair):
                    piece = jnp.where(core == own, parts[(own + turn) % pair], piece)
                out_refs[turn][:, head * head_size : (head + 1) * head_size] = piece


def finish_kernel(steps, exp_count, place_ref, *refs):
    chunk_refs = refs[: steps * exp_count]
    rest = refs[steps * exp_count :]
    residual_refs, id_refs = rest[:exp_count], rest[exp_count : 2 * exp_count]
    keep_ref, gain_ref, router_ref, out_ref, hidden_ref, normed_ref = rest[2 * exp_count :]
    rows, width = residual_refs[0].shape
    columns = chunk_refs[0].shape[1]
    experts = keep_ref.shape[1]
    here = router_ref.shape[0]
    ctx_index, exp_index = place_ref[0], place_ref[1]
    keep = keep_ref[...].astype(jnp.float32)
    upper = (
        lax.broadcasted_iota(jnp.int32, (rows, rows), 0)
        < lax.broadcasted_iota(jnp.int32, (rows, rows), 1)
    ).astype(jnp.bfloat16)
    for back in range(exp_count):
        power = jnp.zeros((rows, 1), jnp.float32)
        for step in range(steps):
            first = 0 if steps == 1 else lax.rem(ctx_index + step, steps) * columns
            part = pl.ds(pl.multiple_of(first, 128), columns)
            hidden = residual_refs[back][:, part].astype(jnp.float32) + chunk_refs[
                step * exp_count + back
            ][...].astype(jnp.float32)
            hidden_ref[:, part] = hidden
            power = power + jnp.sum(hidden * hidden, axis=1, keepdims=True)
        factor = lax.rsqrt(power / width + EPSILON)
        normed_ref[...] = (
            hidden_ref[...] * factor * gain_ref[...].astype(jnp.float32)
        ).astype(jnp.bfloat16)
        ids = id_refs[back][...]
        onehot = ids == lax.broadcasted_iota(jnp.int32, (experts, rows), 0)
        onehot_wide = onehot.astype(jnp.float32)
        earlier = jnp.dot(
            onehot_wide.astype(jnp.bfloat16), upper, preferred_element_type=jnp.float32
        )
        ranking = jnp.sum(onehot_wide * earlier, axis=0, keepdims=True)
        limits = jnp.dot(
            keep.astype(jnp.bfloat16),
            onehot_wide.astype(jnp.bfloat16),
            preferred_element_type=jnp.float32,
        )
        local = ids - exp_index * here
        logits = lax.dot_general(
            router_ref[...],
            normed_ref[...],
            (((1,), (1,)), ((), ())),
            preferred_element_type=jnp.float32,
        )
        chosen = local == lax.broadcasted_iota(jnp.int32, (here, rows), 0)
        gates = jax.nn.sigmoid(jnp.sum(jnp.where(chosen, logits, 0.0), axis=0, keepdims=True))
        target = local * CAP + ranking.astype(jnp.int32)
        target = jnp.where((ranking < limits) & (local >= 0) & (local < here), target, -1)
        table = lax.broadcasted_iota(jnp.int32, (here * CAP, rows), 0) == target
        slot_gates = jnp.sum(jnp.where(table, gates, 0.0), axis=1, keepdims=True)
        slots = jnp.dot(
            table.astype(jnp.bfloat16), normed_ref[...], preferred_element_type=jnp.float32
        )
        source = lax.rem(exp_index - back + exp_count, exp_count)
        out_ref[source] = (slots * slot_gates).astype(jnp.bfloat16)


def on_device(
    queries,
    key_states,
    values,
    doc_ids,
    residual,
    out_proj,
    norm_gain,
    router,
    expert_ids,
    keep_counts,
):
    _, tokens, heads, head_size = queries.shape
    groups = key_states.shape[2]
    ctx_count = lax.axis_size("ctx")
    pair = lax.axis_size("tp")
    exp_count = lax.axis_size("exp")
    part_rows = tokens // pair
    width = residual.shape[2]
    columns = out_proj.shape[1]
    ctx_index = lax.axis_index("ctx")
    core = lax.axis_index("tp")
    exp_index = lax.axis_index("exp")
    reach = -(-(ctx_count * tokens // 2 - 1) // tokens)

    docs = (doc_ids + 1).astype(jnp.bfloat16)
    pack = jnp.concatenate(
        [
            key_states[0].transpose(1, 0, 2).reshape(groups * tokens, head_size),
            values[0].transpose(1, 0, 2).reshape(groups * tokens, head_size),
            jnp.broadcast_to(docs, (DOC_ROWS, tokens)),
        ],
        axis=0,
    )
    packs = [pack] + [
        lax.ppermute(pack, "ctx", [(i, i + step) for i in range(ctx_count - step)])
        for step in range(1, reach + 1)
    ]
    weights = [out_proj] + [
        lax.ppermute(out_proj, "tp", [(i, (i + turn) % pair) for i in range(pair)])
        for turn in range(1, pair)
    ]

    def over_exp(array, back):
        if back == 0:
            return array
        return lax.ppermute(
            array, "exp", [(i, (i + back) % exp_count) for i in range(exp_count)]
        )

    ids = expert_ids[:, :, 0]
    all_ids = [over_exp(ids, back) for back in range(exp_count)]
    all_residual = [over_exp(residual[0], back) for back in range(exp_count)]

    vmem = pl.BlockSpec(memory_space=pltpu.VMEM)
    smem = pl.BlockSpec(memory_space=pltpu.SMEM)
    pieces = pl.pallas_call(
        functools.partial(attention_kernel, heads // groups, pair),
        out_shape=[jax.ShapeDtypeStruct((part_rows, heads * head_size), jnp.bfloat16)] * pair,
        in_specs=[smem] + [vmem] * (2 + len(packs)),
        out_specs=[vmem] * pair,
        compiler_params=pltpu.CompilerParams(vmem_limit_bytes=VMEM_LIMIT),
    )(
        core.reshape(1),
        queries[0].transpose(1, 0, 2),
        (doc_ids + 1).astype(jnp.float32).reshape(tokens, 1),
        *packs,
    )

    arrived = {}
    for step in range(ctx_count):
        for turn in range(pair):
            moves = [
                (z * pair + c, (z + step) % ctx_count * pair + (c + turn) % pair)
                for z in range(ctx_count)
                for c in range(pair)
            ]
            arrived[step, turn] = (
                pieces[0]
                if step == 0 and turn == 0
                else lax.ppermute(pieces[turn], ("ctx", "tp"), moves)
            )
    order = sorted(range(ctx_count), key=lambda step: min(step, ctx_count - step))
    chunks = {}
    for step in order:
        total = sum(
            jnp.dot(arrived[step, turn], weights[turn], preferred_element_type=jnp.float32)
            for turn in range(pair)
        ).astype(jnp.bfloat16)
        away = (ctx_count - step) % ctx_count
        if away:
            total = lax.ppermute(
                total, "ctx", [(z, (z + away) % ctx_count) for z in range(ctx_count)]
            )
        chunks[step] = total
    steps = ctx_count
    if columns % 128:
        steps = 1
        whole = jnp.roll(jnp.stack([chunks[step] for step in range(ctx_count)]), ctx_index, axis=0)
        chunks = {0: whole.transpose(1, 0, 2).reshape(part_rows, width)}
    flat = [over_exp(chunks[step], back) for step in range(steps) for back in range(exp_count)]
    out = pl.pallas_call(
        functools.partial(finish_kernel, steps, exp_count),
        out_shape=jax.ShapeDtypeStruct(
            (exp_count, router.shape[1] * CAP, width), jnp.bfloat16
        ),
        in_specs=[smem] + [vmem] * (len(flat) + 2 * exp_count + 3),
        out_specs=vmem,
        scratch_shapes=[
            pltpu.VMEM((part_rows, width), jnp.float32),
            pltpu.VMEM((part_rows, width), jnp.bfloat16),
        ],
        compiler_params=pltpu.CompilerParams(vmem_limit_bytes=VMEM_LIMIT),
    )(
        jnp.stack([ctx_index, exp_index]),
        *flat,
        *all_residual,
        *all_ids,
        keep_counts.reshape(1, -1),
        norm_gain.reshape(1, -1),
        router.T,
    )
    return out.reshape(exp_count, router.shape[1], CAP, width)


def solution(mesh):
    placed = (
        P(("groups", "exp"), "ctx", "tp", None),
        P(("groups", "exp"), "ctx", "tp", None),
        P(("groups", "exp"), "ctx", "tp", None),
        P(("groups", "exp"), "ctx"),
        P(("groups", "exp"), ("ctx", "tp"), None),
        P("tp", "ctx"),
        P(),
        P(None, "exp"),
        P(("groups", "exp"), ("ctx", "tp"), None),
        P("groups"),
    )
    return jax.shard_map(
        on_device,
        mesh=mesh,
        in_specs=placed,
        out_specs=P(("groups", "ctx", "tp"), "exp", None, None),
        check_vma=False,
    )
```

time: 173 us -> 92.6 us (0.54)
  blocking collectives: 60.6 us -> 0 us
  waiting for transfers between devices: 56.6 us -> 11.7 us
  starting transfers between devices: 4.93 us -> 49.3 us
  between operations: 13.6 us -> 0.22 us
  matrix products: 19.5 us -> 13.2 us
  Pallas kernels: 0 us -> 4.78 us
  other arithmetic: 4.83 us -> 0.75 us
    ppermute x0 -> x19, starting transfers between devices: none -> 49.3 us  [the longest x7 25.5 us: on_device(): lax.ppermute(pieces[turn], ('ctx', 'tp'), moves)]
    all_gather x3 -> x0, blocking collectives: 40.9 us -> none  [the longest x1 14.2 us: on_device(): value_piece = lax.all_gather(values, 'ctx', axis=1, tiled=True)]
    all_gather x1 -> x0, waiting for transfers between devices: 31.1 us -> none  [on_device(): gathered = lax.all_gather(attn_rows, 'ctx', axis=1, tiled=True)]
    all_to_all x1 -> x0, blocking collectives: 19.7 us -> none  [on_device(): lax.all_to_all(outgoing, 'exp', split_axis=0, concat_axis=0, tiled=True)]
    all_to_all x1 -> x0, waiting for transfers between devices: 17.5 us -> none  [on_device(): lax.all_to_all(own_columns.astype(jnp.bfloat16), 'ctx', split_axis=0, con...]
    ppermute x0 -> x19, waiting for transfers between devices: none -> 11.7 us  [the longest x6 7.02 us: over_exp(): lax.ppermute(array, 'exp', [(i, (i + back) % exp_count) for i in range(ex...]
    reduce_scatter x1 -> x0, waiting for transfers between devices: 7.92 us -> none  [on_device(): lax.psum_scatter(jnp.dot(gathered, out_proj, preferred_element_type=jnp.f...]
    unnamed x17 -> x34, local copies, waits for them, and re-layouts: 2.16 us -> 8.89 us
  transfers between devices with their start and end apart: 3 -> 19, of which waited for: 3 -> 6; matrix products, arithmetic and copies ran while one was open for 0% -> 17% of each run, Pallas kernels for 0% -> 3%
where the time goes in v1:
time: 92.6 us; the launch traced here: 92.1 us
  starting transfers between devices  49.3 us (53%)
  matrix products  13.2 us (14%)
  local copies, waits for them, and re-layouts  12.1 us (13%)
  waiting for transfers between devices  11.7 us (13%)
  Pallas kernels  4.78 us (5%)
    ppermute x7, starting transfers between devices, on_device(): lax.ppermute(pieces[turn], ('ctx', 'tp'), moves)  25.5 us
    dot_general x8, matrix products, on_device(): jnp.dot(arrived[step, turn], weights[turn], preferred_element_type=jnp.fl...  13.2 us
    ppermute x2, starting transfers between devices, on_device(): lax.ppermute(pack, 'ctx', [(i, i + step) for i in range(ctx_count - step)])  8.98 us
    unnamed x34, local copies, waits for them, and re-layouts  8.89 us
    ppermute x3, starting transfers between devices, on_device(): lax.ppermute(total, 'ctx', [(z, (z + away) % ctx_count) for z in range(ct...  7.25 us
    ppermute x6, starting transfers between devices, over_exp(): lax.ppermute(array, 'exp', [(i, (i + back) % exp_count) for i in range(ex...  7.1 us
    ppermute x6, waiting for transfers between devices, over_exp(): lax.ppermute(array, 'exp', [(i, (i + back) % exp_count) for i in range(ex...  7.02 us
    ppermute x2, waiting for transfers between devices, on_device(): lax.ppermute(pack, 'ctx', [(i, i + step) for i in range(ctx_count - step)])  3.14 us
  transfers between devices with their start and end apart: 19, of which 6 were waited for; matrix products, arithmetic and copies ran while one was open for 17% of the time, Pallas kernels for 3%

profile of v1, /device:TPU:0, one launch (start us, length us, event | category | flops | bytes accessed | tf_op | source)
XLA Modules:
  0.0 92.1 jit_solution(3403279630648764975)
XLA Ops:
  2.8 4.5 %collective-permute-start = (bf16[528,128]{1,0:T(8,128)(2,1)S(1)}, bf16[528,128]{1,0:T(8,128)(2,1)S(1)}, u32[]{:S(2)}, u32[]{:S(2)}) collective-permute-start(bf16[528,128]{1,0:T(8,128)(2,1)S(1)} %pad_maximum_fusion.refs_0_), channel_id=1, source_target_pairs={{0,4},{4,8},{8,12},{1,5},{5,9},{9,13},{2,6},{6,10},{10,14},{3,7},{... | collective-permute-start | bytes 405512 | tf_op jit(solution)/shard_map/ppermute | solution.py:153
  7.3 4.5 %collective-permute-start.1 = (bf16[528,128]{1,0:T(8,128)(2,1)S(1)}, bf16[528,128]{1,0:T(8,128)(2,1)S(1)}, u32[]{:S(2)}, u32[]{:S(2)}) collective-permute-start(bf16[528,128]{1,0:T(8,128)(2,1)S(1)} %pad_maximum_fusion.refs_0_), channel_id=1, source_target_pairs={{0,8},{4,12},{1,9},{5,13},{2,10},{6,14},{3,11},{7,15},{16,24},{20,... | collective-permute-start | bytes 405512 | tf_op jit(solution)/shard_map/ppermute | solution.py:153
  12.0 3.1 %collective-permute-done.1.refs_2_ = bf16[528,128]{1,0:T(8,128)(2,1)S(1)} collective-permute-done((bf16[528,128]{1,0:T(8,128)(2,1)S(1)}, bf16[528,128]{1,0:T(8,128)(2,1)S(1)}, u32[]{:S(2)}, u32[]{:S(2)}) %collective-permute-start.1) | collective-permute-done | bytes 135200 | tf_op jit(solution)/shard_map/ppermute | solution.py:153
  15.1 1.0 %copy-done.2 = bf16[1,128,10,128]{3,1,2,0:T(8,128)(2,1)S(1)} copy-done((bf16[1,128,10,128]{3,1,2,0:T(8,128)(2,1)S(1)}, bf16[1,128,10,128]{3,1,2,0:T(8,128)(2,1)}, u32[]{:S(2)}) %copy-start.2) | copy-done | bytes 327704
  16.1 2.7 %shard_map.100 = (bf16[64,1280]{1,0:T(8,128)(2,1)S(1)}, bf16[64,1280]{1,0:T(8,128)(2,1)S(1)}) custom-call(s32[1]{0:T(128)} %bitcast.2.core_ref, bf16[10,128,128]{2,1,0:T(8,128)(2,1)S(1)} %bitcast.41, f32[128,1]{1,0:T(8,128)S(1)} %copy.13.doc_ref, bf16[528,128]{1,0:T(8,128)(2,1)S(1)} %pad_maximum_fusion.refs_0_, ...), custom_call_target="tpu_custom_call" | custom-call | tf_op jit(solution)/shard_map/pallas_call | solution.py:174
  18.8 2.5 %collective-permute-start.10 = (bf16[64,1280]{1,0:T(8,128)(2,1)S(1)}, bf16[64,1280]{1,0:T(8,128)(2,1)S(1)}, u32[]{:S(2)}, u32[]{:S(2)}) collective-permute-start(bf16[64,1280]{1,0:T(8,128)(2,1)S(1)} %get-tuple-element.8), channel_id=1, source_target_pairs={{0,9},{1,8},{4,13},{5,12},{8,1},{9,0},{12,5},{13,4},{2,11},{3,10},... | collective-permute-start | bytes 491528 | tf_op jit(solution)/shard_map/ppermute | solution.py:198
  21.3 1.5 %collective-permute-start.17 = (bf16[64,5120]{1,0:T(8,128)(2,1)}, bf16[64,5120]{1,0:T(8,128)(2,1)S(1)}, u32[]{:S(2)}, u32[]{:S(2)}) collective-permute-start(bf16[64,5120]{1,0:T(8,128)(2,1)} %bitcast.38), channel_id=1, source_target_pairs={{0,2},{2,0},{1,3},{3,1},{4,6},{6,4},{5,7},{7,5},{8,10},{10,8},{9,1... | collective-permute-start | bytes 1966088 | tf_op jit(solution)/shard_map/ppermute | solution.py:164
  23.3 2.4 %collective-permute-start.14 = (bf16[64,1280]{1,0:T(8,128)(2,1)S(1)}, bf16[64,1280]{1,0:T(8,128)(2,1)S(1)}, u32[]{:S(2)}, u32[]{:S(2)}) collective-permute-start(bf16[64,1280]{1,0:T(8,128)(2,1)S(1)} %get-tuple-element.8), channel_id=1, source_target_pairs={{0,13},{1,12},{4,1},{5,0},{8,5},{9,4},{12,9},{13,8},{2,15},{3,14},... | collective-permute-start | bytes 491528 | tf_op jit(solution)/shard_map/ppermute | solution.py:198
  25.7 3.7 %collective-permute-start.9 = (bf16[64,1280]{1,0:T(8,128)(2,1)S(1)}, bf16[64,1280]{1,0:T(8,128)(2,1)S(1)}, u32[]{:S(2)}, u32[]{:S(2)}) collective-permute-start(bf16[64,1280]{1,0:T(8,128)(2,1)S(1)} %get-tuple-element.7), channel_id=1, source_target_pairs={{0,8},{1,9},{4,12},{5,13},{8,0},{9,1},{12,4},{13,5},{2,10},{3,11},... | collective-permute-start | bytes 491528 | tf_op jit(solution)/shard_map/ppermute | solution.py:198
  29.3 11.3 %collective-permute-start.13 = (bf16[64,1280]{1,0:T(8,128)(2,1)S(1)}, bf16[64,1280]{1,0:T(8,128)(2,1)S(1)}, u32[]{:S(2)}, u32[]{:S(2)}) collective-permute-start(bf16[64,1280]{1,0:T(8,128)(2,1)S(1)} %get-tuple-element.7), channel_id=1, source_target_pairs={{0,12},{1,13},{4,0},{5,1},{8,4},{9,5},{12,8},{13,9},{2,14},{3,15},... | collective-permute-start | bytes 491528 | tf_op jit(solution)/shard_map/ppermute | solution.py:198
  40.7 2.6 %fusion.6 = f32[64,1280]{1,0:T(8,128)S(1)} fusion(bf16[64,1280]{1,0:T(8,128)(2,1)S(1)} %collective-permute-done.10, bf16[1280,1280]{1,0:T(8,128)(2,1)} %collective-permute-done.3), kind=kOutput, calls=%fused_computation.14 | convolution fusion | flops 209715200 | bytes 3768320 | tf_op jit(solution)/shard_map/dot_general | solution.py:204
  43.3 4.1 %collective-permute-start.6 = (bf16[64,1280]{1,0:T(8,128)(2,1)S(1)}, bf16[64,1280]{1,0:T(8,128)(2,1)S(1)}, u32[]{:S(2)}, u32[]{:S(2)}) collective-permute-start(bf16[64,1280]{1,0:T(8,128)(2,1)S(1)} %get-tuple-element.8), channel_id=1, source_target_pairs={{0,5},{1,4},{4,9},{5,8},{8,13},{9,12},{12,1},{13,0},{2,7},{3,6},{6... | collective-permute-start | bytes 491528 | tf_op jit(solution)/shard_map/ppermute | solution.py:198
  48.1 1.4 %collective-permute-start.5 = (bf16[64,1280]{1,0:T(8,128)(2,1)S(1)}, bf16[64,1280]{1,0:T(8,128)(2,1)S(1)}, u32[]{:S(2)}, u32[]{:S(2)}) collective-permute-start(bf16[64,1280]{1,0:T(8,128)(2,1)S(1)} %get-tuple-element.7), channel_id=1, source_target_pairs={{0,4},{1,5},{4,8},{5,9},{8,12},{9,13},{12,0},{13,1},{2,6},{3,7},{6... | collective-permute-start | bytes 491528 | tf_op jit(solution)/shard_map/ppermute | solution.py:198
  49.5 2.6 %fusion.7 = f32[64,1280]{1,0:T(8,128)S(1)} fusion(bf16[64,1280]{1,0:T(8,128)(2,1)S(1)} %collective-permute-done.14, bf16[1280,1280]{1,0:T(8,128)(2,1)} %collective-permute-done.3), kind=kOutput, calls=%fused_computation.15 | convolution fusion | flops 209715200 | bytes 3768320 | tf_op jit(solution)/shard_map/dot_general | solution.py:204
  53.2 3.3 %collective-permute-start.11 = (bf16[64,1280]{1,0:T(8,128)(2,1)S(1)}, bf16[64,1280]{1,0:T(8,128)(2,1)S(1)}, u32[]{:S(2)}, u32[]{:S(2)}) collective-permute-start(bf16[64,1280]{1,0:T(8,128)(2,1)S(1)} %fusion.2), channel_id=1, source_target_pairs={{0,8},{4,12},{8,0},{12,4},{1,9},{5,13},{9,1},{13,5},{2,10},{6,14},... | collective-permute-start | bytes 491528 | tf_op jit(solution)/shard_map/ppermute | solution.py:209
  56.5 2.6 %fusion.5 = f32[64,1280]{1,0:T(8,128)S(1)} fusion(bf16[64,1280]{1,0:T(8,128)(2,1)S(1)} %collective-permute-done.6, bf16[1280,1280]{1,0:T(8,128)(2,1)} %collective-permute-done.3), kind=kOutput, calls=%fused_computation.13 | convolution fusion | flops 209715200 | bytes 3768320 | tf_op jit(solution)/shard_map/dot_general | solution.py:204
  59.1 2.1 %collective-permute-start.15 = (bf16[64,1280]{1,0:T(8,128)(2,1)S(1)}, bf16[64,1280]{1,0:T(8,128)(2,1)S(1)}, u32[]{:S(2)}, u32[]{:S(2)}) collective-permute-start(bf16[64,1280]{1,0:T(8,128)(2,1)S(1)} %fusion.3), channel_id=1, source_target_pairs={{0,4},{4,8},{8,12},{12,0},{1,5},{5,9},{9,13},{13,1},{2,6},{6,10},{... | collective-permute-start | bytes 491528 | tf_op jit(solution)/shard_map/ppermute | solution.py:209
  62.0 1.8 %collective-permute-start.7 = (bf16[64,1280]{1,0:T(8,128)(2,1)S(1)}, bf16[64,1280]{1,0:T(8,128)(2,1)S(1)}, u32[]{:S(2)}, u32[]{:S(2)}) collective-permute-start(bf16[64,1280]{1,0:T(8,128)(2,1)S(1)} %fusion.1), channel_id=1, source_target_pairs={{0,12},{4,0},{8,4},{12,8},{1,13},{5,1},{9,5},{13,9},{2,14},{6,2},{... | collective-permute-start | bytes 491528 | tf_op jit(solution)/shard_map/ppermute | solution.py:209
  63.8 2.6 %fusion.4 = f32[64,1280]{1,0:T(8,128)S(1)} fusion(bf16[64,1280]{1,0:T(8,128)(2,1)S(1)} %collective-permute-done.2, bf16[1280,1280]{1,0:T(8,128)(2,1)} %collective-permute-done.3), kind=kOutput, calls=%fused_computation.12 | convolution fusion | flops 209715200 | bytes 3768320 | tf_op jit(solution)/shard_map/dot_general | solution.py:204
  67.2 1.6 %collective-permute-start.4 = (bf16[64,1280]{1,0:T(8,128)(2,1)S(1)}, bf16[64,1280]{1,0:T(8,128)(2,1)S(1)}, u32[]{:S(2)}, u32[]{:S(2)}) collective-permute-start(bf16[64,1280]{1,0:T(8,128)(2,1)S(1)} %fusion.refs_0_), channel_id=1, source_target_pairs={{0,2},{2,0},{1,3},{3,1},{4,6},{6,4},{5,7},{7,5},{8,10},{10,8},{9,1... | collective-permute-start | bytes 491528 | tf_op jit(solution)/shard_map/ppermute | solution.py:164
  68.8 1.1 %collective-permute-start.12 = (bf16[64,1280]{1,0:T(8,128)(2,1)S(1)}, bf16[64,1280]{1,0:T(8,128)(2,1)S(1)}, u32[]{:S(2)}, u32[]{:S(2)}) collective-permute-start(bf16[64,1280]{1,0:T(8,128)(2,1)S(1)} %collective-permute-done.11.refs_4_), channel_id=1, source_target_pairs={{0,2},{2,0},{1,3},{3,1},{4,6},{6,4},{5,7},{7,5},{8,10},{10,8},{9,1... | collective-permute-start | bytes 491528 | tf_op jit(solution)/shard_map/ppermute | solution.py:164
  69.8 0.9 %collective-permute-start.16 = (bf16[64,1280]{1,0:T(8,128)(2,1)S(1)}, bf16[64,1280]{1,0:T(8,128)(2,1)S(1)}, u32[]{:S(2)}, u32[]{:S(2)}) collective-permute-start(bf16[64,1280]{1,0:T(8,128)(2,1)S(1)} %collective-permute-done.15.refs_6_), channel_id=1, source_target_pairs={{0,2},{2,0},{1,3},{3,1},{4,6},{6,4},{5,7},{7,5},{8,10},{10,8},{9,1... | collective-permute-start | bytes 491528 | tf_op jit(solution)/shard_map/ppermute | solution.py:164
  70.8 1.4 %collective-permute-done.7.refs_2_ = bf16[64,1280]{1,0:T(8,128)(2,1)S(1)} collective-permute-done((bf16[64,1280]{1,0:T(8,128)(2,1)S(1)}, bf16[64,1280]{1,0:T(8,128)(2,1)S(1)}, u32[]{:S(2)}, u32[]{:S(2)}) %collective-permute-start.7) | collective-permute-done | bytes 163872 | tf_op jit(solution)/shard_map/ppermute | solution.py:209
  72.2 1.5 %collective-permute-start.8 = (bf16[64,1280]{1,0:T(8,128)(2,1)S(1)}, bf16[64,1280]{1,0:T(8,128)(2,1)S(1)}, u32[]{:S(2)}, u32[]{:S(2)}) collective-permute-start(bf16[64,1280]{1,0:T(8,128)(2,1)S(1)} %collective-permute-done.7.refs_2_), channel_id=1, source_target_pairs={{0,2},{2,0},{1,3},{3,1},{4,6},{6,4},{5,7},{7,5},{8,10},{10,8},{9,1... | collective-permute-start | bytes 491528 | tf_op jit(solution)/shard_map/ppermute | solution.py:164
  75.1 2.0 %collective-permute-done.12.refs_5_ = bf16[64,1280]{1,0:T(8,128)(2,1)S(1)} collective-permute-done((bf16[64,1280]{1,0:T(8,128)(2,1)S(1)}, bf16[64,1280]{1,0:T(8,128)(2,1)S(1)}, u32[]{:S(2)}, u32[]{:S(2)}) %collective-permute-start.12) | collective-permute-done | bytes 163872 | tf_op jit(solution)/shard_map/ppermute | solution.py:164
  77.7 2.8 %collective-permute-done.16.refs_7_ = bf16[64,1280]{1,0:T(8,128)(2,1)S(1)} collective-permute-done((bf16[64,1280]{1,0:T(8,128)(2,1)S(1)}, bf16[64,1280]{1,0:T(8,128)(2,1)S(1)}, u32[]{:S(2)}, u32[]{:S(2)}) %collective-permute-start.16) | collective-permute-done | bytes 163872 | tf_op jit(solution)/shard_map/ppermute | solution.py:164
  81.2 2.2 %collective-permute-done.8.refs_3_ = bf16[64,1280]{1,0:T(8,128)(2,1)S(1)} collective-permute-done((bf16[64,1280]{1,0:T(8,128)(2,1)S(1)}, bf16[64,1280]{1,0:T(8,128)(2,1)S(1)}, u32[]{:S(2)}, u32[]{:S(2)}) %collective-permute-start.8) | collective-permute-done | bytes 163872 | tf_op jit(solution)/shard_map/ppermute | solution.py:164
  85.0 0.9 copy-done.6
  85.9 0.9 copy-done.8
  87.8 0.9 copy-done.12
  88.7 2.1 %shard_map.101 = bf16[2,64,5120]{2,1,0:T(8,128)(2,1)S(1)} custom-call(s32[2]{0:T(128)S(1)} %pad_add_fusion.place_ref, bf16[64,1280]{1,0:T(8,128)(2,1)S(1)} %fusion.refs_0_, bf16[64,1280]{1,0:T(8,128)(2,1)S(1)} %copy-done.6, bf16[64,1280]{1,0:T(8,128)(2,1)S(1)} %copy-done.4, bf16[64,1280]{1,0:T(8,128)(2,1)S(1)} %copy-done.12, ...), custom_call_target="tpu_custom_call" | custom-call | tf_op jit(solution)/shard_map/pallas_call | solution.py:219
  90.7 1.4 %reshape.27 = bf16[2,32,2,5120]{3,2,1,0:T(2,128)(2,1)} reshape(bf16[2,64,5120]{2,1,0:T(8,128)(2,1)S(1)} %shard_map.101) | data formatting | bytes 2621440 | tf_op jit(solution)/shard_map/reshape | solution.py:240
  (59 shorter events, 11.9 us)
Async XLA Ops:
  0.0 29.3 %collective-permute-start.3 = (bf16[1280,1280]{1,0:T(8,128)(2,1)}, bf16[1280,1280]{1,0:T(8,128)(2,1)}, u32[]{:S(2)}, u32[]{:S(2)}) collective-permute-start(bf16[1280,1280]{1,0:T(8,128)(2,1)} %param.15), channel_id=1, source_target_pairs={{0,1},{1,0},{2,3},{3,2},{4,5},{5,4},{6,7},{7,6},{8,9},{9,8},{10,11... | collective-permute-start | bytes 9830408 | tf_op jit(solution)/shard_map/ppermute | solution.py:157
  2.8 9.1 %collective-permute-start = (bf16[528,128]{1,0:T(8,128)(2,1)S(1)}, bf16[528,128]{1,0:T(8,128)(2,1)S(1)}, u32[]{:S(2)}, u32[]{:S(2)}) collective-permute-start(bf16[528,128]{1,0:T(8,128)(2,1)S(1)} %pad_maximum_fusion.refs_0_), channel_id=1, source_target_pairs={{0,4},{4,8},{8,12},{1,5},{5,9},{9,13},{2,6},{6,10},{10,14},{3,7},{... | collective-permute-start | bytes 405512 | tf_op jit(solution)/shard_map/ppermute | solution.py:153
  7.3 7.8 %collective-permute-start.1 = (bf16[528,128]{1,0:T(8,128)(2,1)S(1)}, bf16[528,128]{1,0:T(8,128)(2,1)S(1)}, u32[]{:S(2)}, u32[]{:S(2)}) collective-permute-start(bf16[528,128]{1,0:T(8,128)(2,1)S(1)} %pad_maximum_fusion.refs_0_), channel_id=1, source_target_pairs={{0,8},{4,12},{1,9},{5,13},{2,10},{6,14},{3,11},{7,15},{16,24},{20,... | collective-permute-start | bytes 405512 | tf_op jit(solution)/shard_map/ppermute | solution.py:153
  15.1 1.0 %copy-start.2 = (bf16[1,128,10,128]{3,1,2,0:T(8,128)(2,1)S(1)}, bf16[1,128,10,128]{3,1,2,0:T(8,128)(2,1)}, u32[]{:S(2)}) copy-start(bf16[1,128,10,128]{3,1,2,0:T(8,128)(2,1)} %param.10) | copy-start | bytes 983044
  16.1 31.3 %copy-start.15 = (bf16[1280,1280]{1,0:T(8,128)(2,1)S(1)}, bf16[1280,1280]{1,0:T(8,128)(2,1)}, u32[]{:S(2)}) copy-start(bf16[1280,1280]{1,0:T(8,128)(2,1)} %param.15) | copy-start | bytes 9830404
  18.8 6.9 %collective-permute-start.10 = (bf16[64,1280]{1,0:T(8,128)(2,1)S(1)}, bf16[64,1280]{1,0:T(8,128)(2,1)S(1)}, u32[]{:S(2)}, u32[]{:S(2)}) collective-permute-start(bf16[64,1280]{1,0:T(8,128)(2,1)S(1)} %get-tuple-element.8), channel_id=1, source_target_pairs={{0,9},{1,8},{4,13},{5,12},{8,1},{9,0},{12,5},{13,4},{2,11},{3,10},... | collective-permute-start | bytes 491528 | tf_op jit(solution)/shard_map/ppermute | solution.py:198
  21.3 53.1 %collective-permute-start.17 = (bf16[64,5120]{1,0:T(8,128)(2,1)}, bf16[64,5120]{1,0:T(8,128)(2,1)S(1)}, u32[]{:S(2)}, u32[]{:S(2)}) collective-permute-start(bf16[64,5120]{1,0:T(8,128)(2,1)} %bitcast.38), channel_id=1, source_target_pairs={{0,2},{2,0},{1,3},{3,1},{4,6},{6,4},{5,7},{7,5},{8,10},{10,8},{9,1... | collective-permute-start | bytes 1966088 | tf_op jit(solution)/shard_map/ppermute | solution.py:164
  22.8 44.4 %collective-permute-start.18 = (s32[1,64]{1,0:T(1,128)}, s32[1,64]{1,0:T(1,128)S(1)}, u32[]{:S(2)}, u32[]{:S(2)}) collective-permute-start(s32[1,64]{1,0:T(1,128)} %bitcast.42), channel_id=1, source_target_pairs={{0,2},{2,0},{1,3},{3,1},{4,6},{6,4},{5,7},{7,5},{8,10},{10,8},{9,1... | collective-permute-start | bytes 776 | tf_op jit(solution)/shard_map/ppermute | solution.py:164
  23.3 24.8 %collective-permute-start.14 = (bf16[64,1280]{1,0:T(8,128)(2,1)S(1)}, bf16[64,1280]{1,0:T(8,128)(2,1)S(1)}, u32[]{:S(2)}, u32[]{:S(2)}) collective-permute-start(bf16[64,1280]{1,0:T(8,128)(2,1)S(1)} %get-tuple-element.8), channel_id=1, source_target_pairs={{0,13},{1,12},{4,1},{5,0},{8,5},{9,4},{12,9},{13,8},{2,15},{3,14},... | collective-permute-start | bytes 491528 | tf_op jit(solution)/shard_map/ppermute | solution.py:198
  25.7 17.6 %collective-permute-start.9 = (bf16[64,1280]{1,0:T(8,128)(2,1)S(1)}, bf16[64,1280]{1,0:T(8,128)(2,1)S(1)}, u32[]{:S(2)}, u32[]{:S(2)}) collective-permute-start(bf16[64,1280]{1,0:T(8,128)(2,1)S(1)} %get-tuple-element.7), channel_id=1, source_target_pairs={{0,8},{1,9},{4,12},{5,13},{8,0},{9,1},{12,4},{13,5},{2,10},{3,11},... | collective-permute-start | bytes 491528 | tf_op jit(solution)/shard_map/ppermute | solution.py:198
  29.3 22.8 %collective-permute-start.13 = (bf16[64,1280]{1,0:T(8,128)(2,1)S(1)}, bf16[64,1280]{1,0:T(8,128)(2,1)S(1)}, u32[]{:S(2)}, u32[]{:S(2)}) collective-permute-start(bf16[64,1280]{1,0:T(8,128)(2,1)S(1)} %get-tuple-element.7), channel_id=1, source_target_pairs={{0,12},{1,13},{4,0},{5,1},{8,4},{9,5},{12,8},{13,9},{2,14},{3,15},... | collective-permute-start | bytes 491528 | tf_op jit(solution)/shard_map/ppermute | solution.py:198
  43.3 9.9 %collective-permute-start.6 = (bf16[64,1280]{1,0:T(8,128)(2,1)S(1)}, bf16[64,1280]{1,0:T(8,128)(2,1)S(1)}, u32[]{:S(2)}, u32[]{:S(2)}) collective-permute-start(bf16[64,1280]{1,0:T(8,128)(2,1)S(1)} %get-tuple-element.8), channel_id=1, source_target_pairs={{0,5},{1,4},{4,9},{5,8},{8,13},{9,12},{12,1},{13,0},{2,7},{3,6},{6... | collective-permute-start | bytes 491528 | tf_op jit(solution)/shard_map/ppermute | solution.py:198
  48.1 11.1 %collective-permute-start.5 = (bf16[64,1280]{1,0:T(8,128)(2,1)S(1)}, bf16[64,1280]{1,0:T(8,128)(2,1)S(1)}, u32[]{:S(2)}, u32[]{:S(2)}) collective-permute-start(bf16[64,1280]{1,0:T(8,128)(2,1)S(1)} %get-tuple-element.7), channel_id=1, source_target_pairs={{0,4},{1,5},{4,8},{5,9},{8,12},{9,13},{12,0},{13,1},{2,6},{3,7},{6... | collective-permute-start | bytes 491528 | tf_op jit(solution)/shard_map/ppermute | solution.py:198
  52.1 9.9 %collective-permute-start.2 = (bf16[64,1280]{1,0:T(8,128)(2,1)S(1)}, bf16[64,1280]{1,0:T(8,128)(2,1)S(1)}, u32[]{:S(2)}, u32[]{:S(2)}) collective-permute-start(bf16[64,1280]{1,0:T(8,128)(2,1)S(1)} %get-tuple-element.8), channel_id=1, source_target_pairs={{0,1},{1,0},{4,5},{5,4},{8,9},{9,8},{12,13},{13,12},{2,3},{3,2},{6... | collective-permute-start | bytes 491528 | tf_op jit(solution)/shard_map/ppermute | solution.py:198
  53.2 15.6 %collective-permute-start.11 = (bf16[64,1280]{1,0:T(8,128)(2,1)S(1)}, bf16[64,1280]{1,0:T(8,128)(2,1)S(1)}, u32[]{:S(2)}, u32[]{:S(2)}) collective-permute-start(bf16[64,1280]{1,0:T(8,128)(2,1)S(1)} %fusion.2), channel_id=1, source_target_pairs={{0,8},{4,12},{8,0},{12,4},{1,9},{5,13},{9,1},{13,5},{2,10},{6,14},... | collective-permute-start | bytes 491528 | tf_op jit(solution)/shard_map/ppermute | solution.py:209
  59.1 10.7 %collective-permute-start.15 = (bf16[64,1280]{1,0:T(8,128)(2,1)S(1)}, bf16[64,1280]{1,0:T(8,128)(2,1)S(1)}, u32[]{:S(2)}, u32[]{:S(2)}) collective-permute-start(bf16[64,1280]{1,0:T(8,128)(2,1)S(1)} %fusion.3), channel_id=1, source_target_pairs={{0,4},{4,8},{8,12},{12,0},{1,5},{5,9},{9,13},{13,1},{2,6},{6,10},{... | collective-permute-start | bytes 491528 | tf_op jit(solution)/shard_map/ppermute | solution.py:209
  62.0 12.3 %copy-start.16 = (bf16[5120]{0:T(1024)(128)(2,1)S(1)}, bf16[5120]{0:T(1024)(128)(2,1)}, u32[]{:S(2)}) copy-start(bf16[5120]{0:T(1024)(128)(2,1)} %param.16) | copy-start | bytes 30724
  62.0 22.1 %copy-start = (bf16[1,64,5120]{2,1,0:T(8,128)(2,1)S(1)}, bf16[1,64,5120]{2,1,0:T(8,128)(2,1)}, u32[]{:S(2)}) copy-start(bf16[1,64,5120]{2,1,0:T(8,128)(2,1)} %param.14) | copy-start | bytes 1966084
  62.0 22.1 %copy-start.1 = (bf16[5120,32]{0,1:T(8,128)(2,1)S(1)}, bf16[5120,32]{0,1:T(8,128)(2,1)}, u32[]{:S(2)}) copy-start(bf16[5120,32]{0,1:T(8,128)(2,1)} %param.17) | copy-start | bytes 983044
  62.0 22.1 %copy-start.13 = (s32[1,64,1]{1,2,0:T(1,128)S(1)}, s32[1,64,1]{1,2,0:T(1,128)}, u32[]{:S(2)}) copy-start(s32[1,64,1]{1,2,0:T(1,128)} %param.18) | copy-start | bytes 772
  62.0 22.1 %copy-start.14 = (s32[64]{0:T(128)S(1)}, s32[64]{0:T(128)}, u32[]{:S(2)}) copy-start(s32[64]{0:T(128)} %param.19) | copy-start | bytes 772
  62.0 10.1 %collective-permute-start.7 = (bf16[64,1280]{1,0:T(8,128)(2,1)S(1)}, bf16[64,1280]{1,0:T(8,128)(2,1)S(1)}, u32[]{:S(2)}, u32[]{:S(2)}) collective-permute-start(bf16[64,1280]{1,0:T(8,128)(2,1)S(1)} %fusion.1), channel_id=1, source_target_pairs={{0,12},{4,0},{8,4},{12,8},{1,13},{5,1},{9,5},{13,9},{2,14},{6,2},{... | collective-permute-start | bytes 491528 | tf_op jit(solution)/shard_map/ppermute | solution.py:209
  67.2 7.2 %collective-permute-start.4 = (bf16[64,1280]{1,0:T(8,128)(2,1)S(1)}, bf16[64,1280]{1,0:T(8,128)(2,1)S(1)}, u32[]{:S(2)}, u32[]{:S(2)}) collective-permute-start(bf16[64,1280]{1,0:T(8,128)(2,1)S(1)} %fusion.refs_0_), channel_id=1, source_target_pairs={{0,2},{2,0},{1,3},{3,1},{4,6},{6,4},{5,7},{7,5},{8,10},{10,8},{9,1... | collective-permute-start | bytes 491528 | tf_op jit(solution)/shard_map/ppermute | solution.py:164
  68.8 8.3 %collective-permute-start.12 = (bf16[64,1280]{1,0:T(8,128)(2,1)S(1)}, bf16[64,1280]{1,0:T(8,128)(2,1)S(1)}, u32[]{:S(2)}, u32[]{:S(2)}) collective-permute-start(bf16[64,1280]{1,0:T(8,128)(2,1)S(1)} %collective-permute-done.11.refs_4_), channel_id=1, source_target_pairs={{0,2},{2,0},{1,3},{3,1},{4,6},{6,4},{5,7},{7,5},{8,10},{10,8},{9,1... | collective-permute-start | bytes 491528 | tf_op jit(solution)/shard_map/ppermute | solution.py:164
  69.8 10.7 %collective-permute-start.16 = (bf16[64,1280]{1,0:T(8,128)(2,1)S(1)}, bf16[64,1280]{1,0:T(8,128)(2,1)S(1)}, u32[]{:S(2)}, u32[]{:S(2)}) collective-permute-start(bf16[64,1280]{1,0:T(8,128)(2,1)S(1)} %collective-permute-done.15.refs_6_), channel_id=1, source_target_pairs={{0,2},{2,0},{1,3},{3,1},{4,6},{6,4},{5,7},{7,5},{8,10},{10,8},{9,1... | collective-permute-start | bytes 491528 | tf_op jit(solution)/shard_map/ppermute | solution.py:164
  72.2 11.3 %collective-permute-start.8 = (bf16[64,1280]{1,0:T(8,128)(2,1)S(1)}, bf16[64,1280]{1,0:T(8,128)(2,1)S(1)}, u32[]{:S(2)}, u32[]{:S(2)}) collective-permute-start(bf16[64,1280]{1,0:T(8,128)(2,1)S(1)} %collective-permute-done.7.refs_2_), channel_id=1, source_target_pairs={{0,2},{2,0},{1,3},{3,1},{4,6},{6,4},{5,7},{7,5},{8,10},{10,8},{9,1... | collective-permute-start | bytes 491528 | tf_op jit(solution)/shard_map/ppermute | solution.py:164
  74.4 0.7 copy-start.5
  84.1 0.9 copy-start.4
  85.0 0.9 copy-start.6
  85.9 0.9 copy-start.8
  86.8 0.9 copy-start.10
  87.8 0.9 copy-start.12
  (4 other events, 2.6 us)

commit v2 on v1

--- a/solution.py
+++ b/solution.py
@@ -11,30 +11,37 @@
 CAP = 2
 EPSILON = 1e-05
 DOC_ROWS = 16
-VMEM_LIMIT = 40 * 1024 * 1024
-
-
-def attention_kernel(ratio, pair, core_ref, query_ref, doc_ref, *refs):
-    pack_refs, out_refs = refs[:-pair], refs[-pair:]
+VMEM_LIMIT = 16 * 1024 * 1024
+
+
+def attention_kernel(ratio, groups, pair, packs, place_ref, query_ref, *refs):
+    pack_refs, out_refs = refs[:packs], refs[-pair:]
     heads, tokens, head_size = query_ref.shape
-    groups = heads // ratio
     scale = 1.0 / math.sqrt(head_size)
-    own_doc = doc_ref[...]
+    ctx_index, core = place_ref[0], place_ref[1]
     rows = lax.broadcasted_iota(jnp.int32, (tokens, tokens), 0)
     columns = lax.broadcasted_iota(jnp.int32, (tokens, tokens), 1)
-    allowed = []
-    for place, ref in enumerate(pack_refs):
-        docs = ref[2 * groups * tokens : 2 * groups * tokens + 1, :].astype(jnp.float32)
-        same = own_doc == docs
-        allowed.append(same & (columns <= rows) if place == 0 else same)
+    held_rows = groups * tokens
+    docs = [ref[2 * held_rows : 2 * held_rows + 1, :].astype(jnp.float32) for ref in pack_refs]
+    own_doc = jnp.sum(jnp.where(rows == columns, docs[0], 0.0), axis=1, keepdims=True)
+    allowed = [(own_doc == docs[0]) & (columns <= rows)]
+    for step in range(1, len(pack_refs)):
+        allowed.append((own_doc == docs[step]) & (ctx_index >= step))
     allowed = jnp.concatenate(allowed, axis=1)
-    core = core_ref[0]
     part_rows = tokens // pair
+    token = lax.broadcasted_iota(jnp.int32, (tokens, held_rows), 0)
+    row = lax.broadcasted_iota(jnp.int32, (tokens, held_rows), 1)
+
+    def of_group(group, first):
+        pick = (row == token * groups + group).astype(jnp.bfloat16)
+        parts = [
+            jnp.dot(pick, ref[first : first + held_rows, :], preferred_element_type=jnp.float32)
+            for ref in pack_refs
+        ]
+        return jnp.concatenate(parts, axis=0).astype(jnp.bfloat16)
+
     for group in range(groups):
-        first = group * tokens
-        keys = jnp.concatenate([ref[first : first + tokens, :] for ref in pack_refs], axis=0)
-        first = (groups + group) * tokens
-        held = jnp.concatenate([ref[first : first + tokens, :] for ref in pack_refs], axis=0)
+        keys, held = of_group(group, 0), of_group(group, held_rows)
         for head in range(group * ratio, (group + 1) * ratio):
             scores = lax.dot_general(
                 query_ref[head], keys, (((1,), (1,)), ((), ())), preferred_element_type=jnp.float32
@@ -52,6 +59,19 @@
                 for own in range(1, pair):
                     piece = jnp.where(core == own, parts[(own + turn) % pair], piece)
                 out_refs[turn][:, head * head_size : (head + 1) * head_size] = piece
+
+
+def project_kernel(pair, block_ref, *refs):
+    weight_refs, out_ref = refs[:pair], refs[pair]
+    depth = weight_refs[0].shape[0]
+    total = jnp.zeros(out_ref.shape, jnp.float32)
+    for turn in range(pair):
+        total = total + jnp.dot(
+            block_ref[:, turn * depth : (turn + 1) * depth],
+            weight_refs[turn][...],
+            preferred_element_type=jnp.float32,
+        )
+    out_ref[...] = total.astype(out_ref.dtype)
 
 
 def finish_kernel(steps, exp_count, place_ref, *refs):
@@ -140,82 +160,76 @@
     exp_index = lax.axis_index("exp")
     reach = -(-(ctx_count * tokens // 2 - 1) // tokens)
 
-    docs = (doc_ids + 1).astype(jnp.bfloat16)
+    def over(array, axis, step):
+        count = lax.axis_size(axis)
+        if step % count == 0:
+            return array
+        return lax.ppermute(array, axis, [(i, (i + step) % count) for i in range(count)])
+
     pack = jnp.concatenate(
         [
-            key_states[0].transpose(1, 0, 2).reshape(groups * tokens, head_size),
-            values[0].transpose(1, 0, 2).reshape(groups * tokens, head_size),
-            jnp.broadcast_to(docs, (DOC_ROWS, tokens)),
+            key_states.reshape(groups * tokens, head_size),
+            values.reshape(groups * tokens, head_size),
+            jnp.broadcast_to(doc_ids.astype(jnp.bfloat16), (DOC_ROWS, tokens)),
         ],
         axis=0,
     )
-    packs = [pack] + [
-        lax.ppermute(pack, "ctx", [(i, i + step) for i in range(ctx_count - step)])
-        for step in range(1, reach + 1)
-    ]
-    weights = [out_proj] + [
-        lax.ppermute(out_proj, "tp", [(i, (i + turn) % pair) for i in range(pair)])
-        for turn in range(1, pair)
-    ]
-
-    def over_exp(array, back):
-        if back == 0:
-            return array
-        return lax.ppermute(
-            array, "exp", [(i, (i + back) % exp_count) for i in range(exp_count)]
-        )
-
+    packs = [over(pack, "ctx", step) for step in range(reach + 1)]
+    weights = [over(out_proj, "tp", turn) for turn in range(pair)]
     ids = expert_ids[:, :, 0]
-    all_ids = [over_exp(ids, back) for back in range(exp_count)]
-    all_residual = [over_exp(residual[0], back) for back in range(exp_count)]
+    all_ids = [over(ids, "exp", back) for back in range(exp_count)]
+    all_residual = [over(residual[0], "exp", back) for back in range(exp_count)]
 
     vmem = pl.BlockSpec(memory_space=pltpu.VMEM)
     smem = pl.BlockSpec(memory_space=pltpu.SMEM)
+    anywhere = pl.BlockSpec(memory_space=pl.ANY)
+    early = weights[1:] + all_ids[1:] + all_residual[1:]
     pieces = pl.pallas_call(
-        functools.partial(attention_kernel, heads // groups, pair),
+        functools.partial(attention_kernel, heads // groups, groups, pair, len(packs)),
         out_shape=[jax.ShapeDtypeStruct((part_rows, heads * head_size), jnp.bfloat16)] * pair,
-        in_specs=[smem] + [vmem] * (2 + len(packs)),
+        in_specs=[smem] + [vmem] * (1 + len(packs)) + [anywhere] * len(early),
         out_specs=[vmem] * pair,
         compiler_params=pltpu.CompilerParams(vmem_limit_bytes=VMEM_LIMIT),
     )(
-        core.reshape(1),
+        jnp.stack([ctx_index, core]),
         queries[0].transpose(1, 0, 2),
-        (doc_ids + 1).astype(jnp.float32).reshape(tokens, 1),
         *packs,
-    )
-
-    arrived = {}
+        *early,
+    )
+
+    project = pl.pallas_call(
+        functools.partial(project_kernel, pair),
+        out_shape=jax.ShapeDtypeStruct((part_rows, columns), jnp.bfloat16),
+        in_specs=[vmem] * (1 + pair),
+        out_specs=vmem,
+        cost_estimate=pl.CostEstimate(
+            flops=2 * pair * part_rows * out_proj.size,
+            bytes_accessed=2 * pair * out_proj.size,
+            transcendentals=0,
+        ),
+        compiler_params=pltpu.CompilerParams(vmem_limit_bytes=VMEM_LIMIT),
+    )
+    block = jnp.concatenate([over(pieces[turn], "tp", turn) for turn in range(pair)], axis=1)
+    aligned = columns % 128 == 0
+    flat, chunks = [], []
     for step in range(ctx_count):
-        for turn in range(pair):
-            moves = [
-                (z * pair + c, (z + step) % ctx_count * pair + (c + turn) % pair)
-                for z in range(ctx_count)
-                for c in range(pair)
-            ]
-            arrived[step, turn] = (
-                pieces[0]
-                if step == 0 and turn == 0
-                else lax.ppermute(pieces[turn], ("ctx", "tp"), moves)
-            )
-    order = sorted(range(ctx_count), key=lambda step: min(step, ctx_count - step))
-    chunks = {}
-    for step in order:
-        total = sum(
-            jnp.dot(arrived[step, turn], weights[turn], preferred_element_type=jnp.float32)
-            for turn in range(pair)
-        ).astype(jnp.bfloat16)
-        away = (ctx_count - step) % ctx_count
-        if away:
-            total = lax.ppermute(
-                total, "ctx", [(z, (z + away) % ctx_count) for z in range(ctx_count)]
-            )
-        chunks[step] = total
-    steps = ctx_count
-    if columns % 128:
-        steps = 1
-        whole = jnp.roll(jnp.stack([chunks[step] for step in range(ctx_count)]), ctx_index, axis=0)
-        chunks = {0: whole.transpose(1, 0, 2).reshape(part_rows, width)}
-    flat = [over_exp(chunks[step], back) for step in range(steps) for back in range(exp_count)]
+        following = over(block, "ctx", 1) if step < ctx_count - 1 else None
+        if step >= 2 and aligned:
+            block, flat[step - 2] = lax.optimization_barrier((block, flat[step - 2]))
+        total = project(block, *weights)
+        if following is not None:
+            following, total = lax.optimization_barrier((following, total))
+        chunk = over(total, "ctx", ctx_count - step)
+        chunks.append(chunk)
+        if aligned:
+            flat.append([over(chunk, "exp", back) for back in range(exp_count)])
+        block = following
+    if not aligned:
+        whole = jnp.roll(jnp.stack(chunks), ctx_index, axis=0)
+        whole = whole.transpose(1, 0, 2).reshape(part_rows, width)
+        flat = [[over(whole, "exp", back) for back in range(exp_count)]]
+    steps = len(flat)
+    flat = [array for arrays in flat for array in arrays]
     out = pl.pallas_call(
         functools.partial(finish_kernel, steps, exp_count),
         out_shape=jax.ShapeDtypeStruct(

time: 92.6 us -> 91.6 us (0.989)
  waiting for transfers between devices: 11.7 us -> 50.7 us
  starting transfers between devices: 49.3 us -> 19.8 us
  matrix products: 13.2 us -> 0 us
  Pallas kernels: 4.78 us -> 11.6 us
  local copies, waits for them, and re-layouts: 12.1 us -> 7.21 us
  other arithmetic: 0.75 us -> 1.69 us
    ppermute x19 -> x16, waiting for transfers between devices: 11.7 us -> 50.7 us  [over(): lax.ppermute(array, axis, [(i, (i + step) % count) for i in range(count)])]
    ppermute x19 -> x16, starting transfers between devices: 49.3 us -> 19.8 us  [over(): lax.ppermute(array, axis, [(i, (i + step) % count) for i in range(count)])]
    dot_general x8 -> x0, matrix products: 13.2 us -> none  [on_device(): jnp.dot(arrived[step, turn], weights[turn], preferred_element_type=jnp.fl...]
    pallas_call x1 -> x5, Pallas kernels: 2.73 us -> 8.95 us  [the longest x4 4.95 us: on_device(): total = project(block, *weights)]
    unnamed x34 -> x27, local copies, waits for them, and re-layouts: 8.89 us -> 5.82 us
    transpose x2 -> x0, local copies, waits for them, and re-layouts: 1.7 us -> none  [the longest x1 0.85 us: on_device(): key_states[0].transpose(1, 0, 2).reshape(groups * tokens, head_size)]
  transfers between devices with their start and end apart: 19 -> 16, of which waited for: 6 -> 10; matrix products, arithmetic and copies ran while one was open for 17% -> 2% of each run, Pallas kernels for 3% -> 4%
where the time goes in v2:
time: 91.6 us; the launch traced here: 91.1 us
  waiting for transfers between devices  50.7 us (55%)
  starting transfers between devices  19.8 us (22%)
  Pallas kernels  11.6 us (13%)
  local copies, waits for them, and re-layouts  7.21 us (8%)
  other arithmetic  1.69 us (2%)
    ppermute x16, waiting for transfers between devices, over(): lax.ppermute(array, axis, [(i, (i + step) % count) for i in range(count)])  50.7 us
    ppermute x16, starting transfers between devices, over(): lax.ppermute(array, axis, [(i, (i + step) % count) for i in range(count)])  19.8 us
    unnamed x27, local copies, waits for them, and re-layouts  5.82 us
    pallas_call x4, Pallas kernels, on_device(): total = project(block, *weights)  4.95 us
    pallas_call x1, Pallas kernels, on_device(): pl.pallas_call(functools.partial(attention_kernel, heads // groups, group...  4 us
    pallas_call x1, Pallas kernels, on_device(): pl.pallas_call(functools.partial(finish_kernel, steps, exp_count), out_sh...  2.61 us
  transfers between devices with their start and end apart: 16, of which 10 were waited for; matrix products, arithmetic and copies ran while one was open for 2% of the time, Pallas kernels for 4%

profile of v2, /device:TPU:0, one launch (start us, length us, event | category | flops | bytes accessed | tf_op | source)
XLA Modules:
  0.0 91.1 jit_solution(10509355228041209615)
XLA Ops:
  0.5 2.5 %collective-permute-start.4 = (bf16[64,5120]{1,0:T(8,128)(2,1)}, bf16[64,5120]{1,0:T(8,128)(2,1)}, u32[]{:S(2)}, u32[]{:S(2)}) collective-permute-start(bf16[64,5120]{1,0:T(8,128)(2,1)} %bitcast.14), channel_id=1, source_target_pairs={{0,2},{2,0},{1,3},{3,1},{4,6},{6,4},{5,7},{7,5},{8,10},{10,8},{9,1... | collective-permute-start | bytes 1966088 | tf_op jit(solution)/shard_map/ppermute | solution.py:167
  3.6 0.9 pad_maximum_fusion.refs_0_
  4.5 1.6 %collective-permute-start = (bf16[528,128]{1,0:T(8,128)(2,1)S(1)}, bf16[528,128]{1,0:T(8,128)(2,1)S(1)}, u32[]{:S(2)}, u32[]{:S(2)}) collective-permute-start(bf16[528,128]{1,0:T(8,128)(2,1)S(1)} %pad_maximum_fusion.refs_0_), channel_id=1, source_target_pairs={{0,4},{4,8},{8,12},{12,0},{1,5},{5,9},{9,13},{13,1},{2,6},{6,10},{... | collective-permute-start | bytes 405512 | tf_op jit(solution)/shard_map/ppermute | solution.py:167
  6.1 2.6 %collective-permute-start.1 = (bf16[528,128]{1,0:T(8,128)(2,1)S(1)}, bf16[528,128]{1,0:T(8,128)(2,1)}, u32[]{:S(2)}, u32[]{:S(2)}) collective-permute-start(bf16[528,128]{1,0:T(8,128)(2,1)S(1)} %pad_maximum_fusion.refs_0_), channel_id=1, source_target_pairs={{0,8},{4,12},{8,0},{12,4},{1,9},{5,13},{9,1},{13,5},{2,10},{6,14},... | collective-permute-start | bytes 405512 | tf_op jit(solution)/shard_map/ppermute | solution.py:167
  9.3 9.3 %collective-permute-done.3.refs_4_.refs_11_ = s32[1,64]{1,0:T(1,128)S(1)} collective-permute-done((s32[1,64]{1,0:T(1,128)}, s32[1,64]{1,0:T(1,128)S(1)}, u32[]{:S(2)}, u32[]{:S(2)}) %collective-permute-start.3) | collective-permute-done | bytes 288 | tf_op jit(solution)/shard_map/ppermute | solution.py:167
  18.7 1.0 %copy-done.2 = bf16[1,128,10,128]{3,1,2,0:T(8,128)(2,1)S(1)} copy-done((bf16[1,128,10,128]{3,1,2,0:T(8,128)(2,1)S(1)}, bf16[1,128,10,128]{3,1,2,0:T(8,128)(2,1)}, u32[]{:S(2)}) %copy-start.2) | copy-done | bytes 327704
  19.7 4.0 %shard_map.100 = (bf16[64,1280]{1,0:T(8,128)(2,1)S(1)}, bf16[64,1280]{1,0:T(8,128)(2,1)S(1)}) custom-call(s32[2]{0:T(128)S(1)} %pad_add_fusion.1.place_ref, bf16[10,128,128]{2,1,0:T(8,128)(2,1)S(1)} %bitcast.16, bf16[528,128]{1,0:T(8,128)(2,1)S(1)} %pad_maximum_fusion.refs_0_, bf16[528,128]{1,0:T(8,128)(2,1)S(1)} %collective-permute-done.refs_1_, ...), custom_call_target="tpu_custom_call" | custom-call | tf_op jit(solution)/shard_map/pallas_call | solution.py:187
  23.8 1.4 %collective-permute-done.5 = bf16[64,1280]{1,0:T(8,128)(2,1)S(1)} collective-permute-done((bf16[64,1280]{1,0:T(8,128)(2,1)S(1)}, bf16[64,1280]{1,0:T(8,128)(2,1)S(1)}, u32[]{:S(2)}, u32[]{:S(2)}) %collective-permute-start.5) | collective-permute-done | bytes 163872 | tf_op jit(solution)/shard_map/ppermute | solution.py:167
  25.1 1.9 %collective-permute-start.6 = (bf16[64,2560]{1,0:T(8,128)(2,1)S(1)}, bf16[64,2560]{1,0:T(8,128)(2,1)S(1)}, u32[]{:S(2)}, u32[]{:S(2)}) collective-permute-start(bf16[64,2560]{1,0:T(8,128)(2,1)S(1)} %constant_dynamic-update-slice_fusion.block_ref), channel_id=1, source_target_pairs={{0,4},{4,8},{8,12},{12,0},{1,5},{5,9},{9,13},{13,1},{2,6},{6,10},{... | collective-permute-start | bytes 983048 | tf_op jit(solution)/shard_map/ppermute | solution.py:167
  27.0 1.2 %shard_map.101.refs_0_ = bf16[64,1280]{1,0:T(8,128)(2,1)S(1)} custom-call(bf16[64,2560]{1,0:T(8,128)(2,1)S(1)} %constant_dynamic-update-slice_fusion.block_ref, bf16[1280,1280]{1,0:T(8,128)(2,1)S(1)} %copy-done, bf16[1280,1280]{1,0:T(8,128)(2,1)S(1)} %collective-permute-done.2.refs_3_.refs_1_), custom_call_target="tpu_custom_call" | custom-call | flops 419430400 | bytes 6553600 | tf_op jit(solution)/shard_map/pallas_call | solution.py:219
  28.3 8.8 %collective-permute-done.6.block_ref = bf16[64,2560]{1,0:T(8,128)(2,1)S(1)} collective-permute-done((bf16[64,2560]{1,0:T(8,128)(2,1)S(1)}, bf16[64,2560]{1,0:T(8,128)(2,1)S(1)}, u32[]{:S(2)}, u32[]{:S(2)}) %collective-permute-start.6) | collective-permute-done | bytes 327712 | tf_op jit(solution)/shard_map/ppermute | solution.py:167
  37.1 1.2 %shard_map.102 = bf16[64,1280]{1,0:T(8,128)(2,1)S(1)} custom-call(bf16[64,2560]{1,0:T(8,128)(2,1)S(1)} %collective-permute-done.6.block_ref, bf16[1280,1280]{1,0:T(8,128)(2,1)S(1)} %copy-done, bf16[1280,1280]{1,0:T(8,128)(2,1)S(1)} %collective-permute-done.2.refs_3_.refs_1_), custom_call_target="tpu_custom_call" | custom-call | flops 419430400 | bytes 6553600 | tf_op jit(solution)/shard_map/pallas_call | solution.py:219
  38.3 9.8 %collective-permute-done.7.block_ref = bf16[64,2560]{1,0:T(8,128)(2,1)S(1)} collective-permute-done((bf16[64,2560]{1,0:T(8,128)(2,1)S(1)}, bf16[64,2560]{1,0:T(8,128)(2,1)S(1)}, u32[]{:S(2)}, u32[]{:S(2)}) %collective-permute-start.7) | collective-permute-done | bytes 327712 | tf_op jit(solution)/shard_map/ppermute | solution.py:167
  48.2 3.8 %collective-permute-start.10 = (bf16[64,1280]{1,0:T(8,128)(2,1)S(1)}, bf16[64,1280]{1,0:T(8,128)(2,1)S(1)}, u32[]{:S(2)}, u32[]{:S(2)}) collective-permute-start(bf16[64,1280]{1,0:T(8,128)(2,1)S(1)} %shard_map.102), channel_id=1, source_target_pairs={{0,12},{4,0},{8,4},{12,8},{1,13},{5,1},{9,5},{13,9},{2,14},{6,2},{... | collective-permute-start | bytes 491528 | tf_op jit(solution)/shard_map/ppermute | solution.py:167
  52.0 1.2 %collective-permute-start.8 = (bf16[64,1280]{1,0:T(8,128)(2,1)S(1)}, bf16[64,1280]{1,0:T(8,128)(2,1)S(1)}, u32[]{:S(2)}, u32[]{:S(2)}) collective-permute-start(bf16[64,1280]{1,0:T(8,128)(2,1)S(1)} %shard_map.101.refs_0_), channel_id=1, source_target_pairs={{0,2},{2,0},{1,3},{3,1},{4,6},{6,4},{5,7},{7,5},{8,10},{10,8},{9,1... | collective-permute-start | bytes 491528 | tf_op jit(solution)/shard_map/ppermute | solution.py:167
  53.2 6.4 %collective-permute-done.10.refs_2_ = bf16[64,1280]{1,0:T(8,128)(2,1)S(1)} collective-permute-done((bf16[64,1280]{1,0:T(8,128)(2,1)S(1)}, bf16[64,1280]{1,0:T(8,128)(2,1)S(1)}, u32[]{:S(2)}, u32[]{:S(2)}) %collective-permute-start.10) | collective-permute-done | bytes 163872 | tf_op jit(solution)/shard_map/ppermute | solution.py:167
  60.4 1.2 %shard_map.103 = bf16[64,1280]{1,0:T(8,128)(2,1)S(1)} custom-call(bf16[64,2560]{1,0:T(8,128)(2,1)S(1)} %collective-permute-done.7.block_ref, bf16[1280,1280]{1,0:T(8,128)(2,1)S(1)} %copy-done, bf16[1280,1280]{1,0:T(8,128)(2,1)S(1)} %collective-permute-done.2.refs_3_.refs_1_), custom_call_target="tpu_custom_call" | custom-call | flops 419430400 | bytes 6553600 | tf_op jit(solution)/shard_map/pallas_call | solution.py:219
  61.7 3.3 %collective-permute-done.11.refs_3_ = bf16[64,1280]{1,0:T(8,128)(2,1)S(1)} collective-permute-done((bf16[64,1280]{1,0:T(8,128)(2,1)S(1)}, bf16[64,1280]{1,0:T(8,128)(2,1)S(1)}, u32[]{:S(2)}, u32[]{:S(2)}) %collective-permute-start.11) | collective-permute-done | bytes 163872 | tf_op jit(solution)/shard_map/ppermute | solution.py:167
  65.0 1.2 %shard_map.104 = bf16[64,1280]{1,0:T(8,128)(2,1)S(1)} custom-call(bf16[64,2560]{1,0:T(8,128)(2,1)S(1)} %collective-permute-done.9.block_ref, bf16[1280,1280]{1,0:T(8,128)(2,1)S(1)} %copy-done, bf16[1280,1280]{1,0:T(8,128)(2,1)S(1)} %collective-permute-done.2.refs_3_.refs_1_), custom_call_target="tpu_custom_call" | custom-call | flops 419430400 | bytes 6553600 | tf_op jit(solution)/shard_map/pallas_call | solution.py:219
  66.3 2.9 %collective-permute-start.12 = (bf16[64,1280]{1,0:T(8,128)(2,1)S(1)}, bf16[64,1280]{1,0:T(8,128)(2,1)S(1)}, u32[]{:S(2)}, u32[]{:S(2)}) collective-permute-start(bf16[64,1280]{1,0:T(8,128)(2,1)S(1)} %shard_map.103), channel_id=1, source_target_pairs={{0,8},{4,12},{8,0},{12,4},{1,9},{5,13},{9,1},{13,5},{2,10},{6,14},... | collective-permute-start | bytes 491528 | tf_op jit(solution)/shard_map/ppermute | solution.py:167
  69.2 4.3 %collective-permute-done.14.refs_6_ = bf16[64,1280]{1,0:T(8,128)(2,1)S(1)} collective-permute-done((bf16[64,1280]{1,0:T(8,128)(2,1)S(1)}, bf16[64,1280]{1,0:T(8,128)(2,1)S(1)}, u32[]{:S(2)}, u32[]{:S(2)}) %collective-permute-start.14) | collective-permute-done | bytes 163872 | tf_op jit(solution)/shard_map/ppermute | solution.py:167
  73.5 0.7 collective-permute-start.15
  74.2 2.5 %collective-permute-done.12.refs_4_ = bf16[64,1280]{1,0:T(8,128)(2,1)S(1)} collective-permute-done((bf16[64,1280]{1,0:T(8,128)(2,1)S(1)}, bf16[64,1280]{1,0:T(8,128)(2,1)S(1)}, u32[]{:S(2)}, u32[]{:S(2)}) %collective-permute-start.12) | collective-permute-done | bytes 163872 | tf_op jit(solution)/shard_map/ppermute | solution.py:167
  77.5 2.1 %collective-permute-done.15.refs_7_ = bf16[64,1280]{1,0:T(8,128)(2,1)S(1)} collective-permute-done((bf16[64,1280]{1,0:T(8,128)(2,1)S(1)}, bf16[64,1280]{1,0:T(8,128)(2,1)S(1)}, u32[]{:S(2)}, u32[]{:S(2)}) %collective-permute-start.15) | collective-permute-done | bytes 163872 | tf_op jit(solution)/shard_map/ppermute | solution.py:167
  79.5 2.8 %collective-permute-done.13.refs_5_ = bf16[64,1280]{1,0:T(8,128)(2,1)S(1)} collective-permute-done((bf16[64,1280]{1,0:T(8,128)(2,1)S(1)}, bf16[64,1280]{1,0:T(8,128)(2,1)S(1)}, u32[]{:S(2)}, u32[]{:S(2)}) %collective-permute-start.13) | collective-permute-done | bytes 163872 | tf_op jit(solution)/shard_map/ppermute | solution.py:167
  82.4 1.1 %copy-done.1 = bf16[1,64,5120]{2,1,0:T(8,128)(2,1)S(1)} copy-done((bf16[1,64,5120]{2,1,0:T(8,128)(2,1)S(1)}, bf16[1,64,5120]{2,1,0:T(8,128)(2,1)}, u32[]{:S(2)}) %copy-start.1) | copy-done | bytes 655384
  83.4 1.0 %copy-done.3 = bf16[5120,32]{0,1:T(8,128)(2,1)S(1)} copy-done((bf16[5120,32]{0,1:T(8,128)(2,1)S(1)}, bf16[5120,32]{0,1:T(8,128)(2,1)}, u32[]{:S(2)}) %copy-start.3) | copy-done | bytes 327704
  84.4 0.9 %copy-done.5 = bf16[64,1280]{1,0:T(8,128)(2,1)S(1)} copy-done((bf16[64,1280]{1,0:T(8,128)(2,1)S(1)}, bf16[64,1280]{1,0:T(8,128)(2,1)}, u32[]{:S(2)}) %copy-start.5) | copy-done | bytes 163864
  85.3 0.9 %copy-done.7 = bf16[64,1280]{1,0:T(8,128)(2,1)S(1)} copy-done((bf16[64,1280]{1,0:T(8,128)(2,1)S(1)}, bf16[64,1280]{1,0:T(8,128)(2,1)}, u32[]{:S(2)}) %copy-start.7) | copy-done | bytes 163864
  86.3 0.9 %copy-done.9 = bf16[64,1280]{1,0:T(8,128)(2,1)S(1)} copy-done((bf16[64,1280]{1,0:T(8,128)(2,1)S(1)}, bf16[64,1280]{1,0:T(8,128)(2,1)}, u32[]{:S(2)}) %copy-start.9) | copy-done | bytes 163864
  87.2 2.6 %shard_map.105 = bf16[2,64,5120]{2,1,0:T(8,128)(2,1)S(1)} custom-call(s32[2]{0:T(128)S(1)} %pad_add_fusion.place_ref, bf16[64,1280]{1,0:T(8,128)(2,1)S(1)} %shard_map.101.refs_0_, bf16[64,1280]{1,0:T(8,128)(2,1)S(1)} %copy-done.7, bf16[64,1280]{1,0:T(8,128)(2,1)S(1)} %copy-done.5, bf16[64,1280]{1,0:T(8,128)(2,1)S(1)} %copy-done.9, ...), custom_call_target="tpu_custom_call" | custom-call | tf_op jit(solution)/shard_map/pallas_call | solution.py:233
  89.8 1.4 %reshape.19 = bf16[2,32,2,5120]{3,2,1,0:T(2,128)(2,1)} reshape(bf16[2,64,5120]{2,1,0:T(8,128)(2,1)S(1)} %shard_map.105) | data formatting | bytes 2621440 | tf_op jit(solution)/shard_map/reshape | solution.py:254
  (41 shorter events, 3.4 us)
Async XLA Ops:
  0.0 18.7 %collective-permute-start.2 = (bf16[1280,1280]{1,0:T(8,128)(2,1)}, bf16[1280,1280]{1,0:T(8,128)(2,1)S(1)}, u32[]{:S(2)}, u32[]{:S(2)}) collective-permute-start(bf16[1280,1280]{1,0:T(8,128)(2,1)} %refs_0_.7), channel_id=1, source_target_pairs={{0,1},{1,0},{2,3},{3,2},{4,5},{5,4},{6,7},{7,6},{8,9},{9,8},{10,11... | collective-permute-start | bytes 9830408 | tf_op jit(solution)/shard_map/ppermute | solution.py:167
  0.5 18.2 %collective-permute-start.4 = (bf16[64,5120]{1,0:T(8,128)(2,1)}, bf16[64,5120]{1,0:T(8,128)(2,1)}, u32[]{:S(2)}, u32[]{:S(2)}) collective-permute-start(bf16[64,5120]{1,0:T(8,128)(2,1)} %bitcast.14), channel_id=1, source_target_pairs={{0,2},{2,0},{1,3},{3,1},{4,6},{6,4},{5,7},{7,5},{8,10},{10,8},{9,1... | collective-permute-start | bytes 1966088 | tf_op jit(solution)/shard_map/ppermute | solution.py:167
  4.5 14.2 %collective-permute-start = (bf16[528,128]{1,0:T(8,128)(2,1)S(1)}, bf16[528,128]{1,0:T(8,128)(2,1)S(1)}, u32[]{:S(2)}, u32[]{:S(2)}) collective-permute-start(bf16[528,128]{1,0:T(8,128)(2,1)S(1)} %pad_maximum_fusion.refs_0_), channel_id=1, source_target_pairs={{0,4},{4,8},{8,12},{12,0},{1,5},{5,9},{9,13},{13,1},{2,6},{6,10},{... | collective-permute-start | bytes 405512 | tf_op jit(solution)/shard_map/ppermute | solution.py:167
  6.1 12.6 %collective-permute-start.1 = (bf16[528,128]{1,0:T(8,128)(2,1)S(1)}, bf16[528,128]{1,0:T(8,128)(2,1)}, u32[]{:S(2)}, u32[]{:S(2)}) collective-permute-start(bf16[528,128]{1,0:T(8,128)(2,1)S(1)} %pad_maximum_fusion.refs_0_), channel_id=1, source_target_pairs={{0,8},{4,12},{8,0},{12,4},{1,9},{5,13},{9,1},{13,5},{2,10},{6,14},... | collective-permute-start | bytes 405512 | tf_op jit(solution)/shard_map/ppermute | solution.py:167
  8.7 10.0 %collective-permute-start.3 = (s32[1,64]{1,0:T(1,128)}, s32[1,64]{1,0:T(1,128)S(1)}, u32[]{:S(2)}, u32[]{:S(2)}) collective-permute-start(s32[1,64]{1,0:T(1,128)} %bitcast.18), channel_id=1, source_target_pairs={{0,2},{2,0},{1,3},{3,1},{4,6},{6,4},{5,7},{7,5},{8,10},{10,8},{9,1... | collective-permute-start | bytes 776 | tf_op jit(solution)/shard_map/ppermute | solution.py:167
  9.2 17.8 %copy-start = (bf16[1280,1280]{1,0:T(8,128)(2,1)S(1)}, bf16[1280,1280]{1,0:T(8,128)(2,1)}, u32[]{:S(2)}) copy-start(bf16[1280,1280]{1,0:T(8,128)(2,1)} %refs_0_.7) | copy-start | bytes 9830404
  18.7 1.0 %copy-start.2 = (bf16[1,128,10,128]{3,1,2,0:T(8,128)(2,1)S(1)}, bf16[1,128,10,128]{3,1,2,0:T(8,128)(2,1)}, u32[]{:S(2)}) copy-start(bf16[1,128,10,128]{3,1,2,0:T(8,128)(2,1)} %param.10) | copy-start | bytes 983044
  23.7 1.5 %collective-permute-start.5 = (bf16[64,1280]{1,0:T(8,128)(2,1)S(1)}, bf16[64,1280]{1,0:T(8,128)(2,1)S(1)}, u32[]{:S(2)}, u32[]{:S(2)}) collective-permute-start(bf16[64,1280]{1,0:T(8,128)(2,1)S(1)} %get-tuple-element.20), channel_id=1, source_target_pairs={{0,1},{1,0},{2,3},{3,2},{4,5},{5,4},{6,7},{7,6},{8,9},{9,8},{10,11... | collective-permute-start | bytes 491528 | tf_op jit(solution)/shard_map/ppermute | solution.py:167
  25.1 11.9 %collective-permute-start.6 = (bf16[64,2560]{1,0:T(8,128)(2,1)S(1)}, bf16[64,2560]{1,0:T(8,128)(2,1)S(1)}, u32[]{:S(2)}, u32[]{:S(2)}) collective-permute-start(bf16[64,2560]{1,0:T(8,128)(2,1)S(1)} %constant_dynamic-update-slice_fusion.block_ref), channel_id=1, source_target_pairs={{0,4},{4,8},{8,12},{12,0},{1,5},{5,9},{9,13},{13,1},{2,6},{6,10},{... | collective-permute-start | bytes 983048 | tf_op jit(solution)/shard_map/ppermute | solution.py:167
  37.1 11.1 %collective-permute-start.7 = (bf16[64,2560]{1,0:T(8,128)(2,1)S(1)}, bf16[64,2560]{1,0:T(8,128)(2,1)S(1)}, u32[]{:S(2)}, u32[]{:S(2)}) collective-permute-start(bf16[64,2560]{1,0:T(8,128)(2,1)S(1)} %collective-permute-done.6.block_ref), channel_id=1, source_target_pairs={{0,4},{4,8},{8,12},{12,0},{1,5},{5,9},{9,13},{13,1},{2,6},{6,10},{... | collective-permute-start | bytes 983048 | tf_op jit(solution)/shard_map/ppermute | solution.py:167
  48.2 13.5 %collective-permute-start.9 = (bf16[64,2560]{1,0:T(8,128)(2,1)S(1)}, bf16[64,2560]{1,0:T(8,128)(2,1)S(1)}, u32[]{:S(2)}, u32[]{:S(2)}) collective-permute-start(bf16[64,2560]{1,0:T(8,128)(2,1)S(1)} %collective-permute-done.7.block_ref), channel_id=1, source_target_pairs={{0,4},{4,8},{8,12},{12,0},{1,5},{5,9},{9,13},{13,1},{2,6},{6,10},{... | collective-permute-start | bytes 983048 | tf_op jit(solution)/shard_map/ppermute | solution.py:167
  48.2 11.5 %collective-permute-start.10 = (bf16[64,1280]{1,0:T(8,128)(2,1)S(1)}, bf16[64,1280]{1,0:T(8,128)(2,1)S(1)}, u32[]{:S(2)}, u32[]{:S(2)}) collective-permute-start(bf16[64,1280]{1,0:T(8,128)(2,1)S(1)} %shard_map.102), channel_id=1, source_target_pairs={{0,12},{4,0},{8,4},{12,8},{1,13},{5,1},{9,5},{13,9},{2,14},{6,2},{... | collective-permute-start | bytes 491528 | tf_op jit(solution)/shard_map/ppermute | solution.py:167
  52.0 8.4 %collective-permute-start.8 = (bf16[64,1280]{1,0:T(8,128)(2,1)S(1)}, bf16[64,1280]{1,0:T(8,128)(2,1)S(1)}, u32[]{:S(2)}, u32[]{:S(2)}) collective-permute-start(bf16[64,1280]{1,0:T(8,128)(2,1)S(1)} %shard_map.101.refs_0_), channel_id=1, source_target_pairs={{0,2},{2,0},{1,3},{3,1},{4,6},{6,4},{5,7},{7,5},{8,10},{10,8},{9,1... | collective-permute-start | bytes 491528 | tf_op jit(solution)/shard_map/ppermute | solution.py:167
  59.7 1.9 %copy-start.4 = (bf16[64,1280]{1,0:T(8,128)(2,1)}, bf16[64,1280]{1,0:T(8,128)(2,1)S(1)}, u32[]{:S(2)}) copy-start(bf16[64,1280]{1,0:T(8,128)(2,1)S(1)} %collective-permute-done.10.refs_2_) | copy-start | bytes 491524
  59.7 5.3 %collective-permute-start.11 = (bf16[64,1280]{1,0:T(8,128)(2,1)S(1)}, bf16[64,1280]{1,0:T(8,128)(2,1)S(1)}, u32[]{:S(2)}, u32[]{:S(2)}) collective-permute-start(bf16[64,1280]{1,0:T(8,128)(2,1)S(1)} %collective-permute-done.10.refs_2_), channel_id=1, source_target_pairs={{0,2},{2,0},{1,3},{3,1},{4,6},{6,4},{5,7},{7,5},{8,10},{10,8},{9,1... | collective-permute-start | bytes 491528 | tf_op jit(solution)/shard_map/ppermute | solution.py:167
  60.4 1.3 %copy-start.6 = (bf16[64,1280]{1,0:T(8,128)(2,1)}, bf16[64,1280]{1,0:T(8,128)(2,1)S(1)}, u32[]{:S(2)}) copy-start(bf16[64,1280]{1,0:T(8,128)(2,1)S(1)} %collective-permute-done.8.refs_1_) | copy-start | bytes 491524
  61.6 15.7 %copy-start.12 = (bf16[5120]{0:T(1024)(128)(2,1)S(1)}, bf16[5120]{0:T(1024)(128)(2,1)}, u32[]{:S(2)}) copy-start(bf16[5120]{0:T(1024)(128)(2,1)} %param.16) | copy-start | bytes 30724
  61.6 20.7 %copy-start.10 = (s32[1,64,1]{1,2,0:T(1,128)S(1)}, s32[1,64,1]{1,2,0:T(1,128)}, u32[]{:S(2)}) copy-start(s32[1,64,1]{1,2,0:T(1,128)} %param.18) | copy-start | bytes 772
  61.7 20.7 %copy-start.11 = (s32[64]{0:T(128)S(1)}, s32[64]{0:T(128)}, u32[]{:S(2)}) copy-start(s32[64]{0:T(128)} %param.19) | copy-start | bytes 772
  65.0 1.2 %copy-start.8 = (bf16[64,1280]{1,0:T(8,128)(2,1)}, bf16[64,1280]{1,0:T(8,128)(2,1)S(1)}, u32[]{:S(2)}) copy-start(bf16[64,1280]{1,0:T(8,128)(2,1)S(1)} %collective-permute-done.11.refs_3_) | copy-start | bytes 491524
  66.2 7.3 %collective-permute-start.14 = (bf16[64,1280]{1,0:T(8,128)(2,1)S(1)}, bf16[64,1280]{1,0:T(8,128)(2,1)S(1)}, u32[]{:S(2)}, u32[]{:S(2)}) collective-permute-start(bf16[64,1280]{1,0:T(8,128)(2,1)S(1)} %shard_map.104), channel_id=1, source_target_pairs={{0,4},{4,8},{8,12},{12,0},{1,5},{5,9},{9,13},{13,1},{2,6},{6,10},{... | collective-permute-start | bytes 491528 | tf_op jit(solution)/shard_map/ppermute | solution.py:167
  66.3 10.4 %collective-permute-start.12 = (bf16[64,1280]{1,0:T(8,128)(2,1)S(1)}, bf16[64,1280]{1,0:T(8,128)(2,1)S(1)}, u32[]{:S(2)}, u32[]{:S(2)}) collective-permute-start(bf16[64,1280]{1,0:T(8,128)(2,1)S(1)} %shard_map.103), channel_id=1, source_target_pairs={{0,8},{4,12},{8,0},{12,4},{1,9},{5,13},{9,1},{13,5},{2,10},{6,14},... | collective-permute-start | bytes 491528 | tf_op jit(solution)/shard_map/ppermute | solution.py:167
  73.5 6.0 %collective-permute-start.15 = (bf16[64,1280]{1,0:T(8,128)(2,1)S(1)}, bf16[64,1280]{1,0:T(8,128)(2,1)S(1)}, u32[]{:S(2)}, u32[]{:S(2)}) collective-permute-start(bf16[64,1280]{1,0:T(8,128)(2,1)S(1)} %collective-permute-done.14.refs_6_), channel_id=1, source_target_pairs={{0,2},{2,0},{1,3},{3,1},{4,6},{6,4},{5,7},{7,5},{8,10},{10,8},{9,1... | collective-permute-start | bytes 491528 | tf_op jit(solution)/shard_map/ppermute | solution.py:167
  76.7 5.7 %collective-permute-start.13 = (bf16[64,1280]{1,0:T(8,128)(2,1)S(1)}, bf16[64,1280]{1,0:T(8,128)(2,1)S(1)}, u32[]{:S(2)}, u32[]{:S(2)}) collective-permute-start(bf16[64,1280]{1,0:T(8,128)(2,1)S(1)} %collective-permute-done.12.refs_4_), channel_id=1, source_target_pairs={{0,2},{2,0},{1,3},{3,1},{4,6},{6,4},{5,7},{7,5},{8,10},{10,8},{9,1... | collective-permute-start | bytes 491528 | tf_op jit(solution)/shard_map/ppermute | solution.py:167
  82.4 1.1 %copy-start.1 = (bf16[1,64,5120]{2,1,0:T(8,128)(2,1)S(1)}, bf16[1,64,5120]{2,1,0:T(8,128)(2,1)}, u32[]{:S(2)}) copy-start(bf16[1,64,5120]{2,1,0:T(8,128)(2,1)} %param.14) | copy-start | bytes 1966084
  83.4 1.0 %copy-start.3 = (bf16[5120,32]{0,1:T(8,128)(2,1)S(1)}, bf16[5120,32]{0,1:T(8,128)(2,1)}, u32[]{:S(2)}) copy-start(bf16[5120,32]{0,1:T(8,128)(2,1)} %param.17) | copy-start | bytes 983044
  84.4 0.9 %copy-start.5 = (bf16[64,1280]{1,0:T(8,128)(2,1)S(1)}, bf16[64,1280]{1,0:T(8,128)(2,1)}, u32[]{:S(2)}) copy-start(bf16[64,1280]{1,0:T(8,128)(2,1)} %copy-done.4) | copy-start | bytes 491524
  85.3 0.9 %copy-start.7 = (bf16[64,1280]{1,0:T(8,128)(2,1)S(1)}, bf16[64,1280]{1,0:T(8,128)(2,1)}, u32[]{:S(2)}) copy-start(bf16[64,1280]{1,0:T(8,128)(2,1)} %copy-done.6) | copy-start | bytes 491524
  86.3 0.9 %copy-start.9 = (bf16[64,1280]{1,0:T(8,128)(2,1)S(1)}, bf16[64,1280]{1,0:T(8,128)(2,1)}, u32[]{:S(2)}) copy-start(bf16[64,1280]{1,0:T(8,128)(2,1)} %copy-done.8) | copy-start | bytes 491524

commit v3 on v0

v3 whole, which is shorter than its diff:
```python
import functools
import math

import jax
import jax.numpy as jnp
from jax import lax
from jax.experimental import pallas as pl
from jax.experimental.pallas import tpu as pltpu
from jax.sharding import PartitionSpec as P

CAP = 2
EPSILON = 1e-05
DOC_ROWS = 16
VMEM_LIMIT = 56 * 1024 * 1024


def fetch(refs, buffers, sems):
    copies = [
        pltpu.make_async_copy(ref, buffer, sems.at[number])
        for number, (ref, buffer) in enumerate(zip(refs, buffers))
    ]
    for copy in copies:
        copy.start()
    return [copy.wait for copy in copies]


def pack_kernel(groups, key_ref, value_ref, doc_ref, out_ref, *scratch):
    buffers, sems = scratch[:-1], scratch[-1]
    for wait in fetch((key_ref, value_ref, doc_ref), buffers, sems):
        wait()
    key_ref, value_ref, doc_ref = buffers
    rows, head_size = key_ref.shape
    tokens = rows // groups
    token = lax.broadcasted_iota(jnp.int32, (tokens, rows), 0)
    row = lax.broadcasted_iota(jnp.int32, (tokens, rows), 1)
    for group in range(groups):
        pick = (row == token * groups + group).astype(jnp.bfloat16)
        for place, ref in enumerate((key_ref, value_ref)):
            first = (place * groups + group) * tokens
            out_ref[first : first + tokens, :] = jnp.dot(
                pick, ref[...], preferred_element_type=jnp.float32
            ).astype(jnp.bfloat16)
    out_ref[2 * rows :, :] = jnp.broadcast_to(
        doc_ref[...].astype(jnp.float32), (DOC_ROWS, tokens)
    ).astype(jnp.bfloat16)


def block_kernel(ratio, groups, pair, reach, ctx_count, shifts, place_ref, *refs):
    count = len(shifts)
    operands = count + ctx_count + 1
    same_ref, cross_ref, mixed_ref = refs[operands : operands + 3]
    buffers, sems = refs[operands + 3 : -1], refs[-1]
    waits = fetch(refs[:operands], buffers, sems)
    for wait in waits[:-1]:
        wait()
    query_refs, pack_refs, weight_buffer = buffers[:count], buffers[count:-1], buffers[-1]
    heads, tokens, head_size = query_refs[0].shape
    scale = 1.0 / math.sqrt(head_size)
    ctx_index, core = place_ref[0], place_ref[1]
    part_rows = tokens // pair
    rows = lax.broadcasted_iota(jnp.int32, (tokens, tokens), 0)
    columns = lax.broadcasted_iota(jnp.int32, (tokens, tokens), 1)
    held_rows = groups * tokens

    def docs_of(ref):
        return ref[2 * held_rows : 2 * held_rows + 1, :].astype(jnp.float32)

    def attend(number, shift, spot):
        block_place = lax.rem(ctx_index - shift + ctx_count, ctx_count)
        packs = [pack_refs[(shift + step) % ctx_count] for step in range(reach + 1)]
        docs = docs_of(packs[0])
        own_doc = jnp.sum(jnp.where(rows == columns, docs, 0.0), axis=1, keepdims=True)
        allowed = [(own_doc == docs) & (columns <= rows)]
        for step in range(1, reach + 1):
            allowed.append((own_doc == docs_of(packs[step])) & (block_place >= step))
        allowed = jnp.concatenate(allowed, axis=1)
        for group in range(groups):
            first = group * tokens
            keys = jnp.concatenate([ref[first : first + tokens, :] for ref in packs], axis=0)
            first = held_rows + group * tokens
            held = jnp.concatenate([ref[first : first + tokens, :] for ref in packs], axis=0)
            for head in range(group * ratio, (group + 1) * ratio):
                scores = lax.dot_general(
                    query_refs[number][head],
                    keys,
                    (((1,), (1,)), ((), ())),
                    preferred_element_type=jnp.float32,
                )
                scores = jnp.where(allowed, scores * scale, -1e30)
                weights = jnp.exp(scores - jnp.max(scores, axis=1, keepdims=True))
                totals = jnp.sum(weights, axis=1, keepdims=True)
                mixed = jnp.dot(
                    weights.astype(jnp.bfloat16), held, preferred_element_type=jnp.float32
                )
                mixed_ref[spot, :, head * head_size : (head + 1) * head_size] = (
                    mixed / totals
                ).astype(jnp.bfloat16)

    def multiply(spot):
        product = jnp.dot(
            mixed_ref[spot], weight_buffer[...], preferred_element_type=jnp.float32
        )
        parts = [product[i * part_rows : (i + 1) * part_rows] for i in range(pair)]
        for turn in range(pair):
            piece = parts[turn]
            for own in range(1, pair):
                piece = jnp.where(core == own, parts[(own + turn) % pair], piece)
            if turn == 0:
                same_ref[spot] = piece
            else:
                cross_ref[turn - 1, spot] = piece.astype(jnp.bfloat16)

    outputs = same_ref.shape[0]
    valid = [
        ctx_index >= shift if number == 0 else ctx_index < shift
        for number, shift in enumerate(shifts)
    ]
    for number, shift in enumerate(shifts):
        pl.when(valid[number])(
            functools.partial(attend, number, shift, min(number, outputs - 1))
        )
    waits[-1]()
    if outputs < count:
        valid = [functools.reduce(jnp.logical_or, valid)]
    for spot in range(outputs):
        pl.when(valid[spot])(functools.partial(multiply, spot))


def column_of(kind, distance, ctx_index, ctx_count):
    if kind == "own":
        return ctx_index, ctx_index >= 0
    above, below = ctx_index + distance, ctx_index - distance
    if kind == "above":
        return jnp.minimum(above, ctx_count - 1), above < ctx_count
    if kind == "below":
        return jnp.maximum(below, 0), below >= 0
    place = jnp.where(above < ctx_count, above, jnp.maximum(below, 0))
    return place, (above < ctx_count) | (below >= 0)


def finish_kernel(kinds, back, ctx_count, exp_count, place_ref, *refs):
    count = len(kinds)
    operands = count + 2
    id_ref, keep_ref, gain_ref = refs[operands : operands + 3]
    out_ref, hidden_ref, normed_ref, result_ref = refs[-5 - operands - 1 :][:4]
    out_sem, buffers, sems = refs[-2 - operands], refs[-1 - operands : -1], refs[-1]
    waits = fetch(refs[:operands], buffers, sems)
    residual_ref, chunk_refs, router_ref = buffers[0], buffers[1:-1], buffers[-1]
    rows, width = residual_ref.shape
    experts = keep_ref.shape[1]
    here = router_ref.shape[0]
    ctx_index, exp_index = place_ref[0], place_ref[1]
    keep = keep_ref[...].astype(jnp.float32)
    upper = (
        lax.broadcasted_iota(jnp.int32, (rows, rows), 0)
        < lax.broadcasted_iota(jnp.int32, (rows, rows), 1)
    ).astype(jnp.bfloat16)
    ids = id_ref[...]
    onehot = (ids == lax.broadcasted_iota(jnp.int32, (experts, rows), 0)).astype(jnp.float32)
    earlier = jnp.dot(onehot.astype(jnp.bfloat16), upper, preferred_element_type=jnp.float32)
    ranking = jnp.sum(onehot * earlier, axis=0, keepdims=True)
    limits = jnp.dot(
        keep.astype(jnp.bfloat16),
        onehot.astype(jnp.bfloat16),
        preferred_element_type=jnp.float32,
    )
    local = ids - exp_index * here
    chosen = local == lax.broadcasted_iota(jnp.int32, (here, rows), 0)
    target = local * CAP + ranking.astype(jnp.int32)
    target = jnp.where((ranking < limits) & (local >= 0) & (local < here), target, -1)
    table = lax.broadcasted_iota(jnp.int32, (here * CAP, rows), 0) == target
    waits[0]()
    for number, (kind, distance) in enumerate(kinds):
        waits[1 + number]()
        chunk_ref = chunk_refs[number]
        columns = chunk_ref.shape[1]
        place, valid = column_of(kind, distance, ctx_index, ctx_count)
        if columns == width:
            place, valid = 0, ctx_index >= 0

        @pl.when(valid)
        def _(chunk_ref=chunk_ref, place=place, columns=columns):
            part = pl.ds(pl.multiple_of(place * columns, 128), columns)
            hidden_ref[:, part] = residual_ref[:, part].astype(jnp.float32) + chunk_ref[
                ...
            ].astype(jnp.float32)

    hidden = hidden_ref[...]
    power = jnp.sum(hidden * hidden, axis=1, keepdims=True)
    factor = lax.rsqrt(power / width + EPSILON)
    normed_ref[...] = (hidden * factor * gain_ref[...].astype(jnp.float32)).astype(jnp.bfloat16)
    waits[-1]()
    logits = lax.dot_general(
        router_ref[...],
        normed_ref[...],
        (((1,), (1,)), ((), ())),
        preferred_element_type=jnp.float32,
    )
    gates = jax.nn.sigmoid(jnp.sum(jnp.where(chosen, logits, 0.0), axis=0, keepdims=True))
    slot_gates = jnp.sum(jnp.where(table, gates, 0.0), axis=1, keepdims=True)
    slots = jnp.dot(
        table.astype(jnp.bfloat16), normed_ref[...], preferred_element_type=jnp.float32
    )
    result_ref[...] = (slots * slot_gates).astype(jnp.bfloat16)
    source = lax.rem(exp_index - back + exp_count, exp_count)
    copy = pltpu.make_async_copy(result_ref, out_ref.at[source], out_sem)
    copy.start()
    copy.wait()


def on_device(
    queries,
    key_states,
    values,
    doc_ids,
    residual,
    out_proj,
    norm_gain,
    router,
    expert_ids,
    keep_counts,
):
    _, tokens, heads, head_size = queries.shape
    groups = key_states.shape[2]
    ctx_count = lax.axis_size("ctx")
    pair = lax.axis_size("tp")
    exp_count = lax.axis_size("exp")
    part_rows = tokens // pair
    width = residual.shape[2]
    columns = out_proj.shape[1]
    experts_here = router.shape[1]
    ctx_index = lax.axis_index("ctx")
    core = lax.axis_index("tp")
    exp_index = lax.axis_index("exp")
    reach = -(-(ctx_count * tokens // 2 - 1) // tokens)
    vmem = pl.BlockSpec(memory_space=pltpu.VMEM)
    smem = pl.BlockSpec(memory_space=pltpu.SMEM)
    anywhere = pl.BlockSpec(memory_space=pl.ANY)
    params = pltpu.CompilerParams(vmem_limit_bytes=VMEM_LIMIT)
    bf16, f32 = jnp.bfloat16, jnp.float32

    def over(array, axis, step):
        count = lax.axis_size(axis)
        if step % count == 0:
            return array
        return lax.ppermute(array, axis, [(i, (i + step) % count) for i in range(count)])

    def along(array, moves):
        return lax.ppermute(array, "ctx", moves)

    pack = pl.pallas_call(
        functools.partial(pack_kernel, groups),
        out_shape=jax.ShapeDtypeStruct((2 * groups * tokens + DOC_ROWS, head_size), bf16),
        in_specs=[anywhere] * 3,
        out_specs=vmem,
        scratch_shapes=[pltpu.VMEM((groups * tokens, head_size), bf16)] * 2
        + [pltpu.VMEM(doc_ids.shape, doc_ids.dtype), pltpu.SemaphoreType.DMA((3,))],
        compiler_params=params,
    )(
        key_states.reshape(groups * tokens, head_size),
        values.reshape(groups * tokens, head_size),
        doc_ids,
    )
    packs = [over(pack, "ctx", step) for step in range(ctx_count)]
    rising = falling = queries[0].transpose(1, 0, 2)
    place = jnp.stack([ctx_index, core])

    def project(blocks, shifts, outputs, coming=None):
        operands = [*blocks, *packs, out_proj]
        same, cross = pl.pallas_call(
            functools.partial(
                block_kernel, heads // groups, groups, pair, reach, ctx_count, shifts
            ),
            out_shape=[
                jax.ShapeDtypeStruct((outputs, part_rows, columns), f32),
                jax.ShapeDtypeStruct((pair - 1, outputs, part_rows, columns), bf16),
            ],
            in_specs=[smem] + [anywhere] * len(operands),
            out_specs=[vmem] * 2,
            scratch_shapes=[pltpu.VMEM((outputs, tokens, heads * head_size), bf16)]
            + [pltpu.VMEM(array.shape, array.dtype) for array in operands]
            + [pltpu.SemaphoreType.DMA((len(operands),))],
            compiler_params=params,
            cost_estimate=pl.CostEstimate(
                flops=outputs
                * (4 * blocks[0].size * (reach + 1) * tokens + 2 * tokens * out_proj.size),
                bytes_accessed=2 * (out_proj.size + len(blocks) * blocks[0].size),
                transcendentals=outputs * heads * tokens * (reach + 1) * tokens,
            ),
        )(place, *operands)
        if coming is not None:
            coming, cross = lax.optimization_barrier((coming, cross))
        crossed = [over(cross[turn - 1], "tp", turn) for turn in range(1, pair)]
        return [
            sum((other[number].astype(f32) for other in crossed), same[number]).astype(bf16)
            for number in range(outputs)
        ], coming

    aligned = columns % 128 == 0

    def forward(chunk):
        return [over(chunk, "exp", back) for back in range(1, exp_count if aligned else 1)]

    ids = expert_ids[:, :, 0]
    all_ids, all_residual = [ids], [residual[0]]
    kinds, chunks, sent = [], [], []
    for distance in range(1, ctx_count + 1):
        last = distance == ctx_count
        if not last:
            coming = (
                along(rising, [(i, i + 1) for i in range(distance - 1, ctx_count - 1)]),
                along(falling, [(i, i - 1) for i in range(1, ctx_count - distance + 1)]),
            )
        held = distance - 1
        blocks = (rising, falling)
        if held >= 2:
            blocks, sent[held - 2], all_ids, all_residual = lax.optimization_barrier(
                (blocks, sent[held - 2], all_ids, all_residual)
            )
        if last:
            coming = None
        if held == 0:
            totals, coming = project((rising,), (0,), 1, coming)
        else:
            both = 1 if 2 * held >= ctx_count else 2
            totals, coming = project(blocks, (held, ctx_count - held), both, coming)
        if not last:
            rising, falling = coming
        to_lower = [(i, i - held) for i in range(held, ctx_count)]
        to_upper = [(i, i + held) for i in range(ctx_count - held)]
        if held == 0:
            arrived = [("own", totals[0])]
            early_ids, early_residual, _ = lax.optimization_barrier((ids, residual[0], packs))
            all_ids += [over(early_ids, "exp", back) for back in range(1, exp_count)]
            all_residual += [over(early_residual, "exp", back) for back in range(1, exp_count)]
        elif 2 * held >= ctx_count:
            arrived = [("either", along(totals[0], to_lower + to_upper))]
        else:
            arrived = [
                ("above", along(totals[0], to_lower)),
                ("below", along(totals[1], to_upper)),
            ]
        kinds.append([(kind, held) for kind, _ in arrived])
        chunks.append([chunk for _, chunk in arrived])
        sent.append([forward(chunk) for _, chunk in arrived])
    groups_of = [
        [[chunk] + others for chunk, others in zip(group, others_of)]
        for group, others_of in zip(chunks, sent)
    ]
    if aligned:
        kinds = [kind for group in kinds for kind in group]
        flat = [arrays for group in groups_of for arrays in group]
    else:
        whole = jnp.zeros((ctx_count, part_rows, columns), bf16)
        for group, arrays in zip(kinds, chunks):
            for (kind, distance), chunk in zip(group, arrays):
                spot, valid = column_of(kind, distance, ctx_index, ctx_count)
                whole = whole.at[spot].add(jnp.where(valid, chunk, 0))
        whole = whole.transpose(1, 0, 2).reshape(part_rows, width)
        kinds = [("own", 0)]
        flat = [[over(whole, "exp", back) for back in range(exp_count)]]
    out = None
    for back in range(exp_count):
        fetched = [all_residual[back]] + [arrays[back] for arrays in flat] + [router.T]
        others = [all_ids[back], keep_counts.reshape(1, -1), norm_gain.reshape(1, -1)]
        kept = [] if out is None else [out]
        out = pl.pallas_call(
            functools.partial(finish_kernel, kinds, back, ctx_count, exp_count),
            out_shape=jax.ShapeDtypeStruct((exp_count, experts_here * CAP, width), bf16),
            in_specs=[smem]
            + [anywhere] * len(fetched)
            + [vmem] * len(others)
            + [anywhere] * len(kept),
            out_specs=anywhere,
            scratch_shapes=[
                pltpu.VMEM((part_rows, width), f32),
                pltpu.VMEM((part_rows, width), bf16),
                pltpu.VMEM((experts_here * CAP, width), bf16),
                pltpu.SemaphoreType.DMA,
            ]
            + [pltpu.VMEM(array.shape, array.dtype) for array in fetched]
            + [pltpu.SemaphoreType.DMA((len(fetched),))],
            input_output_aliases={1 + len(fetched) + len(others): 0} if kept else {},
            compiler_params=params,
        )(jnp.stack([ctx_index, exp_index]), *fetched, *others, *kept)
    return out.reshape(exp_count, experts_here, CAP, width)


def solution(mesh):
    placed = (
        P(("groups", "exp"), "ctx", "tp", None),
        P(("groups", "exp"), "ctx", "tp", None),
        P(("groups", "exp"), "ctx", "tp", None),
        P(("groups", "exp"), "ctx"),
        P(("groups", "exp"), ("ctx", "tp"), None),
        P("tp", "ctx"),
        P(),
        P(None, "exp"),
        P(("groups", "exp"), ("ctx", "tp"), None),
        P("groups"),
    )
    return jax.shard_map(
        on_device,
        mesh=mesh,
        in_specs=placed,
        out_specs=P(("groups", "ctx", "tp"), "exp", None, None),
        check_vma=False,
    )
```

time: 173 us -> 115 us (0.66)
  blocking collectives: 60.6 us -> 0 us
  Pallas kernels: 0 us -> 34.3 us
  starting transfers between devices: 4.93 us -> 38.6 us
  waiting for transfers between devices: 56.6 us -> 30.3 us
  matrix products: 19.5 us -> 0 us
  between operations: 13.6 us -> 0.5 us
  local copies, waits for them, and re-layouts: 12.5 us -> 7.23 us
    all_gather x3 -> x0, blocking collectives: 40.9 us -> none  [the longest x1 14.2 us: on_device(): value_piece = lax.all_gather(values, 'ctx', axis=1, tiled=True)]
    ppermute x0 -> x24, starting transfers between devices: none -> 38.6 us  [the longest x10 26.1 us: along(): return lax.ppermute(array, 'ctx', moves)]
    pallas_call x0 -> x7, Pallas kernels: none -> 34.3 us  [the longest x4 24.5 us: project(): pl.pallas_call(functools.partial(block_kernel, heads // groups, groups, p...]
    all_gather x1 -> x0, waiting for transfers between devices: 31.1 us -> none  [on_device(): gathered = lax.all_gather(attn_rows, 'ctx', axis=1, tiled=True)]
    ppermute x0 -> x24, waiting for transfers between devices: none -> 30.3 us  [the longest x10 16.5 us: along(): return lax.ppermute(array, 'ctx', moves)]
    all_to_all x1 -> x0, blocking collectives: 19.7 us -> none  [on_device(): lax.all_to_all(outgoing, 'exp', split_axis=0, concat_axis=0, tiled=True)]
    dot_general x6 -> x0, matrix products: 19.5 us -> none  [the longest x1 11.5 us: on_device(): jnp.einsum('secd,de->sec', arrived, router, preferred_element_type=jnp.fl...]
    all_to_all x1 -> x0, waiting for transfers between devices: 17.5 us -> none  [on_device(): lax.all_to_all(own_columns.astype(jnp.bfloat16), 'ctx', split_axis=0, con...]
  transfers between devices with their start and end apart: 3 -> 24, of which waited for: 3 -> 8; matrix products, arithmetic and copies ran while one was open for 0% -> 4% of each run, Pallas kernels for 0% -> 26%
where the time goes in v3:
time: 115 us; the launch traced here: 114 us
  starting transfers between devices  38.6 us (34%)
  Pallas kernels  34.3 us (30%)
  waiting for transfers between devices  30.3 us (26%)
  local copies, waits for them, and re-layouts  7.23 us (6%)
  other arithmetic  3.41 us (3%)
    ppermute x10, starting transfers between devices, along(): return lax.ppermute(array, 'ctx', moves)  26.1 us
    pallas_call x4, Pallas kernels, project(): pl.pallas_call(functools.partial(block_kernel, heads // groups, groups, p...  24.5 us
    ppermute x10, waiting for transfers between devices, along(): return lax.ppermute(array, 'ctx', moves)  16.5 us
    ppermute x14, waiting for transfers between devices, over(): lax.ppermute(array, axis, [(i, (i + step) % count) for i in range(count)])  13.8 us
    ppermute x14, starting transfers between devices, over(): lax.ppermute(array, axis, [(i, (i + step) % count) for i in range(count)])  12.5 us
    pallas_call x2, Pallas kernels, on_device(): pl.pallas_call(functools.partial(finish_kernel, kinds, back, ctx_count, e...  8 us
    reshape x1, local copies, waits for them, and re-layouts, on_device(): return out.reshape(exp_count, experts_here, CAP, width)  3.86 us
    unnamed x52, local copies, waits for them, and re-layouts  2.76 us
  transfers between devices with their start and end apart: 24, of which 8 were waited for; matrix products, arithmetic and copies ran while one was open for 4% of the time, Pallas kernels for 26%

profile of v3, /device:TPU:0, one launch (start us, length us, event | category | flops | bytes accessed | tf_op | source)
XLA Modules:
  0.0 114.4 jit_solution(17828917799421073062)
XLA Ops:
  0.0 1.3 %collective-permute-start.1 = (bf16[10,128,128]{2,1,0:T(8,128)(2,1)}, bf16[10,128,128]{2,1,0:T(8,128)(2,1)S(1)}, u32[]{:S(2)}, u32[]{:S(2)}) collective-permute-start(bf16[10,128,128]{2,1,0:T(8,128)(2,1)} %bitcast.30), channel_id=1, source_target_pairs={{4,0},{8,4},{12,8},{5,1},{9,5},{13,9},{6,2},{10,6},{14,10},{7,3},{... | collective-permute-start | bytes 983048 | tf_op jit(solution)/shard_map/ppermute | solution.py:249
  1.3 5.6 %collective-permute-start = (bf16[10,128,128]{2,1,0:T(8,128)(2,1)}, bf16[10,128,128]{2,1,0:T(8,128)(2,1)S(1)}, u32[]{:S(2)}, u32[]{:S(2)}) collective-permute-start(bf16[10,128,128]{2,1,0:T(8,128)(2,1)} %bitcast.31), channel_id=1, source_target_pairs={{0,4},{4,8},{8,12},{1,5},{5,9},{9,13},{2,6},{6,10},{10,14},{3,7},{... | collective-permute-start | bytes 983048 | tf_op jit(solution)/shard_map/ppermute | solution.py:249
  6.9 1.8 %shard_map.100.refs_1_.refs_2_ = bf16[528,128]{1,0:T(8,128)(2,1)} custom-call(bf16[256,128]{1,0:T(8,128)(2,1)} %bitcast.33, bf16[256,128]{1,0:T(8,128)(2,1)} %bitcast.34, s32[1,128]{1,0:T(1,128)} %doc_ref.1), custom_call_target="tpu_custom_call" | custom-call | tf_op jit(solution)/shard_map/pallas_call | solution.py:251
  8.6 1.9 %collective-permute-start.4 = (bf16[528,128]{1,0:T(8,128)(2,1)}, bf16[528,128]{1,0:T(8,128)(2,1)S(1)}, u32[]{:S(2)}, u32[]{:S(2)}) collective-permute-start(bf16[528,128]{1,0:T(8,128)(2,1)} %shard_map.100.refs_1_.refs_2_), channel_id=1, source_target_pairs={{0,12},{4,0},{8,4},{12,8},{1,13},{5,1},{9,5},{13,9},{2,14},{6,2},{... | collective-permute-start | bytes 405512 | tf_op jit(solution)/shard_map/ppermute | solution.py:246
  10.5 1.6 %collective-permute-start.3 = (bf16[528,128]{1,0:T(8,128)(2,1)}, bf16[528,128]{1,0:T(8,128)(2,1)S(1)}, u32[]{:S(2)}, u32[]{:S(2)}) collective-permute-start(bf16[528,128]{1,0:T(8,128)(2,1)} %shard_map.100.refs_1_.refs_2_), channel_id=1, source_target_pairs={{0,8},{4,12},{8,0},{12,4},{1,9},{5,13},{9,1},{13,5},{2,10},{6,14},... | collective-permute-start | bytes 405512 | tf_op jit(solution)/shard_map/ppermute | solution.py:246
  12.2 1.6 %collective-permute-start.2 = (bf16[528,128]{1,0:T(8,128)(2,1)}, bf16[528,128]{1,0:T(8,128)(2,1)S(1)}, u32[]{:S(2)}, u32[]{:S(2)}) collective-permute-start(bf16[528,128]{1,0:T(8,128)(2,1)} %shard_map.100.refs_1_.refs_2_), channel_id=1, source_target_pairs={{0,4},{4,8},{8,12},{12,0},{1,5},{5,9},{9,13},{13,1},{2,6},{6,10},{... | collective-permute-start | bytes 405512 | tf_op jit(solution)/shard_map/ppermute | solution.py:246
  14.4 3.8 %collective-permute-done.4.refs_4_.refs_5_ = bf16[528,128]{1,0:T(8,128)(2,1)S(1)} collective-permute-done((bf16[528,128]{1,0:T(8,128)(2,1)}, bf16[528,128]{1,0:T(8,128)(2,1)S(1)}, u32[]{:S(2)}, u32[]{:S(2)}) %collective-permute-start.4) | collective-permute-done | bytes 135200 | tf_op jit(solution)/shard_map/ppermute | solution.py:246
  18.2 7.4 %collective-permute-done.3.refs_3_.refs_4_ = bf16[528,128]{1,0:T(8,128)(2,1)S(1)} collective-permute-done((bf16[528,128]{1,0:T(8,128)(2,1)}, bf16[528,128]{1,0:T(8,128)(2,1)S(1)}, u32[]{:S(2)}, u32[]{:S(2)}) %collective-permute-start.3) | collective-permute-done | bytes 135200 | tf_op jit(solution)/shard_map/ppermute | solution.py:246
  26.9 6.0 %shard_map.101 = (f32[1,64,1280]{2,1,0:T(8,128)}, bf16[1,1,64,1280]{3,2,1,0:T(8,128)(2,1)}) custom-call(s32[2]{0:T(128)} %pad_add_fusion.1.place_ref, bf16[10,128,128]{2,1,0:T(8,128)(2,1)} %bitcast.32, bf16[528,128]{1,0:T(8,128)(2,1)} %shard_map.100.refs_1_.refs_2_, bf16[528,128]{1,0:T(8,128)(2,1)} %copy-done.2, bf16[528,128]{1,0:T(8,128)(2,1)} %copy-done.1, ...), custom_call_target="tpu_custom_call" | custom-call | flops 671088640 | bytes 3604480 | tf_op jit(solution)/shard_map/pallas_call | solution.py:270
  33.6 1.3 %collective-permute-start.6 = (bf16[10,128,128]{2,1,0:T(8,128)(2,1)S(1)}, bf16[10,128,128]{2,1,0:T(8,128)(2,1)S(1)}, u32[]{:S(2)}, u32[]{:S(2)}) collective-permute-start(bf16[10,128,128]{2,1,0:T(8,128)(2,1)S(1)} %collective-permute-done.1.refs_1_), channel_id=1, source_target_pairs={{4,0},{8,4},{5,1},{9,5},{6,2},{10,6},{7,3},{11,7},{20,16},{24,20},... | collective-permute-start | bytes 983048 | tf_op jit(solution)/shard_map/ppermute | solution.py:249
  35.0 1.6 %collective-permute-start.11 = (s32[1,64]{1,0:T(1,128)S(1)}, s32[1,64]{1,0:T(1,128)S(1)}, u32[]{:S(2)}, u32[]{:S(2)}) collective-permute-start(s32[1,64]{1,0:T(1,128)S(1)} %bitcast.38), channel_id=1, source_target_pairs={{0,2},{2,0},{1,3},{3,1},{4,6},{6,4},{5,7},{7,5},{8,10},{10,8},{9,1... | collective-permute-start | bytes 776 | tf_op jit(solution)/shard_map/ppermute | solution.py:246
  37.1 6.2 %shard_map.102 = (f32[2,64,1280]{2,1,0:T(8,128)}, bf16[1,2,64,1280]{3,2,1,0:T(8,128)(2,1)}) custom-call(s32[2]{0:T(128)} %pad_add_fusion.1.place_ref, bf16[10,128,128]{2,1,0:T(8,128)(2,1)} %copy-done.25, bf16[10,128,128]{2,1,0:T(8,128)(2,1)} %copy-done.24, bf16[528,128]{1,0:T(8,128)(2,1)} %shard_map.100.refs_1_.refs_2_, bf16[528,128]{1,0:T(8,128)(2,1)} %copy-done.2, ...), custom_call_target="tpu_custom_call" | custom-call | flops 1342177280 | bytes 3932160 | tf_op jit(solution)/shard_map/pallas_call | solution.py:270
  43.4 2.9 %collective-permute-done.6.refs_1_ = bf16[10,128,128]{2,1,0:T(8,128)(2,1)S(1)} collective-permute-done((bf16[10,128,128]{2,1,0:T(8,128)(2,1)S(1)}, bf16[10,128,128]{2,1,0:T(8,128)(2,1)S(1)}, u32[]{:S(2)}, u32[]{:S(2)}) %collective-permute-start.6) | collective-permute-done | bytes 327712 | tf_op jit(solution)/shard_map/ppermute | solution.py:249
  46.4 1.6 %collective-permute-start.10 = (bf16[64,1280]{1,0:T(8,128)(2,1)S(1)}, bf16[64,1280]{1,0:T(8,128)(2,1)S(1)}, u32[]{:S(2)}, u32[]{:S(2)}) collective-permute-start(bf16[64,1280]{1,0:T(8,128)(2,1)S(1)} %fusion.refs_1_), channel_id=1, source_target_pairs={{0,2},{2,0},{1,3},{3,1},{4,6},{6,4},{5,7},{7,5},{8,10},{10,8},{9,1... | collective-permute-start | bytes 491528 | tf_op jit(solution)/shard_map/ppermute | solution.py:246
  48.6 1.3 %collective-permute-start.8 = (bf16[10,128,128]{2,1,0:T(8,128)(2,1)S(1)}, bf16[10,128,128]{2,1,0:T(8,128)(2,1)S(1)}, u32[]{:S(2)}, u32[]{:S(2)}) collective-permute-start(bf16[10,128,128]{2,1,0:T(8,128)(2,1)S(1)} %collective-permute-done.6.refs_1_), channel_id=1, source_target_pairs={{4,0},{5,1},{6,2},{7,3},{20,16},{21,17},{22,18},{23,19}} | collective-permute-start | bytes 983048 | tf_op jit(solution)/shard_map/ppermute | solution.py:249
  49.9 1.1 fusion.2
  51.1 7.9 %collective-permute-start.16 = (bf16[64,1280]{1,0:T(8,128)(2,1)S(1)}, bf16[64,1280]{1,0:T(8,128)(2,1)S(1)}, u32[]{:S(2)}, u32[]{:S(2)}) collective-permute-start(bf16[64,1280]{1,0:T(8,128)(2,1)S(1)} %get-tuple-element.73), channel_id=1, source_target_pairs={{0,4},{4,8},{8,12},{1,5},{5,9},{9,13},{2,6},{6,10},{10,14},{3,7},{... | collective-permute-start | bytes 491528 | tf_op jit(solution)/shard_map/ppermute | solution.py:249
  59.0 1.3 %collective-permute-start.14 = (bf16[64,1280]{1,0:T(8,128)(2,1)S(1)}, bf16[64,1280]{1,0:T(8,128)(2,1)S(1)}, u32[]{:S(2)}, u32[]{:S(2)}) collective-permute-start(bf16[64,1280]{1,0:T(8,128)(2,1)S(1)} %get-tuple-element.74), channel_id=1, source_target_pairs={{4,0},{8,4},{12,8},{5,1},{9,5},{13,9},{6,2},{10,6},{14,10},{7,3},{... | collective-permute-start | bytes 491528 | tf_op jit(solution)/shard_map/ppermute | solution.py:249
  60.3 2.5 %collective-permute-done.16.refs_3_ = bf16[64,1280]{1,0:T(8,128)(2,1)S(1)} collective-permute-done((bf16[64,1280]{1,0:T(8,128)(2,1)S(1)}, bf16[64,1280]{1,0:T(8,128)(2,1)S(1)}, u32[]{:S(2)}, u32[]{:S(2)}) %collective-permute-start.16) | collective-permute-done | bytes 163872 | tf_op jit(solution)/shard_map/ppermute | solution.py:249
  62.7 0.9 collective-permute-start.17
  63.7 4.2 %collective-permute-done.14.refs_2_ = bf16[64,1280]{1,0:T(8,128)(2,1)S(1)} collective-permute-done((bf16[64,1280]{1,0:T(8,128)(2,1)S(1)}, bf16[64,1280]{1,0:T(8,128)(2,1)S(1)}, u32[]{:S(2)}, u32[]{:S(2)}) %collective-permute-start.14) | collective-permute-done | bytes 163872 | tf_op jit(solution)/shard_map/ppermute | solution.py:249
  68.5 6.3 %shard_map.103 = (f32[1,64,1280]{2,1,0:T(8,128)}, bf16[1,1,64,1280]{3,2,1,0:T(8,128)(2,1)}) custom-call(s32[2]{0:T(128)} %pad_add_fusion.1.place_ref, bf16[10,128,128]{2,1,0:T(8,128)(2,1)} %copy-done.6, bf16[10,128,128]{2,1,0:T(8,128)(2,1)} %copy-done.7, bf16[528,128]{1,0:T(8,128)(2,1)} %shard_map.100.refs_1_.refs_2_, bf16[528,128]{1,0:T(8,128)(2,1)} %copy-done.2, ...), custom_call_target="tpu_custom_call" | custom-call | flops 671088640 | bytes 3932160 | tf_op jit(solution)/shard_map/pallas_call | solution.py:270
  75.7 6.1 %shard_map.104 = (f32[1,64,1280]{2,1,0:T(8,128)}, bf16[1,1,64,1280]{3,2,1,0:T(8,128)(2,1)}) custom-call(s32[2]{0:T(128)} %pad_add_fusion.1.place_ref, bf16[10,128,128]{2,1,0:T(8,128)(2,1)} %copy-done.8, bf16[10,128,128]{2,1,0:T(8,128)(2,1)} %copy-done.9, bf16[528,128]{1,0:T(8,128)(2,1)} %shard_map.100.refs_1_.refs_2_, bf16[528,128]{1,0:T(8,128)(2,1)} %copy-done.2, ...), custom_call_target="tpu_custom_call" | custom-call | flops 671088640 | bytes 3932160 | tf_op jit(solution)/shard_map/pallas_call | solution.py:270
  82.0 1.0 collective-permute-start.19
  83.5 1.0 fusion.4
  84.5 5.2 %collective-permute-start.22 = (bf16[64,1280]{1,0:T(8,128)(2,1)S(1)}, bf16[64,1280]{1,0:T(8,128)(2,1)S(1)}, u32[]{:S(2)}, u32[]{:S(2)}) collective-permute-start(bf16[64,1280]{1,0:T(8,128)(2,1)S(1)} %fusion.4), channel_id=1, source_target_pairs={{12,0},{0,12},{13,1},{1,13},{14,2},{2,14},{15,3},{3,15},{28,16},{1... | collective-permute-start | bytes 491528 | tf_op jit(solution)/shard_map/ppermute | solution.py:249
  89.7 6.9 %collective-permute-done.19.refs_4_ = bf16[64,1280]{1,0:T(8,128)(2,1)S(1)} collective-permute-done((bf16[64,1280]{1,0:T(8,128)(2,1)S(1)}, bf16[64,1280]{1,0:T(8,128)(2,1)S(1)}, u32[]{:S(2)}, u32[]{:S(2)}) %collective-permute-start.19) | collective-permute-done | bytes 163872 | tf_op jit(solution)/shard_map/ppermute | solution.py:249
  96.5 1.1 %collective-permute-start.20 = (bf16[64,1280]{1,0:T(8,128)(2,1)S(1)}, bf16[64,1280]{1,0:T(8,128)(2,1)S(1)}, u32[]{:S(2)}, u32[]{:S(2)}) collective-permute-start(bf16[64,1280]{1,0:T(8,128)(2,1)S(1)} %collective-permute-done.19.refs_4_), channel_id=1, source_target_pairs={{0,2},{2,0},{1,3},{3,1},{4,6},{6,4},{5,7},{7,5},{8,10},{10,8},{9,1... | collective-permute-start | bytes 491528 | tf_op jit(solution)/shard_map/ppermute | solution.py:246
  99.7 4.0 %shard_map.105.refs_10_ = bf16[2,64,5120]{2,1,0:T(8,128)(2,1)} custom-call(s32[2]{0:T(128)} %pad_add_fusion.place_ref, bf16[64,5120]{1,0:T(8,128)(2,1)} %bitcast.28, bf16[64,1280]{1,0:T(8,128)(2,1)} %copy-done.3, bf16[64,1280]{1,0:T(8,128)(2,1)} %copy-done.15, bf16[64,1280]{1,0:T(8,128)(2,1)} %copy-done.13, bf16[64,1280]{1,0:T(8,128)(2,1)} %copy-done.17, ...), custom_call_target="tpu_custom_call" | custom-call | tf_op jit(solution)/shard_map/pallas_call | solution.py:367
  103.8 2.1 %collective-permute-done.23.refs_5_ = bf16[64,1280]{1,0:T(8,128)(2,1)S(1)} collective-permute-done((bf16[64,1280]{1,0:T(8,128)(2,1)S(1)}, bf16[64,1280]{1,0:T(8,128)(2,1)S(1)}, u32[]{:S(2)}, u32[]{:S(2)}) %collective-permute-start.23) | collective-permute-done | bytes 163872 | tf_op jit(solution)/shard_map/ppermute | solution.py:246
  106.5 4.0 %shard_map.106 = bf16[2,64,5120]{2,1,0:T(8,128)(2,1)} custom-call(s32[2]{0:T(128)} %pad_add_fusion.place_ref, bf16[64,5120]{1,0:T(8,128)(2,1)} %copy-done.4, bf16[64,1280]{1,0:T(8,128)(2,1)} %copy-done.12, bf16[64,1280]{1,0:T(8,128)(2,1)} %copy-done.16, bf16[64,1280]{1,0:T(8,128)(2,1)} %copy-done.14, ...), custom_call_target="tpu_custom_call", output_to_operand_aliasing={{}: (11, {})} | custom-call | tf_op jit(solution)/shard_map/pallas_call | solution.py:367
  110.5 3.9 %reshape.36 = bf16[2,32,2,5120]{3,2,1,0:T(2,128)(2,1)} reshape(bf16[2,64,5120]{2,1,0:T(8,128)(2,1)} %shard_map.106) | data formatting | bytes 2621440 | tf_op jit(solution)/shard_map/reshape | solution.py:386
  (83 shorter events, 8.7 us)
Async XLA Ops:
  0.0 32.9 %collective-permute-start.1 = (bf16[10,128,128]{2,1,0:T(8,128)(2,1)}, bf16[10,128,128]{2,1,0:T(8,128)(2,1)S(1)}, u32[]{:S(2)}, u32[]{:S(2)}) collective-permute-start(bf16[10,128,128]{2,1,0:T(8,128)(2,1)} %bitcast.30), channel_id=1, source_target_pairs={{4,0},{8,4},{12,8},{5,1},{9,5},{13,9},{6,2},{10,6},{14,10},{7,3},{... | collective-permute-start | bytes 983048 | tf_op jit(solution)/shard_map/ppermute | solution.py:249
  1.3 31.6 %collective-permute-start = (bf16[10,128,128]{2,1,0:T(8,128)(2,1)}, bf16[10,128,128]{2,1,0:T(8,128)(2,1)S(1)}, u32[]{:S(2)}, u32[]{:S(2)}) collective-permute-start(bf16[10,128,128]{2,1,0:T(8,128)(2,1)} %bitcast.31), channel_id=1, source_target_pairs={{0,4},{4,8},{8,12},{1,5},{5,9},{9,13},{2,6},{6,10},{10,14},{3,7},{... | collective-permute-start | bytes 983048 | tf_op jit(solution)/shard_map/ppermute | solution.py:249
  8.6 9.6 %collective-permute-start.4 = (bf16[528,128]{1,0:T(8,128)(2,1)}, bf16[528,128]{1,0:T(8,128)(2,1)S(1)}, u32[]{:S(2)}, u32[]{:S(2)}) collective-permute-start(bf16[528,128]{1,0:T(8,128)(2,1)} %shard_map.100.refs_1_.refs_2_), channel_id=1, source_target_pairs={{0,12},{4,0},{8,4},{12,8},{1,13},{5,1},{9,5},{13,9},{2,14},{6,2},{... | collective-permute-start | bytes 405512 | tf_op jit(solution)/shard_map/ppermute | solution.py:246
  10.5 15.0 %collective-permute-start.3 = (bf16[528,128]{1,0:T(8,128)(2,1)}, bf16[528,128]{1,0:T(8,128)(2,1)S(1)}, u32[]{:S(2)}, u32[]{:S(2)}) collective-permute-start(bf16[528,128]{1,0:T(8,128)(2,1)} %shard_map.100.refs_1_.refs_2_), channel_id=1, source_target_pairs={{0,8},{4,12},{8,0},{12,4},{1,9},{5,13},{9,1},{13,5},{2,10},{6,14},... | collective-permute-start | bytes 405512 | tf_op jit(solution)/shard_map/ppermute | solution.py:246
  12.2 13.4 %collective-permute-start.2 = (bf16[528,128]{1,0:T(8,128)(2,1)}, bf16[528,128]{1,0:T(8,128)(2,1)S(1)}, u32[]{:S(2)}, u32[]{:S(2)}) collective-permute-start(bf16[528,128]{1,0:T(8,128)(2,1)} %shard_map.100.refs_1_.refs_2_), channel_id=1, source_target_pairs={{0,4},{4,8},{8,12},{12,0},{1,5},{5,9},{9,13},{13,1},{2,6},{6,10},{... | collective-permute-start | bytes 405512 | tf_op jit(solution)/shard_map/ppermute | solution.py:246
  14.4 20.6 %copy-start.22 = (s32[1,64,1]{1,2,0:T(1,128)S(1)}, s32[1,64,1]{1,2,0:T(1,128)}, u32[]{:S(2)}) copy-start(s32[1,64,1]{1,2,0:T(1,128)} %param.18) | copy-start | bytes 772
  14.4 22.2 %copy-start.5 = (bf16[1,64,5120]{2,1,0:T(8,128)(2,1)S(1)}, bf16[1,64,5120]{2,1,0:T(8,128)(2,1)}, u32[]{:S(2)}) copy-start(bf16[1,64,5120]{2,1,0:T(8,128)(2,1)} %param.14) | copy-start | bytes 1966084
  32.9 10.4 %collective-permute-start.5 = (bf16[10,128,128]{2,1,0:T(8,128)(2,1)S(1)}, bf16[10,128,128]{2,1,0:T(8,128)(2,1)S(1)}, u32[]{:S(2)}, u32[]{:S(2)}) collective-permute-start(bf16[10,128,128]{2,1,0:T(8,128)(2,1)S(1)} %collective-permute-done.refs_0_), channel_id=1, source_target_pairs={{4,8},{8,12},{5,9},{9,13},{6,10},{10,14},{7,11},{11,15},{20,24},{2... | collective-permute-start | bytes 983048 | tf_op jit(solution)/shard_map/ppermute | solution.py:249
  33.6 12.7 %collective-permute-start.6 = (bf16[10,128,128]{2,1,0:T(8,128)(2,1)S(1)}, bf16[10,128,128]{2,1,0:T(8,128)(2,1)S(1)}, u32[]{:S(2)}, u32[]{:S(2)}) collective-permute-start(bf16[10,128,128]{2,1,0:T(8,128)(2,1)S(1)} %collective-permute-done.1.refs_1_), channel_id=1, source_target_pairs={{4,0},{8,4},{5,1},{9,5},{6,2},{10,6},{7,3},{11,7},{20,16},{24,20},... | collective-permute-start | bytes 983048 | tf_op jit(solution)/shard_map/ppermute | solution.py:249
  34.9 11.4 %collective-permute-start.9 = (bf16[1,64,1280]{2,1,0:T(8,128)(2,1)}, bf16[1,64,1280]{2,1,0:T(8,128)(2,1)S(1)}, u32[]{:S(2)}, u32[]{:S(2)}) collective-permute-start(bf16[1,64,1280]{2,1,0:T(8,128)(2,1)} %bitcast.40), channel_id=1, source_target_pairs={{0,1},{1,0},{2,3},{3,2},{4,5},{5,4},{6,7},{7,6},{8,9},{9,8},{10,11... | collective-permute-start | bytes 491528 | tf_op jit(solution)/shard_map/ppermute | solution.py:246
  35.0 16.0 %collective-permute-start.11 = (s32[1,64]{1,0:T(1,128)S(1)}, s32[1,64]{1,0:T(1,128)S(1)}, u32[]{:S(2)}, u32[]{:S(2)}) collective-permute-start(s32[1,64]{1,0:T(1,128)S(1)} %bitcast.38), channel_id=1, source_target_pairs={{0,2},{2,0},{1,3},{3,1},{4,6},{6,4},{5,7},{7,5},{8,10},{10,8},{9,1... | collective-permute-start | bytes 776 | tf_op jit(solution)/shard_map/ppermute | solution.py:246
  36.6 31.9 %collective-permute-start.12 = (bf16[64,5120]{1,0:T(8,128)(2,1)S(1)}, bf16[64,5120]{1,0:T(8,128)(2,1)S(1)}, u32[]{:S(2)}, u32[]{:S(2)}) collective-permute-start(bf16[64,5120]{1,0:T(8,128)(2,1)S(1)} %bitcast.29), channel_id=1, source_target_pairs={{0,2},{2,0},{1,3},{3,1},{4,6},{6,4},{5,7},{7,5},{8,10},{10,8},{9,1... | collective-permute-start | bytes 1966088 | tf_op jit(solution)/shard_map/ppermute | solution.py:246
  43.4 25.1 %copy-start.6 = (bf16[10,128,128]{2,1,0:T(8,128)(2,1)}, bf16[10,128,128]{2,1,0:T(8,128)(2,1)S(1)}, u32[]{:S(2)}) copy-start(bf16[10,128,128]{2,1,0:T(8,128)(2,1)S(1)} %collective-permute-done.5.refs_0_) | copy-start | bytes 983044
  46.3 22.2 %copy-start.7 = (bf16[10,128,128]{2,1,0:T(8,128)(2,1)}, bf16[10,128,128]{2,1,0:T(8,128)(2,1)S(1)}, u32[]{:S(2)}) copy-start(bf16[10,128,128]{2,1,0:T(8,128)(2,1)S(1)} %collective-permute-done.6.refs_1_) | copy-start | bytes 983044
  46.3 2.3 %collective-permute-start.13 = (bf16[2,64,1280]{2,1,0:T(8,128)(2,1)}, bf16[2,64,1280]{2,1,0:T(8,128)(2,1)S(1)}, u32[]{:S(2)}, u32[]{:S(2)}) collective-permute-start(bf16[2,64,1280]{2,1,0:T(8,128)(2,1)} %bitcast.39), channel_id=1, source_target_pairs={{0,1},{1,0},{2,3},{3,2},{4,5},{5,4},{6,7},{7,6},{8,9},{9,8},{10,11... | collective-permute-start | bytes 983048 | tf_op jit(solution)/shard_map/ppermute | solution.py:246
  46.4 28.4 %copy-start.3 = (bf16[64,1280]{1,0:T(8,128)(2,1)}, bf16[64,1280]{1,0:T(8,128)(2,1)S(1)}, u32[]{:S(2)}) copy-start(bf16[64,1280]{1,0:T(8,128)(2,1)S(1)} %fusion.refs_1_) | copy-start | bytes 491524
  46.4 12.6 %collective-permute-start.10 = (bf16[64,1280]{1,0:T(8,128)(2,1)S(1)}, bf16[64,1280]{1,0:T(8,128)(2,1)S(1)}, u32[]{:S(2)}, u32[]{:S(2)}) collective-permute-start(bf16[64,1280]{1,0:T(8,128)(2,1)S(1)} %fusion.refs_1_), channel_id=1, source_target_pairs={{0,2},{2,0},{1,3},{3,1},{4,6},{6,4},{5,7},{7,5},{8,10},{10,8},{9,1... | collective-permute-start | bytes 491528 | tf_op jit(solution)/shard_map/ppermute | solution.py:246
  47.9 26.9 %collective-permute-start.7 = (bf16[10,128,128]{2,1,0:T(8,128)(2,1)S(1)}, bf16[10,128,128]{2,1,0:T(8,128)(2,1)S(1)}, u32[]{:S(2)}, u32[]{:S(2)}) collective-permute-start(bf16[10,128,128]{2,1,0:T(8,128)(2,1)S(1)} %collective-permute-done.5.refs_0_), channel_id=1, source_target_pairs={{8,12},{9,13},{10,14},{11,15},{24,28},{25,29},{26,30},{27,31}} | collective-permute-start | bytes 983048 | tf_op jit(solution)/shard_map/ppermute | solution.py:249
  48.6 26.2 %collective-permute-start.8 = (bf16[10,128,128]{2,1,0:T(8,128)(2,1)S(1)}, bf16[10,128,128]{2,1,0:T(8,128)(2,1)S(1)}, u32[]{:S(2)}, u32[]{:S(2)}) collective-permute-start(bf16[10,128,128]{2,1,0:T(8,128)(2,1)S(1)} %collective-permute-done.6.refs_1_), channel_id=1, source_target_pairs={{4,0},{5,1},{6,2},{7,3},{20,16},{21,17},{22,18},{23,19}} | collective-permute-start | bytes 983048 | tf_op jit(solution)/shard_map/ppermute | solution.py:249
  51.1 23.7 %copy-start.23 = (s32[1,64]{1,0:T(1,128)}, s32[1,64]{1,0:T(1,128)S(1)}, u32[]{:S(2)}) copy-start(s32[1,64]{1,0:T(1,128)S(1)} %collective-permute-done.11.refs_7_) | copy-start | bytes 772
  51.1 11.7 %collective-permute-start.16 = (bf16[64,1280]{1,0:T(8,128)(2,1)S(1)}, bf16[64,1280]{1,0:T(8,128)(2,1)S(1)}, u32[]{:S(2)}, u32[]{:S(2)}) collective-permute-start(bf16[64,1280]{1,0:T(8,128)(2,1)S(1)} %get-tuple-element.73), channel_id=1, source_target_pairs={{0,4},{4,8},{8,12},{1,5},{5,9},{9,13},{2,6},{6,10},{10,14},{3,7},{... | collective-permute-start | bytes 491528 | tf_op jit(solution)/shard_map/ppermute | solution.py:249
  59.0 15.8 %copy-start.12 = (bf16[64,1280]{1,0:T(8,128)(2,1)}, bf16[64,1280]{1,0:T(8,128)(2,1)S(1)}, u32[]{:S(2)}) copy-start(bf16[64,1280]{1,0:T(8,128)(2,1)S(1)} %collective-permute-done.10.refs_1_) | copy-start | bytes 491524
  59.0 8.9 %collective-permute-start.14 = (bf16[64,1280]{1,0:T(8,128)(2,1)S(1)}, bf16[64,1280]{1,0:T(8,128)(2,1)S(1)}, u32[]{:S(2)}, u32[]{:S(2)}) collective-permute-start(bf16[64,1280]{1,0:T(8,128)(2,1)S(1)} %get-tuple-element.74), channel_id=1, source_target_pairs={{4,0},{8,4},{12,8},{5,1},{9,5},{13,9},{6,2},{10,6},{14,10},{7,3},{... | collective-permute-start | bytes 491528 | tf_op jit(solution)/shard_map/ppermute | solution.py:249
  62.7 12.2 %collective-permute-start.17 = (bf16[64,1280]{1,0:T(8,128)(2,1)S(1)}, bf16[64,1280]{1,0:T(8,128)(2,1)S(1)}, u32[]{:S(2)}, u32[]{:S(2)}) collective-permute-start(bf16[64,1280]{1,0:T(8,128)(2,1)S(1)} %collective-permute-done.16.refs_3_), channel_id=1, source_target_pairs={{0,2},{2,0},{1,3},{3,1},{4,6},{6,4},{5,7},{7,5},{8,10},{10,8},{9,1... | collective-permute-start | bytes 491528 | tf_op jit(solution)/shard_map/ppermute | solution.py:246
  67.9 7.1 %collective-permute-start.15 = (bf16[64,1280]{1,0:T(8,128)(2,1)S(1)}, bf16[64,1280]{1,0:T(8,128)(2,1)S(1)}, u32[]{:S(2)}, u32[]{:S(2)}) collective-permute-start(bf16[64,1280]{1,0:T(8,128)(2,1)S(1)} %collective-permute-done.14.refs_2_), channel_id=1, source_target_pairs={{0,2},{2,0},{1,3},{3,1},{4,6},{6,4},{5,7},{7,5},{8,10},{10,8},{9,1... | collective-permute-start | bytes 491528 | tf_op jit(solution)/shard_map/ppermute | solution.py:246
  74.9 7.0 %collective-permute-start.18 = (bf16[1,64,1280]{2,1,0:T(8,128)(2,1)}, bf16[1,64,1280]{2,1,0:T(8,128)(2,1)S(1)}, u32[]{:S(2)}, u32[]{:S(2)}) collective-permute-start(bf16[1,64,1280]{2,1,0:T(8,128)(2,1)} %bitcast.41), channel_id=1, source_target_pairs={{0,1},{1,0},{2,3},{3,2},{4,5},{5,4},{6,7},{7,6},{8,9},{9,8},{10,11... | collective-permute-start | bytes 491528 | tf_op jit(solution)/shard_map/ppermute | solution.py:246
  81.8 16.8 %copy-start.21 = (bf16[5120]{0:T(1024)(128)(2,1)S(1)}, bf16[5120]{0:T(1024)(128)(2,1)}, u32[]{:S(2)}) copy-start(bf16[5120]{0:T(1024)(128)(2,1)} %param.16) | copy-start | bytes 30724
  81.8 1.7 %collective-permute-start.21 = (bf16[1,64,1280]{2,1,0:T(8,128)(2,1)}, bf16[1,64,1280]{2,1,0:T(8,128)(2,1)S(1)}, u32[]{:S(2)}, u32[]{:S(2)}) collective-permute-start(bf16[1,64,1280]{2,1,0:T(8,128)(2,1)} %bitcast.42), channel_id=1, source_target_pairs={{0,1},{1,0},{2,3},{3,2},{4,5},{5,4},{6,7},{7,6},{8,9},{9,8},{10,11... | collective-permute-start | bytes 491528 | tf_op jit(solution)/shard_map/ppermute | solution.py:246
  82.0 14.6 %collective-permute-start.19 = (bf16[64,1280]{1,0:T(8,128)(2,1)S(1)}, bf16[64,1280]{1,0:T(8,128)(2,1)S(1)}, u32[]{:S(2)}, u32[]{:S(2)}) collective-permute-start(bf16[64,1280]{1,0:T(8,128)(2,1)S(1)} %fusion.3), channel_id=1, source_target_pairs={{8,0},{12,4},{0,8},{4,12},{9,1},{13,5},{1,9},{5,13},{10,2},{14,6},... | collective-permute-start | bytes 491528 | tf_op jit(solution)/shard_map/ppermute | solution.py:249
  84.5 13.2 %collective-permute-start.22 = (bf16[64,1280]{1,0:T(8,128)(2,1)S(1)}, bf16[64,1280]{1,0:T(8,128)(2,1)S(1)}, u32[]{:S(2)}, u32[]{:S(2)}) collective-permute-start(bf16[64,1280]{1,0:T(8,128)(2,1)S(1)} %fusion.4), channel_id=1, source_target_pairs={{12,0},{0,12},{13,1},{1,13},{14,2},{2,14},{15,3},{3,15},{28,16},{1... | collective-permute-start | bytes 491528 | tf_op jit(solution)/shard_map/ppermute | solution.py:249
  96.5 7.2 %collective-permute-start.20 = (bf16[64,1280]{1,0:T(8,128)(2,1)S(1)}, bf16[64,1280]{1,0:T(8,128)(2,1)S(1)}, u32[]{:S(2)}, u32[]{:S(2)}) collective-permute-start(bf16[64,1280]{1,0:T(8,128)(2,1)S(1)} %collective-permute-done.19.refs_4_), channel_id=1, source_target_pairs={{0,2},{2,0},{1,3},{3,1},{4,6},{6,4},{5,7},{7,5},{8,10},{10,8},{9,1... | collective-permute-start | bytes 491528 | tf_op jit(solution)/shard_map/ppermute | solution.py:246
  97.7 8.2 %collective-permute-start.23 = (bf16[64,1280]{1,0:T(8,128)(2,1)S(1)}, bf16[64,1280]{1,0:T(8,128)(2,1)S(1)}, u32[]{:S(2)}, u32[]{:S(2)}) collective-permute-start(bf16[64,1280]{1,0:T(8,128)(2,1)S(1)} %collective-permute-done.22.refs_5_), channel_id=1, source_target_pairs={{0,2},{2,0},{1,3},{3,1},{4,6},{6,4},{5,7},{7,5},{8,10},{10,8},{9,1... | collective-permute-start | bytes 491528 | tf_op jit(solution)/shard_map/ppermute | solution.py:246
  (18 other events, 83.2 us)

commit v4 on v2

v4 whole, which is shorter than its diff:
```python
import functools
import math

import jax
import jax.numpy as jnp
from jax import lax
from jax.experimental import pallas as pl
from jax.experimental.pallas import tpu as pltpu
from jax.sharding import PartitionSpec as P

CAP = 2
EPSILON = 1e-05
DOC_ROWS = 16
VMEM_LIMIT = 16 * 1024 * 1024
VMEM_MOST = 56 * 1024 * 1024


def fetch(refs, buffers, sems):
    copies = [
        pltpu.make_async_copy(ref, buffer, sems.at[number])
        for number, (ref, buffer) in enumerate(zip(refs, buffers))
    ]
    for copy in copies:
        copy.start()
    return [copy.wait for copy in copies]


def pack_kernel(groups, key_ref, value_ref, doc_ref, out_ref, *scratch):
    buffers, sems = scratch[:-1], scratch[-1]
    for wait in fetch((key_ref, value_ref, doc_ref), buffers, sems):
        wait()
    key_ref, value_ref, doc_ref = buffers
    rows, head_size = key_ref.shape
    tokens = rows // groups
    token = lax.broadcasted_iota(jnp.int32, (tokens, rows), 0)
    row = lax.broadcasted_iota(jnp.int32, (tokens, rows), 1)
    for group in range(groups):
        pick = (row == token * groups + group).astype(jnp.bfloat16)
        for place, ref in enumerate((key_ref, value_ref)):
            first = (place * groups + group) * tokens
            out_ref[first : first + tokens, :] = jnp.dot(
                pick, ref[...], preferred_element_type=jnp.float32
            ).astype(jnp.bfloat16)
    out_ref[2 * rows :, :] = jnp.broadcast_to(
        (doc_ref[...] + 1).astype(jnp.float32), (DOC_ROWS, tokens)
    ).astype(jnp.bfloat16)


def stage_kernel(in_ref, out_ref, sem):
    copy = pltpu.make_async_copy(in_ref, out_ref, sem)
    copy.start()
    copy.wait()


def attention_kernel(ratio, groups, pair, place_ref, query_ref, *refs):
    pack_refs, out_refs = refs[:-pair], refs[-pair:]
    heads, tokens, head_size = query_ref.shape
    scale = 1.0 / math.sqrt(head_size)
    core = place_ref[0]
    part_rows = tokens // pair
    held_rows = groups * tokens
    rows = lax.broadcasted_iota(jnp.int32, (tokens, tokens), 0)
    columns = lax.broadcasted_iota(jnp.int32, (tokens, tokens), 1)
    docs = [ref[2 * held_rows : 2 * held_rows + 1, :].astype(jnp.float32) for ref in pack_refs]
    own_doc = jnp.sum(jnp.where(rows == columns, docs[0], 0.0), axis=1, keepdims=True)
    allowed = [(own_doc == docs[0]) & (columns <= rows)] + [own_doc == doc for doc in docs[1:]]
    allowed = jnp.concatenate(allowed, axis=1)
    for group in range(groups):
        first = group * tokens
        keys = jnp.concatenate([ref[first : first + tokens, :] for ref in pack_refs], axis=0)
        first = held_rows + group * tokens
        held = jnp.concatenate([ref[first : first + tokens, :] for ref in pack_refs], axis=0)
        for head in range(group * ratio, (group + 1) * ratio):
            scores = lax.dot_general(
                query_ref[head], keys, (((1,), (1,)), ((), ())), preferred_element_type=jnp.float32
            )
            scores = jnp.where(allowed, scores * scale, -1e30)
            weights = jnp.exp(scores - jnp.max(scores, axis=1, keepdims=True))
            totals = jnp.sum(weights, axis=1, keepdims=True)
            mixed = jnp.dot(
                weights.astype(jnp.bfloat16), held, preferred_element_type=jnp.float32
            )
            mixed = (mixed / totals).astype(jnp.bfloat16)
            parts = [mixed[i * part_rows : (i + 1) * part_rows] for i in range(pair)]
            for turn in range(pair):
                piece = parts[turn]
                for own in range(1, pair):
                    piece = jnp.where(core == own, parts[(own + turn) % pair], piece)
                out_refs[turn][:, head * head_size : (head + 1) * head_size] = piece


def project_kernel(pair, block_ref, *refs):
    weight_refs, out_ref = refs[:pair], refs[pair]
    depth = weight_refs[0].shape[0]
    total = jnp.zeros(out_ref.shape, jnp.float32)
    for turn in range(pair):
        total = total + jnp.dot(
            block_ref[:, turn * depth : (turn + 1) * depth],
            weight_refs[turn][...],
            preferred_element_type=jnp.float32,
        )
    out_ref[...] = total.astype(out_ref.dtype)


def add_chunks(out_ref, base, chunk_refs, steps, spots, ctx_index):
    for step, chunk_ref in zip(steps, chunk_refs):
        columns = chunk_ref.shape[1]
        first = 0 if spots == 1 else lax.rem(ctx_index + step, spots) * columns
        part = pl.ds(pl.multiple_of(first, 128), columns)
        out_ref[:, part] = base[:, part].astype(jnp.float32) + chunk_ref[...].astype(jnp.float32)


def collect_kernel(steps, spots, exp_count, place_ref, *refs):
    count = len(steps)
    residual_refs, chunk_refs = refs[:exp_count], refs[exp_count:-exp_count]
    for back, out_ref in enumerate(refs[-exp_count:]):
        out_ref[...] = residual_refs[back][...].astype(jnp.float32)
        add_chunks(
            out_ref,
            residual_refs[back],
            chunk_refs[back * count : (back + 1) * count],
            steps,
            spots,
            place_ref[0],
        )


def finish_kernel(steps, spots, back, exp_count, place_ref, *refs):
    chunk_refs = refs[: len(steps)]
    hidden_ref, id_ref, keep_ref, gain_ref, router_ref = refs[len(steps) :][:5]
    kept_refs = refs[len(steps) + 5 : -3]
    out_ref, total_ref, normed_ref = refs[-3:]
    rows, width = hidden_ref.shape
    experts = keep_ref.shape[1]
    here = router_ref.shape[0]
    ctx_index, exp_index = place_ref[0], place_ref[1]
    keep = keep_ref[...].astype(jnp.float32)
    upper = (
        lax.broadcasted_iota(jnp.int32, (rows, rows), 0)
        < lax.broadcasted_iota(jnp.int32, (rows, rows), 1)
    ).astype(jnp.bfloat16)
    total_ref[...] = hidden_ref[...]
    add_chunks(total_ref, hidden_ref, chunk_refs, steps, spots, ctx_index)
    hidden = total_ref[...]
    power = jnp.sum(hidden * hidden, axis=1, keepdims=True)
    factor = lax.rsqrt(power / width + EPSILON)
    normed_ref[...] = (hidden * factor * gain_ref[...].astype(jnp.float32)).astype(jnp.bfloat16)
    ids = id_ref[...]
    onehot = (ids == lax.broadcasted_iota(jnp.int32, (experts, rows), 0)).astype(jnp.float32)
    earlier = jnp.dot(onehot.astype(jnp.bfloat16), upper, preferred_element_type=jnp.float32)
    ranking = jnp.sum(onehot * earlier, axis=0, keepdims=True)
    limits = jnp.dot(
        keep.astype(jnp.bfloat16),
        onehot.astype(jnp.bfloat16),
        preferred_element_type=jnp.float32,
    )
    local = ids - exp_index * here
    logits = lax.dot_general(
        router_ref[...],
        normed_ref[...],
        (((1,), (1,)), ((), ())),
        preferred_element_type=jnp.float32,
    )
    chosen = local == lax.broadcasted_iota(jnp.int32, (here, rows), 0)
    gates = jax.nn.sigmoid(jnp.sum(jnp.where(chosen, logits, 0.0), axis=0, keepdims=True))
    target = local * CAP + ranking.astype(jnp.int32)
    target = jnp.where((ranking < limits) & (local >= 0) & (local < here), target, -1)
    table = lax.broadcasted_iota(jnp.int32, (here * CAP, rows), 0) == target
    slot_gates = jnp.sum(jnp.where(table, gates, 0.0), axis=1, keepdims=True)
    slots = jnp.dot(
        table.astype(jnp.bfloat16), normed_ref[...], preferred_element_type=jnp.float32
    )
    result = (slots * slot_gates).astype(jnp.bfloat16)
    if back < exp_count - 1:
        out_ref[...] = result
        return
    for number, ref in enumerate(kept_refs):
        out_ref[lax.rem(exp_index - number + exp_count, exp_count)] = ref[...]
    out_ref[lax.rem(exp_index - back + exp_count, exp_count)] = result


def on_device(
    queries,
    key_states,
    values,
    doc_ids,
    residual,
    out_proj,
    norm_gain,
    router,
    expert_ids,
    keep_counts,
):
    _, tokens, heads, head_size = queries.shape
    groups = key_states.shape[2]
    ctx_count = lax.axis_size("ctx")
    pair = lax.axis_size("tp")
    exp_count = lax.axis_size("exp")
    part_rows = tokens // pair
    width = residual.shape[2]
    columns = out_proj.shape[1]
    experts_here = router.shape[1]
    ctx_index = lax.axis_index("ctx")
    core = lax.axis_index("tp")
    exp_index = lax.axis_index("exp")
    reach = -(-(ctx_count * tokens // 2 - 1) // tokens)
    vmem = pl.BlockSpec(memory_space=pltpu.VMEM)
    smem = pl.BlockSpec(memory_space=pltpu.SMEM)
    anywhere = pl.BlockSpec(memory_space=pl.ANY)
    params = pltpu.CompilerParams(vmem_limit_bytes=VMEM_LIMIT)
    bf16, f32 = jnp.bfloat16, jnp.float32

    def over(array, axis, step):
        count = lax.axis_size(axis)
        if step % count == 0:
            return array
        return lax.ppermute(array, axis, [(i, (i + step) % count) for i in range(count)])

    def along(array, moves):
        return lax.ppermute(array, "ctx", moves)

    pack = pl.pallas_call(
        functools.partial(pack_kernel, groups),
        out_shape=jax.ShapeDtypeStruct((2 * groups * tokens + DOC_ROWS, head_size), bf16),
        in_specs=[anywhere] * 3,
        out_specs=vmem,
        scratch_shapes=[pltpu.VMEM((groups * tokens, head_size), bf16)] * 2
        + [pltpu.VMEM(doc_ids.shape, doc_ids.dtype), pltpu.SemaphoreType.DMA((3,))],
        compiler_params=pltpu.CompilerParams(vmem_limit_bytes=VMEM_MOST),
    )(
        key_states.reshape(groups * tokens, head_size),
        values.reshape(groups * tokens, head_size),
        doc_ids,
    )
    packs = [pack] + [
        lax.ppermute(pack, "ctx", [(i, i + step) for i in range(ctx_count - step)])
        for step in range(1, reach + 1)
    ]
    own_weights, own_queries, pack = lax.optimization_barrier(
        (out_proj, queries[0].transpose(1, 0, 2), pack)
    )
    packs[0] = pack
    weights = [out_proj] + [over(own_weights, "tp", turn) for turn in range(1, pair)]
    staged = pl.pallas_call(
        stage_kernel,
        out_shape=jax.ShapeDtypeStruct(own_queries.shape, bf16),
        in_specs=[anywhere],
        out_specs=vmem,
        scratch_shapes=[pltpu.SemaphoreType.DMA],
        compiler_params=params,
    )(own_queries)
    pieces = pl.pallas_call(
        functools.partial(attention_kernel, heads // groups, groups, pair),
        out_shape=[jax.ShapeDtypeStruct((part_rows, heads * head_size), bf16)] * pair,
        in_specs=[smem] + [vmem] * (1 + len(packs)),
        out_specs=[vmem] * pair,
        compiler_params=params,
    )(core.reshape(1), staged, *packs)

    project = pl.pallas_call(
        functools.partial(project_kernel, pair),
        out_shape=jax.ShapeDtypeStruct((part_rows, columns), bf16),
        in_specs=[vmem] * (1 + pair),
        out_specs=vmem,
        compiler_params=params,
        cost_estimate=pl.CostEstimate(
            flops=2 * pair * part_rows * out_proj.size,
            bytes_accessed=2 * pair * out_proj.size,
            transcendentals=0,
        ),
    )
    block = jnp.concatenate([over(pieces[turn], "tp", turn) for turn in range(pair)], axis=1)
    ids, own_residual = expert_ids[:, :, 0], residual[0]
    block, early_ids, early_residual = lax.optimization_barrier((block, ids, own_residual))
    all_ids = [ids] + [over(early_ids, "exp", back) for back in range(1, exp_count)]
    all_residual = [own_residual] + [
        over(early_residual, "exp", back) for back in range(1, exp_count)
    ]

    aligned = columns % 128 == 0
    hidden = None

    def forward(chunk):
        return [over(chunk, "exp", back) for back in range(1, exp_count if aligned else 1)]

    def collect(arrays, steps, spots):
        return pl.pallas_call(
            functools.partial(collect_kernel, steps, spots, exp_count),
            out_shape=[jax.ShapeDtypeStruct((part_rows, width), f32)] * exp_count,
            in_specs=[smem] + [vmem] * (exp_count + len(arrays)),
            out_specs=[vmem] * exp_count,
            compiler_params=params,
        )(ctx_index.reshape(1), *all_residual, *arrays)

    flat = []
    for step in range(ctx_count):
        last = step == ctx_count - 1
        following = None if last else over(block, "ctx", 1)
        if step >= 2 and aligned:
            block, flat[step - 2] = lax.optimization_barrier((block, flat[step - 2]))
        if step == 2:
            block, flat[1][0] = lax.optimization_barrier((block, flat[1][0]))
        total = project(block, *weights)
        chunk = over(total, "ctx", ctx_count - step)
        if not last:
            block, _ = lax.optimization_barrier((following, total))
        if last and aligned:
            steps = list(range(step))
            hidden = collect(
                [flat[number][back] for back in range(exp_count) for number in steps],
                steps,
                ctx_count,
            )
            chunk, hidden, all_ids = lax.optimization_barrier((chunk, hidden, all_ids))
        flat.append([chunk] + forward(chunk))
    if aligned:
        late_steps, late, spots = [ctx_count - 1], [flat[-1]], ctx_count
    else:
        whole = jnp.roll(jnp.stack([arrays[0] for arrays in flat]), ctx_index, axis=0)
        whole = whole.transpose(1, 0, 2).reshape(part_rows, width)
        hidden = collect([over(whole, "exp", back) for back in range(exp_count)], [0], 1)
        late_steps, late, spots = [], [], 1
    places = jnp.stack([ctx_index, exp_index])
    results = []
    for back in range(exp_count):
        operands = (
            [places]
            + [arrays[back] for arrays in late]
            + [hidden[back], all_ids[back], keep_counts.reshape(1, -1)]
            + [norm_gain.reshape(1, -1), router.T]
        )
        shape = (experts_here * CAP, width)
        if back == exp_count - 1:
            operands += results
            shape = (exp_count,) + shape
        out = pl.pallas_call(
            functools.partial(finish_kernel, late_steps, spots, back, exp_count),
            out_shape=jax.ShapeDtypeStruct(shape, bf16),
            in_specs=[smem] + [vmem] * (len(operands) - 1),
            out_specs=vmem,
            scratch_shapes=[
                pltpu.VMEM((part_rows, width), f32),
                pltpu.VMEM((part_rows, width), bf16),
            ],
            compiler_params=params,
        )(*operands)
        results.append(out)
    return out.reshape(exp_count, experts_here, CAP, width)


def solution(mesh):
    placed = (
        P(("groups", "exp"), "ctx", "tp", None),
        P(("groups", "exp"), "ctx", "tp", None),
        P(("groups", "exp"), "ctx", "tp", None),
        P(("groups", "exp"), "ctx"),
        P(("groups", "exp"), ("ctx", "tp"), None),
        P("tp", "ctx"),
        P(),
        P(None, "exp"),
        P(("groups", "exp"), ("ctx", "tp"), None),
        P("groups"),
    )
    return jax.shard_map(
        on_device,
        mesh=mesh,
        in_specs=placed,
        out_specs=P(("groups", "ctx", "tp"), "exp", None, None),
        check_vma=False,
    )
```

time: 91.6 us -> 83.9 us (0.916)
  waiting for transfers between devices: 50.7 us -> 35.4 us
  starting transfers between devices: 19.8 us -> 25 us
  Pallas kernels: 11.6 us -> 14.9 us
  other arithmetic: 1.69 us -> 0.1 us
    ppermute x16 -> x14, waiting for transfers between devices: 50.7 us -> 32.9 us  [over(): lax.ppermute(array, axis, [(i, (i + step) % count) for i in range(count)])]
    ppermute x0 -> x2, starting transfers between devices: none -> 9 us  [on_device(): lax.ppermute(pack, 'ctx', [(i, i + step) for i in range(ctx_count - step)])]
    pallas_call x1 -> x5, Pallas kernels: 2.61 us -> 6.56 us  [the longest x2 3 us: on_device(): pl.pallas_call(functools.partial(finish_kernel, late_steps, spots, back,...]
    ppermute x16 -> x14, starting transfers between devices: 19.8 us -> 16 us  [over(): lax.ppermute(array, axis, [(i, (i + step) % count) for i in range(count)])]
    ppermute x0 -> x2, waiting for transfers between devices: none -> 2.44 us  [on_device(): lax.ppermute(pack, 'ctx', [(i, i + step) for i in range(ctx_count - step)])]
    pallas_call x1, Pallas kernels: 4 us -> 2.73 us  [on_device(): pl.pallas_call(functools.partial(attention_kernel, heads // groups, group...]
    unnamed x27 -> x28, local copies, waits for them, and re-layouts: 5.82 us -> 6.58 us
  transfers between devices with their start and end apart: 16 -> 16, of which waited for: 10 -> 9; matrix products, arithmetic and copies ran while one was open for 2% -> 0% of each run, Pallas kernels for 4% -> 14%
where the time goes in v4:
time: 83.9 us; the launch traced here: 83.5 us
  waiting for transfers between devices  35.4 us (42%)
  starting transfers between devices  25 us (30%)
  Pallas kernels  14.9 us (18%)
  local copies, waits for them, and re-layouts  7.96 us (9%)
    ppermute x14, waiting for transfers between devices, over(): lax.ppermute(array, axis, [(i, (i + step) % count) for i in range(count)])  32.9 us
    ppermute x14, starting transfers between devices, over(): lax.ppermute(array, axis, [(i, (i + step) % count) for i in range(count)])  16 us
    ppermute x2, starting transfers between devices, on_device(): lax.ppermute(pack, 'ctx', [(i, i + step) for i in range(ctx_count - step)])  9 us
    unnamed x28, local copies, waits for them, and re-layouts  6.58 us
    pallas_call x4, Pallas kernels, on_device(): total = project(block, *weights)  5.63 us
    pallas_call x2, Pallas kernels, on_device(): pl.pallas_call(functools.partial(finish_kernel, late_steps, spots, back,...  3 us
    pallas_call x1, Pallas kernels, on_device(): pl.pallas_call(functools.partial(attention_kernel, heads // groups, group...  2.73 us
    ppermute x2, waiting for transfers between devices, on_device(): lax.ppermute(pack, 'ctx', [(i, i + step) for i in range(ctx_count - step)])  2.44 us
  transfers between devices with their start and end apart: 16, of which 9 were waited for; matrix products, arithmetic and copies ran while one was open for 0% of the time, Pallas kernels for 14%

profile of v4, /device:TPU:0, one launch (start us, length us, event | category | flops | bytes accessed | tf_op | source)
XLA Modules:
  0.0 83.5 jit_solution(18003719062661692514)
XLA Ops:
  0.0 1.8 %shard_map.100.refs_0_ = bf16[528,128]{1,0:T(8,128)(2,1)} custom-call(bf16[256,128]{1,0:T(8,128)(2,1)} %bitcast.19, bf16[256,128]{1,0:T(8,128)(2,1)} %bitcast.20, s32[1,128]{1,0:T(1,128)} %doc_ref.1), custom_call_target="tpu_custom_call" | custom-call | tf_op jit(solution)/shard_map/pallas_call | solution.py:222
  2.3 4.5 %collective-permute-start = (bf16[528,128]{1,0:T(8,128)(2,1)}, bf16[528,128]{1,0:T(8,128)(2,1)S(1)}, u32[]{:S(2)}, u32[]{:S(2)}) collective-permute-start(bf16[528,128]{1,0:T(8,128)(2,1)} %shard_map.100.refs_0_), channel_id=1, source_target_pairs={{0,4},{4,8},{8,12},{1,5},{5,9},{9,13},{2,6},{6,10},{10,14},{3,7},{... | collective-permute-start | bytes 405512 | tf_op jit(solution)/shard_map/ppermute | solution.py:236
  6.8 4.5 %collective-permute-start.1 = (bf16[528,128]{1,0:T(8,128)(2,1)}, bf16[528,128]{1,0:T(8,128)(2,1)S(1)}, u32[]{:S(2)}, u32[]{:S(2)}) collective-permute-start(bf16[528,128]{1,0:T(8,128)(2,1)} %shard_map.100.refs_0_), channel_id=1, source_target_pairs={{0,8},{4,12},{1,9},{5,13},{2,10},{6,14},{3,11},{7,15},{16,24},{20,... | collective-permute-start | bytes 405512 | tf_op jit(solution)/shard_map/ppermute | solution.py:236
  11.3 1.0 %copy-done.4 = bf16[1,128,10,128]{3,1,2,0:T(8,128)(2,1)S(1)} copy-done((bf16[1,128,10,128]{3,1,2,0:T(8,128)(2,1)S(1)}, bf16[1,128,10,128]{3,1,2,0:T(8,128)(2,1)}, u32[]{:S(2)}) %copy-start.4) | copy-done | bytes 327704
  12.4 2.4 %collective-permute-done.1.refs_2_ = bf16[528,128]{1,0:T(8,128)(2,1)S(1)} collective-permute-done((bf16[528,128]{1,0:T(8,128)(2,1)}, bf16[528,128]{1,0:T(8,128)(2,1)S(1)}, u32[]{:S(2)}, u32[]{:S(2)}) %collective-permute-start.1) | collective-permute-done | bytes 135200 | tf_op jit(solution)/shard_map/ppermute | solution.py:236
  15.8 2.7 %shard_map.102 = (bf16[64,1280]{1,0:T(8,128)(2,1)S(1)}, bf16[64,1280]{1,0:T(8,128)(2,1)S(1)}) custom-call(s32[1]{0:T(128)} %bitcast.2.place_ref, bf16[10,128,128]{2,1,0:T(8,128)(2,1)S(1)} %shard_map.101.query_ref, bf16[528,128]{1,0:T(8,128)(2,1)S(1)} %copy-done.3, bf16[528,128]{1,0:T(8,128)(2,1)S(1)} %collective-permute-done.refs_1_, ...), custom_call_target="tpu_custom_call" | custom-call | tf_op jit(solution)/shard_map/pallas_call | solution.py:252
  18.6 1.4 %collective-permute-done.2 = bf16[64,1280]{1,0:T(8,128)(2,1)S(1)} collective-permute-done((bf16[64,1280]{1,0:T(8,128)(2,1)S(1)}, bf16[64,1280]{1,0:T(8,128)(2,1)S(1)}, u32[]{:S(2)}, u32[]{:S(2)}) %collective-permute-start.2) | collective-permute-done | bytes 163872 | tf_op jit(solution)/shard_map/ppermute | solution.py:217
  20.0 3.1 %collective-permute-start.3 = (bf16[64,2560]{1,0:T(8,128)(2,1)S(1)}, bf16[64,2560]{1,0:T(8,128)(2,1)S(1)}, u32[]{:S(2)}, u32[]{:S(2)}) collective-permute-start(bf16[64,2560]{1,0:T(8,128)(2,1)S(1)} %pad_maximum_fusion.block_ref), channel_id=1, source_target_pairs={{0,4},{4,8},{8,12},{12,0},{1,5},{5,9},{9,13},{13,1},{2,6},{6,10},{... | collective-permute-start | bytes 983048 | tf_op jit(solution)/shard_map/ppermute | solution.py:217
  23.1 1.9 %copy-done = bf16[1280,1280]{1,0:T(8,128)(2,1)S(1)} copy-done((bf16[1280,1280]{1,0:T(8,128)(2,1)S(1)}, bf16[1280,1280]{1,0:T(8,128)(2,1)}, u32[]{:S(2)}) %copy-start) | copy-done | bytes 3276824
  25.1 1.2 %shard_map.103.refs_2_ = bf16[64,1280]{1,0:T(8,128)(2,1)S(1)} custom-call(bf16[64,2560]{1,0:T(8,128)(2,1)S(1)} %pad_maximum_fusion.block_ref, bf16[1280,1280]{1,0:T(8,128)(2,1)S(1)} %copy-done, bf16[1280,1280]{1,0:T(8,128)(2,1)S(1)} %collective-permute-done.4.refs_1_), custom_call_target="tpu_custom_call" | custom-call | flops 419430400 | bytes 6553600 | tf_op jit(solution)/shard_map/pallas_call | solution.py:303
  26.3 7.6 %collective-permute-done.3.block_ref = bf16[64,2560]{1,0:T(8,128)(2,1)S(1)} collective-permute-done((bf16[64,2560]{1,0:T(8,128)(2,1)S(1)}, bf16[64,2560]{1,0:T(8,128)(2,1)S(1)}, u32[]{:S(2)}, u32[]{:S(2)}) %collective-permute-start.3) | collective-permute-done | bytes 327712 | tf_op jit(solution)/shard_map/ppermute | solution.py:217
  33.9 1.5 %collective-permute-start.11 = (bf16[64,5120]{1,0:T(8,128)(2,1)}, bf16[64,5120]{1,0:T(8,128)(2,1)}, u32[]{:S(2)}, u32[]{:S(2)}) collective-permute-start(bf16[64,5120]{1,0:T(8,128)(2,1)} %bitcast.8.refs_0_), channel_id=1, source_target_pairs={{0,2},{2,0},{1,3},{3,1},{4,6},{6,4},{5,7},{7,5},{8,10},{10,8},{9,1... | collective-permute-start | bytes 1966088 | tf_op jit(solution)/shard_map/ppermute | solution.py:217
  35.9 1.2 %shard_map.104 = bf16[64,1280]{1,0:T(8,128)(2,1)S(1)} custom-call(bf16[64,2560]{1,0:T(8,128)(2,1)S(1)} %collective-permute-done.3.block_ref, bf16[1280,1280]{1,0:T(8,128)(2,1)S(1)} %copy-done, bf16[1280,1280]{1,0:T(8,128)(2,1)S(1)} %collective-permute-done.4.refs_1_), custom_call_target="tpu_custom_call" | custom-call | flops 419430400 | bytes 6553600 | tf_op jit(solution)/shard_map/pallas_call | solution.py:303
  37.1 3.9 %collective-permute-start.8 = (bf16[64,1280]{1,0:T(8,128)(2,1)S(1)}, bf16[64,1280]{1,0:T(8,128)(2,1)S(1)}, u32[]{:S(2)}, u32[]{:S(2)}) collective-permute-start(bf16[64,1280]{1,0:T(8,128)(2,1)S(1)} %shard_map.104), channel_id=1, source_target_pairs={{0,12},{4,0},{8,4},{12,8},{1,13},{5,1},{9,5},{13,9},{2,14},{6,2},{... | collective-permute-start | bytes 491528 | tf_op jit(solution)/shard_map/ppermute | solution.py:217
  41.0 5.3 %collective-permute-done.5.block_ref = bf16[64,2560]{1,0:T(8,128)(2,1)S(1)} collective-permute-done((bf16[64,2560]{1,0:T(8,128)(2,1)S(1)}, bf16[64,2560]{1,0:T(8,128)(2,1)S(1)}, u32[]{:S(2)}, u32[]{:S(2)}) %collective-permute-start.5) | collective-permute-done | bytes 327712 | tf_op jit(solution)/shard_map/ppermute | solution.py:217
  46.3 7.5 %collective-permute-done.7.refs_5_ = bf16[64,1280]{1,0:T(8,128)(2,1)S(1)} collective-permute-done((bf16[64,1280]{1,0:T(8,128)(2,1)S(1)}, bf16[64,1280]{1,0:T(8,128)(2,1)S(1)}, u32[]{:S(2)}, u32[]{:S(2)}) %collective-permute-start.7) | collective-permute-done | bytes 163872 | tf_op jit(solution)/shard_map/ppermute | solution.py:217
  53.9 1.2 %shard_map.105 = bf16[64,1280]{1,0:T(8,128)(2,1)S(1)} custom-call(bf16[64,2560]{1,0:T(8,128)(2,1)S(1)} %collective-permute-done.5.block_ref, bf16[1280,1280]{1,0:T(8,128)(2,1)S(1)} %copy-done, bf16[1280,1280]{1,0:T(8,128)(2,1)S(1)} %collective-permute-done.4.refs_1_), custom_call_target="tpu_custom_call" | custom-call | flops 419430400 | bytes 6553600 | tf_op jit(solution)/shard_map/pallas_call | solution.py:303
  55.1 1.8 %collective-permute-start.12 = (bf16[64,1280]{1,0:T(8,128)(2,1)S(1)}, bf16[64,1280]{1,0:T(8,128)(2,1)}, u32[]{:S(2)}, u32[]{:S(2)}) collective-permute-start(bf16[64,1280]{1,0:T(8,128)(2,1)S(1)} %shard_map.105), channel_id=1, source_target_pairs={{0,8},{4,12},{8,0},{12,4},{1,9},{5,13},{9,1},{13,5},{2,10},{6,14},... | collective-permute-start | bytes 491528 | tf_op jit(solution)/shard_map/ppermute | solution.py:217
  56.9 1.5 %collective-permute-start.9 = (bf16[64,1280]{1,0:T(8,128)(2,1)S(1)}, bf16[64,1280]{1,0:T(8,128)(2,1)S(1)}, u32[]{:S(2)}, u32[]{:S(2)}) collective-permute-start(bf16[64,1280]{1,0:T(8,128)(2,1)S(1)} %collective-permute-done.8.refs_3_), channel_id=1, source_target_pairs={{0,2},{2,0},{1,3},{3,1},{4,6},{6,4},{5,7},{7,5},{8,10},{10,8},{9,1... | collective-permute-start | bytes 491528 | tf_op jit(solution)/shard_map/ppermute | solution.py:217
  58.4 6.2 %collective-permute-done.12.refs_4_ = bf16[64,1280]{1,0:T(8,128)(2,1)} collective-permute-done((bf16[64,1280]{1,0:T(8,128)(2,1)S(1)}, bf16[64,1280]{1,0:T(8,128)(2,1)}, u32[]{:S(2)}, u32[]{:S(2)}) %collective-permute-start.12) | collective-permute-done | bytes 163872 | tf_op jit(solution)/shard_map/ppermute | solution.py:217
  64.6 1.5 %collective-permute-start.13 = (bf16[64,1280]{1,0:T(8,128)(2,1)}, bf16[64,1280]{1,0:T(8,128)(2,1)}, u32[]{:S(2)}, u32[]{:S(2)}) collective-permute-start(bf16[64,1280]{1,0:T(8,128)(2,1)} %collective-permute-done.12.refs_4_), channel_id=1, source_target_pairs={{0,2},{2,0},{1,3},{3,1},{4,6},{6,4},{5,7},{7,5},{8,10},{10,8},{9,1... | collective-permute-start | bytes 491528 | tf_op jit(solution)/shard_map/ppermute | solution.py:217
  66.1 1.9 %shard_map.106 = bf16[64,1280]{1,0:T(8,128)(2,1)} custom-call(bf16[64,2560]{1,0:T(8,128)(2,1)S(1)} %collective-permute-done.6.block_ref, bf16[1280,1280]{1,0:T(8,128)(2,1)S(1)} %copy-done.1, bf16[1280,1280]{1,0:T(8,128)(2,1)S(1)} %collective-permute-done.4.refs_1_), custom_call_target="tpu_custom_call" | custom-call | flops 419430400 | bytes 6553600 | tf_op jit(solution)/shard_map/pallas_call | solution.py:303
  68.6 1.7 %collective-permute-done.13.refs_7_ = bf16[64,1280]{1,0:T(8,128)(2,1)} collective-permute-done((bf16[64,1280]{1,0:T(8,128)(2,1)}, bf16[64,1280]{1,0:T(8,128)(2,1)}, u32[]{:S(2)}, u32[]{:S(2)}) %collective-permute-start.13) | collective-permute-done | bytes 163872 | tf_op jit(solution)/shard_map/ppermute | solution.py:217
  70.3 0.9 %copy-done.6 = bf16[64,1280]{1,0:T(8,128)(2,1)S(1)} copy-done((bf16[64,1280]{1,0:T(8,128)(2,1)S(1)}, bf16[64,1280]{1,0:T(8,128)(2,1)}, u32[]{:S(2)}) %copy-start.6) | copy-done | bytes 163864
  71.3 0.9 %copy-done.8 = bf16[64,1280]{1,0:T(8,128)(2,1)S(1)} copy-done((bf16[64,1280]{1,0:T(8,128)(2,1)S(1)}, bf16[64,1280]{1,0:T(8,128)(2,1)}, u32[]{:S(2)}) %copy-start.8) | copy-done | bytes 163864
  72.2 0.9 %copy-done.10 = bf16[64,1280]{1,0:T(8,128)(2,1)S(1)} copy-done((bf16[64,1280]{1,0:T(8,128)(2,1)S(1)}, bf16[64,1280]{1,0:T(8,128)(2,1)}, u32[]{:S(2)}) %copy-start.10) | copy-done | bytes 163864
  73.1 1.7 %shard_map.107 = (f32[64,5120]{1,0:T(8,128)S(1)}, f32[64,5120]{1,0:T(8,128)S(1)}) custom-call(s32[1]{0:T(128)} %bitcast.place_ref, bf16[64,5120]{1,0:T(8,128)(2,1)} %bitcast.8.refs_0_, bf16[64,5120]{1,0:T(8,128)(2,1)} %collective-permute-done.11.refs_1_, bf16[64,1280]{1,0:T(8,128)(2,1)S(1)} %shard_map.103.refs_2_, bf16[64,1280]{1,0:T(8,128)(2,1)S(1)} %copy-done.8, ...), custom_call_target="tpu_custom_call" | custom-call | tf_op jit(solution)/shard_map/pallas_call | solution.py:287
  75.4 1.0 %collective-permute-start.15 = (bf16[64,1280]{1,0:T(8,128)(2,1)S(1)}, bf16[64,1280]{1,0:T(8,128)(2,1)S(1)}, u32[]{:S(2)}, u32[]{:S(2)}) collective-permute-start(bf16[64,1280]{1,0:T(8,128)(2,1)S(1)} %collective-permute-done.10.refs_0_), channel_id=1, source_target_pairs={{0,2},{2,0},{1,3},{3,1},{4,6},{6,4},{5,7},{7,5},{8,10},{10,8},{9,1... | collective-permute-start | bytes 491528 | tf_op jit(solution)/shard_map/ppermute | solution.py:217
  76.5 1.5 %shard_map.108.refs_6_ = bf16[64,5120]{1,0:T(8,128)(2,1)S(1)} custom-call(s32[2]{0:T(128)S(1)} %pad_add_fusion.place_ref, bf16[64,1280]{1,0:T(8,128)(2,1)S(1)} %collective-permute-done.10.refs_0_, f32[64,5120]{1,0:T(8,128)S(1)} %get-tuple-element.55.refs_1_, s32[1,64]{1,0:T(1,128)S(1)} %bitcast.18, s32[1,64]{1,0:T(1,128)S(1)} %bitcast.15, ...), custom_call_target="tpu_custom_call" | custom-call | tf_op jit(solution)/shard_map/pallas_call | solution.py:336
  78.0 2.7 %collective-permute-done.15.refs_0_ = bf16[64,1280]{1,0:T(8,128)(2,1)S(1)} collective-permute-done((bf16[64,1280]{1,0:T(8,128)(2,1)S(1)}, bf16[64,1280]{1,0:T(8,128)(2,1)S(1)}, u32[]{:S(2)}, u32[]{:S(2)}) %collective-permute-start.15) | collective-permute-done | bytes 163872 | tf_op jit(solution)/shard_map/ppermute | solution.py:217
  80.7 1.5 %shard_map.109 = bf16[2,64,5120]{2,1,0:T(8,128)(2,1)S(1)} custom-call(s32[2]{0:T(128)S(1)} %pad_add_fusion.place_ref, bf16[64,1280]{1,0:T(8,128)(2,1)S(1)} %collective-permute-done.15.refs_0_, f32[64,5120]{1,0:T(8,128)S(1)} %get-tuple-element.53.refs_1_, s32[1,64]{1,0:T(1,128)S(1)} %collective-permute-done.14.refs_2_, s32[1,64]{1,0:T(1,128)S(1)} %bitcast.16, ...), custom_call_target="tpu_custom_call" | custom-call | tf_op jit(solution)/shard_map/pallas_call | solution.py:336
  82.2 1.4 %reshape.26 = bf16[2,32,2,5120]{3,2,1,0:T(2,128)(2,1)} reshape(bf16[2,64,5120]{2,1,0:T(8,128)(2,1)S(1)} %shard_map.109) | data formatting | bytes 2621440 | tf_op jit(solution)/shard_map/reshape | solution.py:348
  (42 shorter events, 3.5 us)
Async XLA Ops:
  1.8 21.4 %collective-permute-start.4 = (bf16[1280,1280]{1,0:T(8,128)(2,1)}, bf16[1280,1280]{1,0:T(8,128)(2,1)S(1)}, u32[]{:S(2)}, u32[]{:S(2)}) collective-permute-start(bf16[1280,1280]{1,0:T(8,128)(2,1)} %refs_0_.7), channel_id=1, source_target_pairs={{0,1},{1,0},{2,3},{3,2},{4,5},{5,4},{6,7},{7,6},{8,9},{9,8},{10,11... | collective-permute-start | bytes 9830408 | tf_op jit(solution)/shard_map/ppermute | solution.py:217
  2.3 10.1 %collective-permute-start = (bf16[528,128]{1,0:T(8,128)(2,1)}, bf16[528,128]{1,0:T(8,128)(2,1)S(1)}, u32[]{:S(2)}, u32[]{:S(2)}) collective-permute-start(bf16[528,128]{1,0:T(8,128)(2,1)} %shard_map.100.refs_0_), channel_id=1, source_target_pairs={{0,4},{4,8},{8,12},{1,5},{5,9},{9,13},{2,6},{6,10},{10,14},{3,7},{... | collective-permute-start | bytes 405512 | tf_op jit(solution)/shard_map/ppermute | solution.py:236
  6.8 8.1 %collective-permute-start.1 = (bf16[528,128]{1,0:T(8,128)(2,1)}, bf16[528,128]{1,0:T(8,128)(2,1)S(1)}, u32[]{:S(2)}, u32[]{:S(2)}) collective-permute-start(bf16[528,128]{1,0:T(8,128)(2,1)} %shard_map.100.refs_0_), channel_id=1, source_target_pairs={{0,8},{4,12},{1,9},{5,13},{2,10},{6,14},{3,11},{7,15},{16,24},{20,... | collective-permute-start | bytes 405512 | tf_op jit(solution)/shard_map/ppermute | solution.py:236
  11.3 1.0 %copy-start.4 = (bf16[1,128,10,128]{3,1,2,0:T(8,128)(2,1)S(1)}, bf16[1,128,10,128]{3,1,2,0:T(8,128)(2,1)}, u32[]{:S(2)}) copy-start(bf16[1,128,10,128]{3,1,2,0:T(8,128)(2,1)} %param.10) | copy-start | bytes 983044
  14.9 0.9 %copy-start.3 = (bf16[528,128]{1,0:T(8,128)(2,1)S(1)}, bf16[528,128]{1,0:T(8,128)(2,1)}, u32[]{:S(2)}) copy-start(bf16[528,128]{1,0:T(8,128)(2,1)} %shard_map.100.refs_0_) | copy-start | bytes 405508
  18.5 1.5 %collective-permute-start.2 = (bf16[64,1280]{1,0:T(8,128)(2,1)S(1)}, bf16[64,1280]{1,0:T(8,128)(2,1)S(1)}, u32[]{:S(2)}, u32[]{:S(2)}) collective-permute-start(bf16[64,1280]{1,0:T(8,128)(2,1)S(1)} %get-tuple-element.34), channel_id=1, source_target_pairs={{0,1},{1,0},{2,3},{3,2},{4,5},{5,4},{6,7},{7,6},{8,9},{9,8},{10,11... | collective-permute-start | bytes 491528 | tf_op jit(solution)/shard_map/ppermute | solution.py:217
  20.0 13.9 %collective-permute-start.3 = (bf16[64,2560]{1,0:T(8,128)(2,1)S(1)}, bf16[64,2560]{1,0:T(8,128)(2,1)S(1)}, u32[]{:S(2)}, u32[]{:S(2)}) collective-permute-start(bf16[64,2560]{1,0:T(8,128)(2,1)S(1)} %pad_maximum_fusion.block_ref), channel_id=1, source_target_pairs={{0,4},{4,8},{8,12},{12,0},{1,5},{5,9},{9,13},{13,1},{2,6},{6,10},{... | collective-permute-start | bytes 983048 | tf_op jit(solution)/shard_map/ppermute | solution.py:217
  23.1 1.9 %copy-start = (bf16[1280,1280]{1,0:T(8,128)(2,1)S(1)}, bf16[1280,1280]{1,0:T(8,128)(2,1)}, u32[]{:S(2)}) copy-start(bf16[1280,1280]{1,0:T(8,128)(2,1)} %refs_0_.7) | copy-start | bytes 9830404
  33.9 12.5 %collective-permute-start.5 = (bf16[64,2560]{1,0:T(8,128)(2,1)S(1)}, bf16[64,2560]{1,0:T(8,128)(2,1)S(1)}, u32[]{:S(2)}, u32[]{:S(2)}) collective-permute-start(bf16[64,2560]{1,0:T(8,128)(2,1)S(1)} %collective-permute-done.3.block_ref), channel_id=1, source_target_pairs={{0,4},{4,8},{8,12},{12,0},{1,5},{5,9},{9,13},{13,1},{2,6},{6,10},{... | collective-permute-start | bytes 983048 | tf_op jit(solution)/shard_map/ppermute | solution.py:217
  33.9 34.8 %collective-permute-start.11 = (bf16[64,5120]{1,0:T(8,128)(2,1)}, bf16[64,5120]{1,0:T(8,128)(2,1)}, u32[]{:S(2)}, u32[]{:S(2)}) collective-permute-start(bf16[64,5120]{1,0:T(8,128)(2,1)} %bitcast.8.refs_0_), channel_id=1, source_target_pairs={{0,2},{2,0},{1,3},{3,1},{4,6},{6,4},{5,7},{7,5},{8,10},{10,8},{9,1... | collective-permute-start | bytes 1966088 | tf_op jit(solution)/shard_map/ppermute | solution.py:217
  35.4 18.5 %collective-permute-start.7 = (bf16[64,1280]{1,0:T(8,128)(2,1)S(1)}, bf16[64,1280]{1,0:T(8,128)(2,1)S(1)}, u32[]{:S(2)}, u32[]{:S(2)}) collective-permute-start(bf16[64,1280]{1,0:T(8,128)(2,1)S(1)} %shard_map.103.refs_2_), channel_id=1, source_target_pairs={{0,2},{2,0},{1,3},{3,1},{4,6},{6,4},{5,7},{7,5},{8,10},{10,8},{9,1... | collective-permute-start | bytes 491528 | tf_op jit(solution)/shard_map/ppermute | solution.py:217
  37.1 16.7 %collective-permute-start.8 = (bf16[64,1280]{1,0:T(8,128)(2,1)S(1)}, bf16[64,1280]{1,0:T(8,128)(2,1)S(1)}, u32[]{:S(2)}, u32[]{:S(2)}) collective-permute-start(bf16[64,1280]{1,0:T(8,128)(2,1)S(1)} %shard_map.104), channel_id=1, source_target_pairs={{0,12},{4,0},{8,4},{12,8},{1,13},{5,1},{9,5},{13,9},{2,14},{6,2},{... | collective-permute-start | bytes 491528 | tf_op jit(solution)/shard_map/ppermute | solution.py:217
  46.3 19.7 %collective-permute-start.6 = (bf16[64,2560]{1,0:T(8,128)(2,1)S(1)}, bf16[64,2560]{1,0:T(8,128)(2,1)S(1)}, u32[]{:S(2)}, u32[]{:S(2)}) collective-permute-start(bf16[64,2560]{1,0:T(8,128)(2,1)S(1)} %collective-permute-done.5.block_ref), channel_id=1, source_target_pairs={{0,4},{4,8},{8,12},{12,0},{1,5},{5,9},{9,13},{13,1},{2,6},{6,10},{... | collective-permute-start | bytes 983048 | tf_op jit(solution)/shard_map/ppermute | solution.py:217
  53.9 1.3 %copy-start.5 = (bf16[64,1280]{1,0:T(8,128)(2,1)}, bf16[64,1280]{1,0:T(8,128)(2,1)S(1)}, u32[]{:S(2)}) copy-start(bf16[64,1280]{1,0:T(8,128)(2,1)S(1)} %collective-permute-done.7.refs_5_) | copy-start | bytes 491524
  53.9 3.0 %copy-start.7 = (bf16[64,1280]{1,0:T(8,128)(2,1)}, bf16[64,1280]{1,0:T(8,128)(2,1)S(1)}, u32[]{:S(2)}) copy-start(bf16[64,1280]{1,0:T(8,128)(2,1)S(1)} %collective-permute-done.8.refs_3_) | copy-start | bytes 491524
  53.9 12.2 %copy-start.1 = (bf16[1280,1280]{1,0:T(8,128)(2,1)S(1)}, bf16[1280,1280]{1,0:T(8,128)(2,1)}, u32[]{:S(2)}) copy-start(bf16[1280,1280]{1,0:T(8,128)(2,1)} %refs_0_.7) | copy-start | bytes 9830404
  55.1 12.9 %copy-start.12 = (s32[1,64,1]{1,2,0:T(1,128)S(1)}, s32[1,64,1]{1,2,0:T(1,128)}, u32[]{:S(2)}) copy-start(s32[1,64,1]{1,2,0:T(1,128)} %param.18) | copy-start | bytes 772
  55.1 9.4 %collective-permute-start.12 = (bf16[64,1280]{1,0:T(8,128)(2,1)S(1)}, bf16[64,1280]{1,0:T(8,128)(2,1)}, u32[]{:S(2)}, u32[]{:S(2)}) collective-permute-start(bf16[64,1280]{1,0:T(8,128)(2,1)S(1)} %shard_map.105), channel_id=1, source_target_pairs={{0,8},{4,12},{8,0},{12,4},{1,9},{5,13},{9,1},{13,5},{2,10},{6,14},... | collective-permute-start | bytes 491528 | tf_op jit(solution)/shard_map/ppermute | solution.py:217
  56.9 9.2 %collective-permute-start.9 = (bf16[64,1280]{1,0:T(8,128)(2,1)S(1)}, bf16[64,1280]{1,0:T(8,128)(2,1)S(1)}, u32[]{:S(2)}, u32[]{:S(2)}) collective-permute-start(bf16[64,1280]{1,0:T(8,128)(2,1)S(1)} %collective-permute-done.8.refs_3_), channel_id=1, source_target_pairs={{0,2},{2,0},{1,3},{3,1},{4,6},{6,4},{5,7},{7,5},{8,10},{10,8},{9,1... | collective-permute-start | bytes 491528 | tf_op jit(solution)/shard_map/ppermute | solution.py:217
  64.6 5.8 %collective-permute-start.13 = (bf16[64,1280]{1,0:T(8,128)(2,1)}, bf16[64,1280]{1,0:T(8,128)(2,1)}, u32[]{:S(2)}, u32[]{:S(2)}) collective-permute-start(bf16[64,1280]{1,0:T(8,128)(2,1)} %collective-permute-done.12.refs_4_), channel_id=1, source_target_pairs={{0,2},{2,0},{1,3},{3,1},{4,6},{6,4},{5,7},{7,5},{8,10},{10,8},{9,1... | collective-permute-start | bytes 491528 | tf_op jit(solution)/shard_map/ppermute | solution.py:217
  66.1 2.0 %copy-start.9 = (bf16[64,1280]{1,0:T(8,128)(2,1)}, bf16[64,1280]{1,0:T(8,128)(2,1)S(1)}, u32[]{:S(2)}) copy-start(bf16[64,1280]{1,0:T(8,128)(2,1)S(1)} %collective-permute-done.9.refs_6_) | copy-start | bytes 491524
  66.1 10.3 %copy-start.13 = (bf16[5120]{0:T(1024)(128)(2,1)S(1)}, bf16[5120]{0:T(1024)(128)(2,1)}, u32[]{:S(2)}) copy-start(bf16[5120]{0:T(1024)(128)(2,1)} %param.16) | copy-start | bytes 30724
  66.1 10.4 %copy-start.11 = (s32[64]{0:T(128)S(1)}, s32[64]{0:T(128)}, u32[]{:S(2)}) copy-start(s32[64]{0:T(128)} %param.19) | copy-start | bytes 772
  68.0 8.4 %copy-start.2 = (bf16[5120,32]{0,1:T(8,128)(2,1)S(1)}, bf16[5120,32]{0,1:T(8,128)(2,1)}, u32[]{:S(2)}) copy-start(bf16[5120,32]{0,1:T(8,128)(2,1)} %param.17) | copy-start | bytes 983044
  68.0 7.3 %collective-permute-start.10 = (bf16[64,1280]{1,0:T(8,128)(2,1)}, bf16[64,1280]{1,0:T(8,128)(2,1)S(1)}, u32[]{:S(2)}, u32[]{:S(2)}) collective-permute-start(bf16[64,1280]{1,0:T(8,128)(2,1)} %shard_map.106), channel_id=1, source_target_pairs={{0,4},{4,8},{8,12},{12,0},{1,5},{5,9},{9,13},{13,1},{2,6},{6,10},{... | collective-permute-start | bytes 491528 | tf_op jit(solution)/shard_map/ppermute | solution.py:217
  68.0 6.7 %collective-permute-start.14 = (s32[1,64]{1,0:T(1,128)S(1)}, s32[1,64]{1,0:T(1,128)S(1)}, u32[]{:S(2)}, u32[]{:S(2)}) collective-permute-start(s32[1,64]{1,0:T(1,128)S(1)} %bitcast.17), channel_id=1, source_target_pairs={{0,2},{2,0},{1,3},{3,1},{4,6},{6,4},{5,7},{7,5},{8,10},{10,8},{9,1... | collective-permute-start | bytes 776 | tf_op jit(solution)/shard_map/ppermute | solution.py:217
  70.3 0.9 %copy-start.6 = (bf16[64,1280]{1,0:T(8,128)(2,1)S(1)}, bf16[64,1280]{1,0:T(8,128)(2,1)}, u32[]{:S(2)}) copy-start(bf16[64,1280]{1,0:T(8,128)(2,1)} %copy-done.5) | copy-start | bytes 491524
  71.2 0.9 %copy-start.8 = (bf16[64,1280]{1,0:T(8,128)(2,1)S(1)}, bf16[64,1280]{1,0:T(8,128)(2,1)}, u32[]{:S(2)}) copy-start(bf16[64,1280]{1,0:T(8,128)(2,1)} %copy-done.7) | copy-start | bytes 491524
  72.2 0.9 %copy-start.10 = (bf16[64,1280]{1,0:T(8,128)(2,1)S(1)}, bf16[64,1280]{1,0:T(8,128)(2,1)}, u32[]{:S(2)}) copy-start(bf16[64,1280]{1,0:T(8,128)(2,1)} %copy-done.9) | copy-start | bytes 491524
  75.4 5.3 %collective-permute-start.15 = (bf16[64,1280]{1,0:T(8,128)(2,1)S(1)}, bf16[64,1280]{1,0:T(8,128)(2,1)S(1)}, u32[]{:S(2)}, u32[]{:S(2)}) collective-permute-start(bf16[64,1280]{1,0:T(8,128)(2,1)S(1)} %collective-permute-done.10.refs_0_), channel_id=1, source_target_pairs={{0,2},{2,0},{1,3},{3,1},{4,6},{6,4},{5,7},{7,5},{8,10},{10,8},{9,1... | collective-permute-start | bytes 491528 | tf_op jit(solution)/shard_map/ppermute | solution.py:217
